TPU v7x, 32 devices: a whole 2x2x4 slice. The times are simulated.
32 devices in a mesh: rep: 4 (over y, core), fsdp: 8 (over z, x).
Axes of the slice: x: 2, y: 2, z: 4, core: 2. Of those that a mesh axis runs over, the one named last changes fastest.
Arguments:
- tokens: bfloat16 [32768, 8192], P(('rep', 'fsdp')), may hold values from -6 to 6
- cotangent: bfloat16 [32768, 512], P(('rep', 'fsdp')), may hold values from -0.03125 to 0.03125
- old_weight: bfloat16 [8192, 512], P(('rep', 'fsdp')), may hold values from -0.0625 to 0.0625
- old_first: float32 [8192, 512], P(('rep', 'fsdp')), may hold values from -4 to 4
- old_second: float32 [8192, 512], P(('rep', 'fsdp')), may hold values from 0.05 to 2
- old_owner: int32 [32], replicated, may hold values from 0 to 31, each once
- new_owner: int32 [8], replicated, may hold values from 0 to 7, each once
Outputs:
- projected: bfloat16 [32768, 512], P(('rep', 'fsdp'))
- new_weight: bfloat16 [8192, 512], P(('rep', 'fsdp'))
- new_first: float32 [8192, 512], P(('rep', 'fsdp'))
- new_second: float32 [8192, 512], P(('rep', 'fsdp'))
Inputs may be any that keep to these rules, and one draw needn't show every extreme that they name: `old_owner`: a permutation. `new_owner`: a permutation.
All inputs are finite; a program needn't handle non-finite values.
Results may differ from a plain program's by a relative error of at most 0.008.
Values may be sent and summed in bfloat16 or wider, within the bound.
No kernel may reach another device: no remote copies, remote signals or barrier semaphores. Data moves between devices by JAX's collectives and lax.ppermute only.
A program may use at most 192 MiB of HBM per device.

v0:
```python
import jax
import jax.numpy as jnp
from jax import lax
from jax.sharding import PartitionSpec as P

beta_one = 0.9
beta_two = 0.95
learn_rate = 0.001
decay_rate = 0.1
epsilon = 1e-08
correction_one = 1.0 - 0.9**10
correction_two = 1.0 - 0.95**10


def body(tokens, cotangent, old_weight, old_first, old_second, old_owner, new_owner):
    devices = lax.axis_size(("rep", "fsdp"))
    groups = lax.axis_size("rep")
    shards = lax.axis_size("fsdp")
    tok_rows = tokens.shape[0]
    feature_count = tokens.shape[1]
    out_width = cotangent.shape[1]
    row_block = old_weight.shape[0]
    group_block = row_block * groups
    strip = row_block * out_width // devices
    slot_ids = jnp.arange(devices, dtype=jnp.int32)
    placing = jnp.take(new_owner, slot_ids % shards) * groups + slot_ids // shards
    inverse = jnp.zeros((devices,), jnp.int32).at[old_owner].set(slot_ids)
    own_block = jnp.take(placing, lax.axis_index(("rep", "fsdp")))
    tok_order = jnp.take(tokens.reshape(tok_rows, shards, group_block), new_owner, axis=1).reshape(
        tok_rows, feature_count
    )

    def outgoing(source):
        return jnp.take(source.reshape(devices, strip), placing, axis=0)

    stacked = jnp.stack([outgoing(old_first), outgoing(old_second)])
    layers = stacked.shape[0]
    arrived = lax.all_to_all(stacked, ("rep", "fsdp"), split_axis=1, concat_axis=1, tiled=True)
    moved = jnp.take(arrived, inverse, axis=1).reshape(layers, row_block, out_width)
    first_rows = moved[0]
    second_rows = moved[1]
    whole = lax.all_gather(old_weight, ("rep", "fsdp"), axis=0, tiled=True)
    held = jnp.take(whole.reshape(devices, devices, strip), inverse, axis=0)
    logical = jnp.transpose(held, (1, 0, 2)).reshape(feature_count, out_width)
    outputs = jnp.dot(tokens, logical, preferred_element_type=jnp.float32)
    weight_rows = lax.dynamic_slice_in_dim(logical, own_block * row_block, row_block, 0)
    projected = outputs.astype(jnp.bfloat16)
    partial_sum = lax.psum_scatter(
        lax.dot_general(
            tok_order, cotangent, (((0,), (0,)), ((), ())), preferred_element_type=jnp.float32
        ).astype(jnp.bfloat16),
        "fsdp",
        scatter_dimension=0,
        tiled=True,
    )
    gradient = lax.psum_scatter(partial_sum, "rep", scatter_dimension=0, tiled=True).astype(
        jnp.float32
    )
    first_next = beta_one * first_rows + (1.0 - beta_one) * gradient
    second_next = beta_two * second_rows + (1.0 - beta_two) * gradient * gradient
    step_size = first_next / correction_one / (jnp.sqrt(second_next / correction_two) + epsilon)
    updated = (
        weight_rows.astype(jnp.float32) * (1.0 - learn_rate * decay_rate) - learn_rate * step_size
    ).astype(jnp.bfloat16)
    return (projected, updated, first_next, second_next)


def solution(mesh):
    placed = (
        P(("rep", "fsdp"), None),
        P(("rep", "fsdp"), None),
        P(("rep", "fsdp"), None),
        P(("rep", "fsdp"), None),
        P(("rep", "fsdp"), None),
        P(),
        P(),
    )
    return jax.shard_map(
        body,
        mesh=mesh,
        in_specs=placed,
        out_specs=(
            P(("rep", "fsdp"), None),
            P(("rep", "fsdp"), None),
            P(("rep", "fsdp"), None),
            P(("rep", "fsdp"), None),
        ),
        check_vma=False,
    )
```

profile of v0, /device:TPU:8, one launch (start us, length us, event | category | flops | bytes accessed | tf_op | source)
XLA Modules:
  0.0 359.2 jit_solution(4369755567244602510)
XLA Ops:
  8.0 0.0 copy-start
  8.0 0.0 all-gather.2.cloned.1.call-start
  8.1 0.7 all-gather.2.cloned.1.call-update
  8.7 0.0 reduce-scatter.3.cloned.1.call-start
  8.8 11.6 %fusion.12 = (bf16[512,8192]{1,0:T(8,128)(2,1)}, bf16[512,8192]{1,0:T(8,128)(2,1)}) fusion(bf16[1024,8192]{1,0:T(8,128)(2,1)} %param.9), kind=kLoop, calls=%fused_computation.53 | loop fusion | bytes 33554432 | tf_op jit(solution)/shard_map/jit(_take)/gather | solution.py:29
  20.4 12.0 %copy.32 = bf16[512,8192]{0,1:T(8,128)(2,1)} copy(bf16[512,8192]{1,0:T(8,128)(2,1)} %get-tuple-element.40) | data formatting | bytes 16777216
  32.3 11.4 %copy.28 = bf16[512,8,1024]{2,0,1:T(8,128)(2,1)} copy(bf16[512,8,1024]{0,2,1:T(8,128)(2,1)} %bitcast.31) | data formatting | bytes 16777216 | tf_op jit(solution)/shard_map/jit(_take)/gather | solution.py:29
  43.8 12.0 %copy.31 = bf16[512,8192]{0,1:T(8,128)(2,1)} copy(bf16[512,8192]{1,0:T(8,128)(2,1)} %get-tuple-element.39) | data formatting | bytes 16777216
  55.7 0.0 copy-start.2
  55.7 11.7 %copy.26 = bf16[512,8,1024]{2,0,1:T(8,128)(2,1)} copy(bf16[512,8,1024]{0,2,1:T(8,128)(2,1)} %bitcast.32) | data formatting | bytes 16777216 | tf_op jit(solution)/shard_map/jit(_take)/gather | solution.py:29
  67.4 0.0 copy-done.2
  67.4 8.1 %gather_fusion.4 = bf16[8,512,1024]{2,1,0:T(8,128)(2,1)} fusion(bf16[512,8,1024]{2,0,1:T(8,128)(2,1)} %copy.28, s32[1024]{0:T(1024)S(1)} %pad_clamp_fusion), kind=kCustom, calls=%fused_computation.6 | custom fusion | bytes 16777248 | tf_op jit(solution)/shard_map/jit(_take)/gather | solution.py:29
  75.6 8.1 %gather_fusion.3 = bf16[8,512,1024]{2,1,0:T(8,128)(2,1)} fusion(bf16[512,8,1024]{2,0,1:T(8,128)(2,1)} %copy.26, s32[1024]{0:T(1024)S(1)} %pad_clamp_fusion), kind=kCustom, calls=%fused_computation.5 | custom fusion | bytes 16777248 | tf_op jit(solution)/shard_map/jit(_take)/gather | solution.py:29
  83.6 13.7 %pad_maximum_fusion = bf16[1024,8,1024]{2,0,1:T(8,128)(2,1)} fusion(bf16[512,8,1024]{2,0,1:T(8,128)(2,1)} %bitcast.29, bf16[512,8,1024]{2,0,1:T(8,128)(2,1)} %bitcast.30), kind=kLoop, calls=%fused_computation.8 | loop fusion | flops 33554432 | bytes 33554432
  97.4 21.6 %copy.29 = bf16[1024,8,1024]{0,2,1:T(8,128)(2,1)} copy(bf16[1024,8,1024]{2,0,1:T(8,128)(2,1)} %pad_maximum_fusion) | data formatting | bytes 33554432
  119.0 0.1 broadcast_bitcast_fusion
  119.1 14.2 %bitcast_select_fusion = bf16[1024,8192]{0,1:T(8,128)(2,1)} fusion(bf16[1024,8,1024]{0,2,1:T(8,128)(2,1)} %copy.29, pred[8192]{0:T(1024)(128)(4,1)S(1)} %bitcast.33), kind=kLoop, calls=%fused_computation.9 | loop fusion | flops 8388608 | bytes 33562624 | tf_op jit(solution)/shard_map/jit(_take)/select_n | solution.py:29
  133.2 0.0 copy-done
  133.2 16.9 %convolution_convert_fusion = bf16[8192,512]{1,0:T(8,128)(2,1)} fusion(bf16[1024,8192]{0,1:T(8,128)(2,1)} %bitcast_select_fusion, bf16[1024,512]{1,0:T(8,128)(2,1)S(1)} %copy-done), kind=kOutput, calls=%fused_computation.10 | convolution fusion | flops 8594128896 | bytes 26214400 | tf_op jit(solution)/shard_map/dot_general | solution.py:49
  150.1 0.0 copy-start.3
  150.1 0.0 copy-start.4
  150.1 0.0 reduce-scatter.3.cloned.1.call-update
  150.2 0.7 gather_fusion.1
  150.9 0.3 copy-done.3
  151.2 0.1 reshape.89
  151.3 0.1 copy-done.4
  151.3 0.1 reshape.90
  151.5 0.0 copy-start.5
  151.5 0.7 gather_fusion.5
  152.2 0.7 gather_fusion.6
  152.9 0.1 select_bitcast_fusion.3
  153.1 0.1 pad_maximum_fusion.1
  153.2 1.8 copy.24
  154.9 6.4 %all-to-all-start = ((f32[2,32,4096]{2,0,1:T(2,128)}), f32[2,32,4096]{2,0,1:T(2,128)S(1)}, u32[]{:S(2)}, u32[]{:S(2)}) async-start(f32[2,32,4096]{2,0,1:T(2,128)} %copy.24), calls=%async_computation | async-start | bytes 2097152 | tf_op jit(solution)/shard_map/all_to_all | solution.py:38
  161.3 0.0 reduce-scatter.5.cloned.1.call-start
  161.4 0.6 dynamic-slice.2
  162.6 0.0 copy-done.5
  162.7 0.9 scatter_custom_fusion
  163.6 47.5 %all-to-all-done = f32[2,32,4096]{2,0,1:T(2,128)S(1)} async-done(((f32[2,32,4096]{2,0,1:T(2,128)}), f32[2,32,4096]{2,0,1:T(2,128)S(1)}, u32[]{:S(2)}, u32[]{:S(2)}) %all-to-all-start) | async-done | bytes 1048608 | tf_op jit(solution)/shard_map/all_to_all | solution.py:38
  211.1 1.7 gather_fusion.2
  212.8 0.8 select_bitcast_fusion.1
  213.5 3.1 fusion.4
  216.6 0.1 mul.65
  216.7 0.1 mul.70
  216.8 0.0 all-gather.2.cloned.1.call-done
  216.9 13.6 %reshape.87 = bf16[32,32,4096]{2,1,0:T(8,128)(2,1)} reshape(bf16[8192,512]{1,0:T(8,128)(2,1)} %all-gather.2.cloned.1.call-done) | data formatting | bytes 16777216 | tf_op jit(solution)/shard_map/reshape | solution.py:43
  230.5 8.6 %gather_fusion = bf16[32,32,4096]{2,1,0:T(8,128)(2,1)} fusion(bf16[32,32,4096]{2,1,0:T(8,128)(2,1)} %reshape.87, s32[1024]{0:T(1024)S(1)} %pad_clamp_fusion.3), kind=kCustom, calls=%fused_computation.2 | custom fusion | bytes 16777344 | tf_op jit(solution)/shard_map/jit(_take)/gather | solution.py:43
  239.1 7.5 %select_bitcast_fusion = bf16[32,32,4096]{2,0,1:T(8,128)(2,1)} fusion(bf16[32,32,4096]{2,1,0:T(8,128)(2,1)} %gather_fusion, pred[32]{0:T(512)(128)(4,1)S(1)} %compare_and_fusion.2), kind=kLoop, calls=%fused_computation.11 | loop fusion | flops 4194304 | bytes 16777248 | tf_op jit(solution)/shard_map/jit(_take)/select_n | solution.py:43
  246.6 11.4 %copy.23 = bf16[32,32,4096]{2,1,0:T(8,128)(2,1)} copy(bf16[32,32,4096]{2,0,1:T(8,128)(2,1)} %select_bitcast_fusion) | data formatting | bytes 16777216 | tf_op jit(solution)/shard_map/jit(_take)/select_n | solution.py:43
  258.0 13.6 %reshape.88 = bf16[8192,512]{1,0:T(8,128)(2,1)} reshape(bf16[32,32,4096]{2,1,0:T(8,128)(2,1)} %copy.23) | data formatting | bytes 16777216 | tf_op jit(solution)/shard_map/reshape | solution.py:44
  271.5 50.4 %reduce-scatter.3.cloned.1.call-done = bf16[1024,512]{1,0:T(8,128)(2,1)} async-done(((bf16[8192,512]{1,0:T(8,128)(2,1)}), bf16[1024,512]{1,0:T(8,128)(2,1)}) %reduce-scatter.3.cloned.1.call-update) | async-done | bytes 1048592 | tf_op jit(solution)/shard_map/reduce_scatter | solution.py:48
  321.9 0.0 reduce-scatter.5.cloned.1.call-update
  321.9 0.0 copy-start.1
  321.9 15.0 %fusion = bf16[1024,512]{0,1:T(8,128)(2,1)S(1)} fusion(bf16[8192,512]{1,0:T(8,128)(2,1)} %reshape.88, bf16[1024,8192]{1,0:T(8,128)(2,1)} %param.9), kind=kOutput, calls=%fused_computation.13 | convolution fusion | flops 8590458880 | bytes 26214400 | tf_op jit(solution)/shard_map/dot_general | solution.py:45
  336.9 1.3 copy.30
  338.2 11.2 %reduce-scatter.5.cloned.1.call-done = bf16[256,512]{1,0:T(8,128)(2,1)} async-done(((bf16[1024,512]{1,0:T(8,128)(2,1)}), bf16[256,512]{1,0:T(8,128)(2,1)}) %reduce-scatter.5.cloned.1.call-update) | async-done | bytes 262160 | tf_op jit(solution)/shard_map/reduce_scatter | solution.py:56
  349.4 2.3 subtract_convert_fusion
  351.8 0.0 copy-done.1
  (14 shorter events, 0.1 us)
Async XLA Ops:
  8.0 125.2 %copy-start = (bf16[1024,512]{1,0:T(8,128)(2,1)S(1)}, bf16[1024,512]{1,0:T(8,128)(2,1)}, u32[]{:S(2)}) copy-start(bf16[1024,512]{1,0:T(8,128)(2,1)} %param.10) | copy-start | bytes 3145732
  8.0 208.9 %all-gather.2.cloned.1.call-start = ((), (), s32[]{:S(2)}) async-start(), calls=%async_computation.3 | async-start | bytes 8650752 | tf_op jit(solution)/shard_map/all_gather | solution.py:42
  8.7 313.2 %reduce-scatter.3.cloned.1.call-start = ((), (), s32[]{:S(2)}) async-start(), calls=%async_computation.4 | async-start | bytes 9437184 | tf_op jit(solution)/shard_map/reduce_scatter | solution.py:48
  55.7 11.7 %copy-start.2 = (s32[8]{0:T(128)S(1)}, s32[8]{0:T(128)}, u32[]{:S(2)}) copy-start(s32[8]{0:T(128)} %param.15) | copy-start | bytes 100
  150.1 1.0 copy-start.3
  150.1 1.2 copy-start.4
  151.5 11.2 %copy-start.5 = (s32[32]{0:T(128)S(1)}, s32[32]{0:T(128)}, u32[]{:S(2)}) copy-start(s32[32]{0:T(128)} %param.14) | copy-start | bytes 388
  154.9 56.2 %all-to-all-start = ((f32[2,32,4096]{2,0,1:T(2,128)}), f32[2,32,4096]{2,0,1:T(2,128)S(1)}, u32[]{:S(2)}, u32[]{:S(2)}) async-start(f32[2,32,4096]{2,0,1:T(2,128)} %copy.24), calls=%async_computation | async-start | bytes 2097152 | tf_op jit(solution)/shard_map/all_to_all | solution.py:38
  161.3 188.1 %reduce-scatter.5.cloned.1.call-start = ((), (), s32[]{:S(2)}) async-start(), calls=%async_computation.5 | async-start | bytes 1310720 | tf_op jit(solution)/shard_map/reduce_scatter | solution.py:56
  321.9 29.9 %copy-start.1 = (bf16[1024,512]{1,0:T(8,128)(2,1)S(1)}, bf16[1024,512]{1,0:T(8,128)(2,1)}, u32[]{:S(2)}) copy-start(bf16[1024,512]{1,0:T(8,128)(2,1)} %param.10) | copy-start | bytes 3145732
Sparse Core Ops, SparseCore 0:
  11.8 78.4 all-gather.1
Sparse Core Ops, SparseCore 1:
  150.2 171.6 reduce-scatter.2
  324.5 24.9 reduce-scatter.4
where the time goes:
time: 364 us; the launch traced here: 359 us
  local copies, waits for them, and re-layouts  153 us (42%)
  waiting for transfers between devices  110 us (30%)
  other arithmetic  41.9 us (12%)
  matrix products  31.8 us (9%)
  between operations  16.4 us (5%)
  starting transfers between devices  6.49 us (2%)
    gather x5, local copies, waits for them, and re-layouts, body(): jnp.take(tokens.reshape(tok_rows, shards, group_block), new_owner, axis=1)  50.9 us
    reduce_scatter x1, waiting for transfers between devices, body(): lax.psum_scatter(lax.dot_general(tok_order, cotangent, (((0,), (0,)), (()...  50.4 us
    all_to_all x1, waiting for transfers between devices, body(): lax.all_to_all(stacked, ('rep', 'fsdp'), split_axis=1, concat_axis=1, til...  47.5 us
    unnamed x18, local copies, waits for them, and re-layouts  47.3 us
    dot_general x1, matrix products, body(): lax.dot_general(tok_order, cotangent, (((0,), (0,)), ((), ())), preferred...  16.9 us
    dot_general x1, matrix products, body(): outputs = jnp.dot(tokens, logical, preferred_element_type=jnp.float32)  15 us
    select_n x2, other arithmetic, body(): jnp.take(tokens.reshape(tok_rows, shards, group_block), new_owner, axis=1)  14.2 us
    unnamed x1, other arithmetic  13.7 us
  transfers between devices with their start and end apart: 4, of which 3 were waited for; matrix products, arithmetic and copies ran while one was open for 62% of the time, Pallas kernels for 0%

commit v1 on v0

v1 whole, which is shorter than its diff:
```python
import functools
import jax
import jax.numpy as jnp
from jax import lax
from jax.experimental import pallas as pl
from jax.experimental.pallas import tpu as pltpu
from jax.sharding import PartitionSpec as P

beta_one = 0.9
beta_two = 0.95
learn_rate = 0.001
decay_rate = 0.1
epsilon = 1e-08
correction_one = 1.0 - 0.9**10
correction_two = 1.0 - 0.95**10

AXES = ("rep", "fsdp")
GRANT = 48 * 1024 * 1024
SUB = 8
PER_STEP = 4


def cost(flops, moved):
    return pl.CostEstimate(flops=flops, bytes_accessed=moved, transcendentals=0)


def grad_kernel(order_ref, *refs):
    token_refs, (cot_ref, out_ref, turned) = refs[:-3], refs[-3:]

    @pl.when(pl.program_id(0) == 0)
    def _():
        turned[...] = cot_ref[...].T

    for slot, token_ref in enumerate(token_refs):
        out_ref[slot] = jnp.dot(
            turned[...], token_ref[...], preferred_element_type=jnp.float32
        ).astype(out_ref.dtype)


def grad_blocks(tokens, cotangent, order, row_block):
    rows, features = tokens.shape
    width = cotangent.shape[1]
    blocks = order.shape[0]
    if row_block % 128 or blocks % PER_STEP:
        whole = lax.dot_general(
            cotangent, tokens, (((0,), (0,)), ((), ())), preferred_element_type=jnp.float32
        ).astype(jnp.bfloat16)
        cut = jnp.transpose(whole.reshape(width, features // row_block, row_block), (1, 0, 2))
        return jnp.take(cut, order, axis=0)

    def token_map(slot):
        return lambda i, order_ref: (0, order_ref[i * PER_STEP + slot])

    return pl.pallas_call(
        grad_kernel,
        grid_spec=pltpu.PrefetchScalarGridSpec(
            num_scalar_prefetch=1,
            grid=(blocks // PER_STEP,),
            in_specs=[pl.BlockSpec((rows, row_block), token_map(s)) for s in range(PER_STEP)]
            + [pl.BlockSpec((rows, width), lambda i, order_ref: (0, 0))],
            out_specs=pl.BlockSpec((PER_STEP, width, row_block), lambda i, order_ref: (i, 0, 0)),
            scratch_shapes=[pltpu.VMEM((width, rows), jnp.bfloat16)],
        ),
        out_shape=jax.ShapeDtypeStruct((blocks, width, row_block), jnp.bfloat16),
        compiler_params=pltpu.CompilerParams(vmem_limit_bytes=GRANT),
        cost_estimate=cost(
            2 * rows * width * blocks * row_block,
            2 * blocks * row_block * (rows + width) + 2 * rows * width,
        ),
        name="weight_gradient",
    )(order, *([tokens] * PER_STEP), cotangent)


def pack_kernel(placing_ref, first_ref, second_ref, out_ref):
    for slot in range(out_ref.shape[0]):
        rows = pl.ds(pl.multiple_of(placing_ref[slot] * SUB, SUB), SUB)
        pair = jnp.concatenate([first_ref[rows, :], second_ref[rows, :]], axis=0)
        out_ref[slot] = pair.astype(out_ref.dtype)


def pack_moments(first, second, placing):
    devices = placing.shape[0]
    width = first.shape[1]
    return pl.pallas_call(
        pack_kernel,
        in_specs=[
            pl.BlockSpec(memory_space=pltpu.SMEM),
            pl.BlockSpec(memory_space=pltpu.VMEM),
            pl.BlockSpec(memory_space=pltpu.VMEM),
        ],
        out_specs=pl.BlockSpec(memory_space=pltpu.VMEM),
        out_shape=jax.ShapeDtypeStruct((devices, 2 * SUB, width), jnp.bfloat16),
        cost_estimate=cost(0, 12 * first.size),
        name="pack_moments",
    )(placing, first, second)


def project_kernel(inverse_ref, own_ref, token_ref, held_ref, out_ref, rows_ref, logical):
    devices, row_block, _ = held_ref.shape

    @pl.when(pl.program_id(0) == 0)
    def _():
        def place(pair, carry):
            even = inverse_ref[2 * pair]
            odd = inverse_ref[2 * pair + 1]
            for block in range(0, devices, 2):
                span = pl.ds(block * SUB, 2 * SUB)
                top = held_ref[even, span, :]
                low = held_ref[odd, span, :]
                for half in range(2):
                    part = slice(half * SUB, (half + 1) * SUB)
                    start = (block + half) * row_block + pair * 2 * SUB
                    logical[pl.ds(pl.multiple_of(start, 2 * SUB), 2 * SUB), :] = jnp.concatenate(
                        [top[part], low[part]], axis=0
                    )
            return carry

        lax.fori_loop(0, devices // 2, place, 0)
        start = pl.multiple_of(own_ref[0] * row_block, row_block)
        rows_ref[...] = logical[pl.ds(start, row_block), :]

    out_ref[...] = jnp.dot(
        token_ref[...], logical[...], preferred_element_type=jnp.float32
    ).astype(out_ref.dtype)


def project(tokens, held, inverse, own):
    rows, features = tokens.shape
    devices, row_block, width = held.shape
    tile = rows // 4
    return pl.pallas_call(
        project_kernel,
        grid_spec=pltpu.PrefetchScalarGridSpec(
            num_scalar_prefetch=2,
            grid=(rows // tile,),
            in_specs=[
                pl.BlockSpec((tile, features), lambda i, *_: (i, 0)),
                pl.BlockSpec((devices, row_block, width), lambda i, *_: (0, 0, 0)),
            ],
            out_specs=[
                pl.BlockSpec((tile, width), lambda i, *_: (i, 0)),
                pl.BlockSpec((row_block, width), lambda i, *_: (0, 0)),
            ],
            scratch_shapes=[pltpu.VMEM((features, width), jnp.bfloat16)],
        ),
        out_shape=[
            jax.ShapeDtypeStruct((rows, width), jnp.bfloat16),
            jax.ShapeDtypeStruct((row_block, width), jnp.bfloat16),
        ],
        compiler_params=pltpu.CompilerParams(vmem_limit_bytes=GRANT),
        cost_estimate=cost(
            2 * rows * width * features, 2 * (rows * features + features * width + rows * width)
        ),
        name="project",
    )(inverse, own, tokens, held)


def adam(weight_rows, first_rows, second_rows, gradient):
    first_next = beta_one * first_rows + (1.0 - beta_one) * gradient
    second_next = beta_two * second_rows + (1.0 - beta_two) * gradient * gradient
    step_size = first_next / correction_one / (jnp.sqrt(second_next / correction_two) + epsilon)
    updated = (
        weight_rows.astype(jnp.float32) * (1.0 - learn_rate * decay_rate) - learn_rate * step_size
    ).astype(jnp.bfloat16)
    return updated, first_next, second_next


def adam_kernel(
    inverse_ref, turned_ref, moments_ref, weight_ref, new_ref, first_ref, second_ref, gradient
):
    gradient[...] = turned_ref[...].astype(jnp.float32).T
    for pair in range(moments_ref.shape[0] // 2):
        even = moments_ref[inverse_ref[2 * pair]].astype(jnp.float32)
        odd = moments_ref[inverse_ref[2 * pair + 1]].astype(jnp.float32)
        rows = pl.ds(pair * 2 * SUB, 2 * SUB)
        new_ref[rows, :], first_ref[rows, :], second_ref[rows, :] = adam(
            weight_ref[rows, :],
            jnp.concatenate([even[:SUB], odd[:SUB]], axis=0),
            jnp.concatenate([even[SUB:], odd[SUB:]], axis=0),
            gradient[rows, :],
        )


def adam_rows(turned, moments, weight_rows, inverse):
    row_block, width = weight_rows.shape
    return pl.pallas_call(
        adam_kernel,
        in_specs=[pl.BlockSpec(memory_space=pltpu.SMEM)]
        + [pl.BlockSpec(memory_space=pltpu.VMEM)] * 3,
        out_specs=[pl.BlockSpec(memory_space=pltpu.VMEM)] * 3,
        out_shape=[
            jax.ShapeDtypeStruct((row_block, width), jnp.bfloat16),
            jax.ShapeDtypeStruct((row_block, width), jnp.float32),
            jax.ShapeDtypeStruct((row_block, width), jnp.float32),
        ],
        scratch_shapes=[pltpu.VMEM((row_block, width), jnp.float32)],
        compiler_params=pltpu.CompilerParams(vmem_limit_bytes=GRANT),
        cost_estimate=cost(20 * row_block * width, 16 * row_block * width),
        name="adam_rows",
    )(inverse, turned, moments, weight_rows)


def body(tokens, cotangent, old_weight, old_first, old_second, old_owner, new_owner):
    devices = lax.axis_size(AXES)
    groups = lax.axis_size("rep")
    shards = lax.axis_size("fsdp")
    features = tokens.shape[1]
    row_block, width = old_weight.shape
    strip = row_block * width // devices
    slot_ids = jnp.arange(devices, dtype=jnp.int32)
    placing = jnp.take(new_owner, slot_ids % shards) * groups + slot_ids // shards
    inverse = jnp.zeros((devices,), jnp.int32).at[old_owner].set(slot_ids)
    own_block = jnp.take(placing, lax.axis_index(AXES))
    by_tile = row_block == devices * SUB and width % 128 == 0 and devices % 2 == 0

    held = lax.all_gather(old_weight, AXES, axis=0, tiled=False)
    if by_tile:
        packed = pack_moments(old_first, old_second, placing)
    else:
        both = jnp.stack([old_first, old_second]).astype(jnp.bfloat16)
        packed = jnp.take(
            jnp.transpose(both.reshape(2, devices, strip), (1, 0, 2)), placing, axis=0
        )
    arrived = lax.all_to_all(packed, AXES, split_axis=0, concat_axis=0, tiled=True)

    partial = grad_blocks(tokens, cotangent, placing, row_block)
    turned = lax.psum_scatter(partial, AXES, scatter_dimension=0, tiled=True).reshape(
        width, row_block
    )
    if by_tile:
        projected, weight_rows = project(tokens, held, inverse, own_block.reshape(1))
        return (projected, *adam_rows(turned, arrived, weight_rows, inverse))
    logical = jnp.transpose(
        jnp.take(held.reshape(devices, devices, strip), inverse, axis=0), (1, 0, 2)
    ).reshape(features, width)
    projected = jnp.dot(tokens, logical, preferred_element_type=jnp.float32).astype(jnp.bfloat16)
    weight_rows = lax.dynamic_slice_in_dim(logical, own_block * row_block, row_block, 0)
    moved = jnp.transpose(jnp.take(arrived, inverse, axis=0), (1, 0, 2))
    first_rows, second_rows = moved.astype(jnp.float32).reshape(2, row_block, width)
    return (projected, *adam(weight_rows, first_rows, second_rows, turned.T.astype(jnp.float32)))


def solution(mesh):
    placed = P(AXES, None)
    return jax.shard_map(
        body,
        mesh=mesh,
        in_specs=(placed,) * 5 + (P(), P()),
        out_specs=(placed,) * 4,
        check_vma=False,
    )
```

time: 364 us -> 293 us (0.80)
  local copies, waits for them, and re-layouts: 153 us -> 4.16 us
  waiting for transfers between devices: 110 us -> 229 us
  other arithmetic: 41.9 us -> 0.02 us
  Pallas kernels: 0 us -> 36.7 us
  matrix products: 31.8 us -> 0 us
    reduce_scatter x2 -> x1, waiting for transfers between devices: 61.6 us -> 168 us  [body(): lax.psum_scatter(partial, AXES, scatter_dimension=0, tiled=True)]
    gather x9 -> x0, local copies, waits for them, and re-layouts: 62.6 us -> none  [the longest x5 50.9 us: body(): jnp.take(tokens.reshape(tok_rows, shards, group_block), new_owner, axis=1)]
    all_gather x1, waiting for transfers between devices: 0.02 us -> 59.8 us  [body(): held = lax.all_gather(old_weight, AXES, axis=0, tiled=False)]
    all_to_all x1, waiting for transfers between devices: 47.5 us -> 0.01 us  [body(): lax.all_to_all(packed, AXES, split_axis=0, concat_axis=0, tiled=True)]
    unnamed x18 -> x12, local copies, waits for them, and re-layouts: 47.3 us -> 2.2 us
    pallas_call x0 -> x4, Pallas kernels: none -> 36.7 us  [the longest x1 16.6 us: project(): pl.pallas_call(project_kernel, grid_spec=pltpu.PrefetchScalarGridSpec(num...]
    dot_general x2 -> x0, matrix products: 31.8 us -> none  [the longest x1 16.9 us: body(): lax.dot_general(tok_order, cotangent, (((0,), (0,)), ((), ())), preferred...]
    reshape x4 -> x0, local copies, waits for them, and re-layouts: 27.4 us -> none  [the longest x1 13.6 us: body(): held = jnp.take(whole.reshape(devices, devices, strip), inverse, axis=0)]
  transfers between devices with their start and end apart: 4 -> 3, of which waited for: 3 -> 2; matrix products, arithmetic and copies ran while one was open for 62% -> 1% of each run, Pallas kernels for 0% -> 12%
where the time goes in v1:
time: 293 us; the launch traced here: 290 us
  waiting for transfers between devices  229 us (78%)
  Pallas kernels  36.7 us (13%)
  between operations  14.8 us (5%)
  starting transfers between devices  6.13 us (2%)
  local copies, waits for them, and re-layouts  4.16 us (1%)
    reduce_scatter x1, waiting for transfers between devices, body(): lax.psum_scatter(partial, AXES, scatter_dimension=0, tiled=True)  168 us
    all_gather x1, waiting for transfers between devices, body(): held = lax.all_gather(old_weight, AXES, axis=0, tiled=False)  59.8 us
    pallas_call x1, Pallas kernels, project(): pl.pallas_call(project_kernel, grid_spec=pltpu.PrefetchScalarGridSpec(num...  16.6 us
    pallas_call x1, Pallas kernels, grad_blocks(): pl.pallas_call(grad_kernel, grid_spec=pltpu.PrefetchScalarGridSpec(num_sc...  15.9 us
    all_to_all x1, starting transfers between devices, body(): lax.all_to_all(packed, AXES, split_axis=0, concat_axis=0, tiled=True)  6.06 us
  transfers between devices with their start and end apart: 3, of which 2 were waited for; matrix products, arithmetic and copies ran while one was open for 1% of the time, Pallas kernels for 12%

profile of v1, /device:TPU:8, one launch (start us, length us, event | category | flops | bytes accessed | tf_op | source)
XLA Modules:
  0.0 290.3 jit_solution(3834348450675479509)
XLA Ops:
  7.2 0.0 copy-start
  7.2 0.0 all-gather.3.cloned.1.call-start
  7.2 0.7 all-gather.3.cloned.1.call-update
  7.9 0.0 reduce-scatter.2.cloned.1.call-start
  8.0 0.0 copy-done
  8.0 0.7 gather_fusion
  8.7 0.0 copy-start.1
  8.7 1.2 copy-done.1
  9.9 0.0 copy-start.3
  9.9 15.9 %weight_gradient.1 = bf16[32,512,256]{2,1,0:T(8,128)(2,1)} custom-call(s32[32]{0:T(128)S(1)} %fusion.order_ref.placing_ref, bf16[1024,8192]{1,0:T(8,128)(2,1)} %refs_3_.1, bf16[1024,8192]{1,0:T(8,128)(2,1)} %refs_3_.1, bf16[1024,8192]{1,0:T(8,128)(2,1)} %refs_3_.1, bf16[1024,8192]{1,0:T(8,128)(2,1)} %refs_3_.1, bf16[1024,512]{1,0:T(8,128)(2,1)S(1)} %copy-done.1), custom_call_target="tpu_custom_call" | custom-call | flops 8589934592 | bytes 26214400 | tf_op jit(solution)/shard_map/weight_gradient/pallas_call | solution.py:54
  25.9 0.0 copy-done.3
  25.9 0.0 copy-start.5
  25.9 0.0 copy-start.4
  25.9 0.0 reduce-scatter.2.cloned.1.call-update
  25.9 2.1 pack_moments.1
  28.0 6.1 %all-to-all-start = ((bf16[32,16,512]{2,1,0:T(8,128)(2,1)}), bf16[32,16,512]{2,1,0:T(8,128)(2,1)S(1)}, u32[]{:S(2)}, u32[]{:S(2)}) async-start(bf16[32,16,512]{2,1,0:T(8,128)(2,1)} %pack_moments.1), calls=%async_computation.1 | async-start | bytes 1048576 | tf_op jit(solution)/shard_map/all_to_all | solution.py:224
  34.1 0.0 copy-done.4
  34.1 0.6 dynamic-slice.2
  34.7 0.0 copy-done.5
  34.7 0.7 scatter_custom_fusion.inverse_ref
  36.0 59.8 %all-gather.3.cloned.1.call-done = bf16[8192,512]{1,0:T(8,128)(2,1)} async-done(((bf16[256,512]{1,0:T(8,128)(2,1)}), bf16[8192,512]{1,0:T(8,128)(2,1)}) %all-gather.3.cloned.1.call-update) | async-done | bytes 8388624 | tf_op jit(solution)/shard_map/all_gather | solution.py:216
  95.8 16.6 %project.1 = (bf16[1024,512]{1,0:T(8,128)(2,1)}, bf16[256,512]{1,0:T(8,128)(2,1)S(1)}) custom-call(s32[32]{0:T(128)S(1)} %scatter_custom_fusion.inverse_ref, s32[1]{0:T(128)S(6)} %select_n.62.own_ref, bf16[1024,8192]{1,0:T(8,128)(2,1)} %refs_3_.1, bf16[32,256,512]{2,1,0:T(8,128)(2,1)} %bitcast.6), custom_call_target="tpu_custom_call" | custom-call | flops 8589934592 | bytes 26214400 | tf_op jit(solution)/shard_map/project/pallas_call | solution.py:131
  112.4 0.0 all-to-all-done.moments_ref
  112.4 168.0 %reduce-scatter.2.cloned.1.call-done = bf16[1,512,256]{2,1,0:T(8,128)(2,1)} async-done(((bf16[32,512,256]{2,1,0:T(8,128)(2,1)}), bf16[1,512,256]{2,1,0:T(8,128)(2,1)}) %reduce-scatter.2.cloned.1.call-update) | async-done | bytes 262160 | tf_op jit(solution)/shard_map/reduce_scatter | solution.py:227
  280.4 0.0 copy-start.2
  280.5 0.9 copy-done.2
  281.4 2.1 adam_rows.1
  (5 shorter events, 0.0 us)
Async XLA Ops:
  7.2 0.8 copy-start
  7.2 88.7 %all-gather.3.cloned.1.call-start = ((), (), s32[]{:S(2)}) async-start(), calls=%async_computation.3 | async-start | bytes 8650752 | tf_op jit(solution)/shard_map/all_gather | solution.py:216
  7.9 272.5 %reduce-scatter.2.cloned.1.call-start = ((), (), s32[]{:S(2)}) async-start(), calls=%async_computation.2 | async-start | bytes 8650752 | tf_op jit(solution)/shard_map/reduce_scatter | solution.py:227
  8.7 1.2 copy-start.1
  9.9 15.9 %copy-start.3 = (s32[32]{0:T(128)}, s32[32]{0:T(128)S(1)}, u32[]{:S(2)}) copy-start(s32[32]{0:T(128)S(1)} %fusion.order_ref.placing_ref) | copy-start | bytes 388
  25.9 8.8 %copy-start.5 = (s32[32]{0:T(128)S(1)}, s32[32]{0:T(128)}, u32[]{:S(2)}) copy-start(s32[32]{0:T(128)} %param.12) | copy-start | bytes 388
  25.9 8.2 %copy-start.4 = (s32[32]{0:T(128)S(1)}, s32[32]{0:T(128)}, u32[]{:S(2)}) copy-start(s32[32]{0:T(128)} %copy-done.3) | copy-start | bytes 388
  28.0 84.4 %all-to-all-start = ((bf16[32,16,512]{2,1,0:T(8,128)(2,1)}), bf16[32,16,512]{2,1,0:T(8,128)(2,1)S(1)}, u32[]{:S(2)}, u32[]{:S(2)}) async-start(bf16[32,16,512]{2,1,0:T(8,128)(2,1)} %pack_moments.1), calls=%async_computation.1 | async-start | bytes 1048576 | tf_op jit(solution)/shard_map/all_to_all | solution.py:224
  280.4 0.9 copy-start.2
Sparse Core Ops, SparseCore 0:
  11.0 84.7 all-gather.2
  98.1 182.2 reduce-scatter.1

commit v2 on v1

v2 whole, which is shorter than its diff:
```python
import functools
import jax
import jax.numpy as jnp
from jax import lax
from jax.experimental import pallas as pl
from jax.experimental.pallas import tpu as pltpu
from jax.sharding import PartitionSpec as P

beta_one = 0.9
beta_two = 0.95
learn_rate = 0.001
decay_rate = 0.1
epsilon = 1e-08
correction_one = 1.0 - 0.9**10
correction_two = 1.0 - 0.95**10

AXES = ("rep", "fsdp")
GRANT = 48 * 1024 * 1024
SUB = 8


def cost(flops, moved):
    return pl.CostEstimate(flops=flops, bytes_accessed=moved, transcendentals=0)


def grad_kernel(order_ref, *refs):
    per_step = order_ref.shape[0] // pl.num_programs(0)
    token_refs, turned_ref, out_refs = refs[:per_step], refs[per_step], refs[per_step + 1 :]
    for step, out_ref in enumerate(out_refs):

        @pl.when(pl.program_id(0) == step)
        def _():
            for slot, token_ref in enumerate(token_refs):
                out_ref[slot] = jnp.dot(
                    turned_ref[...], token_ref[...], preferred_element_type=jnp.float32
                ).astype(out_ref.dtype)


def grad_blocks(tokens, turned, order, row_block, parts):
    rows, features = tokens.shape
    width = turned.shape[0]
    per_step = order.shape[0] // parts
    if row_block % 128:
        whole = jnp.dot(turned, tokens, preferred_element_type=jnp.float32).astype(jnp.bfloat16)
        cut = jnp.transpose(whole.reshape(width, features // row_block, row_block), (1, 0, 2))
        return [jnp.take(cut, part, axis=0) for part in order.reshape(parts, per_step)]

    def token_map(slot):
        return lambda i, order_ref: (0, order_ref[i * per_step + slot])

    block = (per_step, width, row_block)
    return pl.pallas_call(
        grad_kernel,
        grid_spec=pltpu.PrefetchScalarGridSpec(
            num_scalar_prefetch=1,
            grid=(parts,),
            in_specs=[pl.BlockSpec((rows, row_block), token_map(s)) for s in range(per_step)]
            + [pl.BlockSpec((width, rows), lambda i, order_ref: (0, 0))],
            out_specs=[pl.BlockSpec(block, lambda i, order_ref: (0, 0, 0))] * parts,
        ),
        out_shape=[jax.ShapeDtypeStruct(block, jnp.bfloat16)] * parts,
        compiler_params=pltpu.CompilerParams(vmem_limit_bytes=GRANT),
        cost_estimate=cost(
            2 * rows * width * order.shape[0] * row_block,
            2 * order.shape[0] * row_block * (rows + width) + 2 * rows * width,
        ),
        name="weight_gradient",
    )(order, *([tokens] * per_step), turned)


def pack_kernel(placing_ref, first_ref, second_ref, out_ref):
    for slot in range(out_ref.shape[0]):
        rows = pl.ds(pl.multiple_of(placing_ref[slot] * SUB, SUB), SUB)
        pair = jnp.concatenate([first_ref[rows, :], second_ref[rows, :]], axis=0)
        out_ref[slot] = pair.astype(out_ref.dtype)


def pack_moments(first, second, placing):
    devices = placing.shape[0]
    width = first.shape[1]
    return pl.pallas_call(
        pack_kernel,
        in_specs=[
            pl.BlockSpec(memory_space=pltpu.SMEM),
            pl.BlockSpec(memory_space=pltpu.VMEM),
            pl.BlockSpec(memory_space=pltpu.VMEM),
        ],
        out_specs=pl.BlockSpec(memory_space=pltpu.VMEM),
        out_shape=jax.ShapeDtypeStruct((devices, 2 * SUB, width), jnp.bfloat16),
        cost_estimate=cost(0, 12 * first.size),
        name="pack_moments",
    )(placing, first, second)


def project_kernel(counts, owner_ref, own_ref, token_ref, *refs):
    piece_refs = refs[: len(counts)]
    out_ref, rows_ref, held, logical, sems = refs[len(counts) :]
    devices, row_block, _ = held.shape

    @pl.when(pl.program_id(0) == 0)
    def _():
        copies = []
        for piece_ref, count in zip(piece_refs, counts):
            for index in range(count):
                slot = len(copies)
                copies.append(
                    pltpu.make_async_copy(
                        piece_ref.at[index], held.at[owner_ref[slot]], sems.at[slot]
                    )
                )
        for copy in copies:
            copy.start()
        for copy in copies:
            copy.wait()

        def place(pair, carry):
            for block in range(0, devices, 2):
                span = pl.ds(block * SUB, 2 * SUB)
                top = held[2 * pair, span, :]
                low = held[2 * pair + 1, span, :]
                for half in range(2):
                    part = slice(half * SUB, (half + 1) * SUB)
                    start = (block + half) * row_block + pair * 2 * SUB
                    logical[pl.ds(pl.multiple_of(start, 2 * SUB), 2 * SUB), :] = jnp.concatenate(
                        [top[part], low[part]], axis=0
                    )
            return carry

        lax.fori_loop(0, devices // 2, place, 0)
        start = pl.multiple_of(own_ref[0] * row_block, row_block)
        rows_ref[...] = logical[pl.ds(start, row_block), :]

    out_ref[...] = jnp.dot(
        token_ref[...], logical[...], preferred_element_type=jnp.float32
    ).astype(out_ref.dtype)


def project(tokens, pieces, owners, own):
    rows, features = tokens.shape
    _, row_block, width = pieces[0].shape
    devices = owners.shape[0]
    counts = tuple(piece.shape[0] for piece in pieces)
    tile = rows // 4
    return pl.pallas_call(
        functools.partial(project_kernel, counts),
        grid_spec=pltpu.PrefetchScalarGridSpec(
            num_scalar_prefetch=2,
            grid=(rows // tile,),
            in_specs=[pl.BlockSpec((tile, features), lambda i, *_: (i, 0))]
            + [pl.BlockSpec(memory_space=pl.ANY)] * len(pieces),
            out_specs=[
                pl.BlockSpec((tile, width), lambda i, *_: (i, 0)),
                pl.BlockSpec((row_block, width), lambda i, *_: (0, 0)),
            ],
            scratch_shapes=[
                pltpu.VMEM((devices, row_block, width), jnp.bfloat16),
                pltpu.VMEM((features, width), jnp.bfloat16),
                pltpu.SemaphoreType.DMA((devices,)),
            ],
        ),
        out_shape=[
            jax.ShapeDtypeStruct((rows, width), jnp.bfloat16),
            jax.ShapeDtypeStruct((row_block, width), jnp.bfloat16),
        ],
        compiler_params=pltpu.CompilerParams(vmem_limit_bytes=GRANT),
        cost_estimate=cost(
            2 * rows * width * features, 2 * (rows * features + features * width + rows * width)
        ),
        name="project",
    )(owners, own, tokens, *pieces)


def adam(weight_rows, first_rows, second_rows, gradient):
    first_next = beta_one * first_rows + (1.0 - beta_one) * gradient
    second_next = beta_two * second_rows + (1.0 - beta_two) * gradient * gradient
    step_size = first_next / correction_one / (jnp.sqrt(second_next / correction_two) + epsilon)
    updated = (
        weight_rows.astype(jnp.float32) * (1.0 - learn_rate * decay_rate) - learn_rate * step_size
    ).astype(jnp.bfloat16)
    return updated, first_next, second_next


def adam_kernel(inverse_ref, moments_ref, weight_ref, *refs):
    part_refs, (new_ref, first_ref, second_ref, gradient) = refs[:-4], refs[-4:]
    total = part_refs[0][0].astype(jnp.float32)
    for part_ref in part_refs[1:]:
        total = total + part_ref[0].astype(jnp.float32)
    gradient[...] = total.T
    for pair in range(moments_ref.shape[0] // 2):
        even = moments_ref[inverse_ref[2 * pair]].astype(jnp.float32)
        odd = moments_ref[inverse_ref[2 * pair + 1]].astype(jnp.float32)
        rows = pl.ds(pair * 2 * SUB, 2 * SUB)
        new_ref[rows, :], first_ref[rows, :], second_ref[rows, :] = adam(
            weight_ref[rows, :],
            jnp.concatenate([even[:SUB], odd[:SUB]], axis=0),
            jnp.concatenate([even[SUB:], odd[SUB:]], axis=0),
            gradient[rows, :],
        )


def adam_rows(parts, moments, weight_rows, inverse):
    row_block, width = weight_rows.shape
    whole = pl.BlockSpec((row_block, width), lambda i, *_: (0, 0))
    return pl.pallas_call(
        adam_kernel,
        grid_spec=pltpu.PrefetchScalarGridSpec(
            num_scalar_prefetch=1,
            grid=(1,),
            in_specs=[pl.BlockSpec(moments.shape, lambda i, *_: (0, 0, 0)), whole]
            + [pl.BlockSpec((1, width, row_block), lambda i, *_: (0, 0, 0))] * len(parts),
            out_specs=[whole] * 3,
            scratch_shapes=[pltpu.VMEM((row_block, width), jnp.float32)],
        ),
        out_shape=[
            jax.ShapeDtypeStruct((row_block, width), jnp.bfloat16),
            jax.ShapeDtypeStruct((row_block, width), jnp.float32),
            jax.ShapeDtypeStruct((row_block, width), jnp.float32),
        ],
        compiler_params=pltpu.CompilerParams(vmem_limit_bytes=GRANT),
        cost_estimate=cost(20 * row_block * width, 16 * row_block * width),
        name="adam_rows",
    )(inverse, moments, weight_rows, *parts)


class Grid:
    def __init__(self, groups, shards):
        self.shards = shards
        self.cores = 2 if groups % 2 == 0 else 1
        self.minor = 2 if shards % 2 == 0 else 1
        self.outer = groups // self.cores
        self.far = shards // self.minor
        self.swaps = self.cores == 2 and self.minor == self.outer
        self.near, self.side = self.minor, self.outer

    def moved(self, position, core=0, near=0, side=0, far=0):
        group, shard = position // self.shards, position % self.shards
        outer, on = group // self.cores, (group % self.cores + core) % self.cores
        depth, minor = shard // self.minor, shard % self.minor
        swapped = on if self.swaps else 0
        minor = (minor + near + (side - near) * swapped) % self.minor
        outer = (outer + side + (near - side) * swapped) % self.outer
        depth = (depth + far) % self.far
        return (outer * self.cores + on) * self.shards + depth * self.minor + minor

    def send(self, value, **steps):
        devices = self.outer * self.cores * self.shards
        pairs = [(p, self.moved(p, **steps)) for p in range(devices)]
        return lax.ppermute(value, AXES, pairs)


def rounded_sum(*terms):
    total = terms[0].astype(jnp.float32)
    for term in terms[1:]:
        total = total + term.astype(jnp.float32)
    return total.astype(terms[0].dtype)


def reduce_rows(grid, blocks_of):
    near, side = grid.near, grid.side
    last = []
    for far in sorted(range(grid.far), key=lambda k: -min(k, grid.far - k)):
        parts = blocks_of(far)
        terms = [parts[0]]
        for core in range(1, grid.cores):
            terms.append(grid.send(parts[core], core=core))
        kept = list(terms)
        for step in range(1, near):
            cut = slice(step * side, (step + 1) * side)
            kept.append(grid.send(rounded_sum(*[t[cut] for t in terms]), near=step))
        ends = list(kept)
        for step in range(1, side):
            cut = slice(step, step + 1)
            ends.append(grid.send(rounded_sum(*[t[cut] for t in kept]), side=step))
        if far:
            last.append(grid.send(rounded_sum(*[t[:1] for t in ends]), far=far))
        else:
            last.extend(ends)
    return last


def body(tokens, cotangent, old_weight, old_first, old_second, old_owner, new_owner):
    devices = lax.axis_size(AXES)
    groups = lax.axis_size("rep")
    shards = lax.axis_size("fsdp")
    features = tokens.shape[1]
    row_block, width = old_weight.shape
    strip = row_block * width // devices
    grid = Grid(groups, shards)
    me = lax.axis_index(AXES)
    slot_ids = jnp.arange(devices, dtype=jnp.int32)
    placing = jnp.take(new_owner, slot_ids % shards) * groups + slot_ids // shards
    inverse = jnp.zeros((devices,), jnp.int32).at[old_owner].set(slot_ids)
    own_block = jnp.take(placing, me)
    by_tile = row_block == devices * SUB and width % 128 == 0 and devices % 2 == 0

    held = lax.all_gather(old_weight, AXES, axis=0, tiled=False)
    if by_tile:
        packed = pack_moments(old_first, old_second, placing)
    else:
        both = jnp.stack([old_first, old_second]).astype(jnp.bfloat16)
        packed = jnp.take(
            jnp.transpose(both.reshape(2, devices, strip), (1, 0, 2)), placing, axis=0
        )
    arrived = lax.all_to_all(packed, AXES, split_axis=0, concat_axis=0, tiled=True)

    cot_turned = cotangent.T

    def blocks_of(far):
        targets = [
            grid.moved(me, core, near, side, far)
            for core in reversed(range(grid.cores))
            for near in range(grid.near)
            for side in range(grid.side)
        ]
        order = jnp.take(placing, jnp.stack(targets))
        return grad_blocks(tokens, cot_turned, order, row_block, grid.cores)[::-1]

    parts = reduce_rows(grid, blocks_of)
    if by_tile:
        projected, weight_rows = project(tokens, [held], old_owner, own_block.reshape(1))
        return (projected, *adam_rows(parts, arrived, weight_rows, inverse))
    logical = jnp.transpose(
        jnp.take(held.reshape(devices, devices, strip), inverse, axis=0), (1, 0, 2)
    ).reshape(features, width)
    projected = jnp.dot(tokens, logical, preferred_element_type=jnp.float32).astype(jnp.bfloat16)
    weight_rows = lax.dynamic_slice_in_dim(logical, own_block * row_block, row_block, 0)
    moved = jnp.transpose(jnp.take(arrived, inverse, axis=0), (1, 0, 2))
    first_rows, second_rows = moved.astype(jnp.float32).reshape(2, row_block, width)
    gradient = sum(part[0].astype(jnp.float32) for part in parts).T
    return (projected, *adam(weight_rows, first_rows, second_rows, gradient))


def solution(mesh):
    placed = P(AXES, None)
    return jax.shard_map(
        body,
        mesh=mesh,
        in_specs=(placed,) * 5 + (P(), P()),
        out_specs=(placed,) * 4,
        check_vma=False,
    )
```

time: 293 us -> 150 us (0.51)
  the two profiles are of different devices: /device:TPU:8 before, /device:TPU:0 now
where the time goes in v2:
time: 150 us; the launch traced here: 149 us
  Pallas kernels  46.3 us (31%)
  waiting for transfers between devices  37.5 us (25%)
  starting transfers between devices  24.8 us (17%)
  between operations  15.3 us (10%)
  other arithmetic  14.1 us (9%)
  local copies, waits for them, and re-layouts  11.1 us (7%)
    ppermute x15, waiting for transfers between devices, send(): return lax.ppermute(value, AXES, pairs)  36.9 us
    pallas_call x4, Pallas kernels, grad_blocks(): pl.pallas_call(grad_kernel, grid_spec=pltpu.PrefetchScalarGridSpec(num_sc...  22.8 us
    pallas_call x1, Pallas kernels, project(): pl.pallas_call(functools.partial(project_kernel, counts), grid_spec=pltpu...  18.1 us
    ppermute x15, starting transfers between devices, send(): return lax.ppermute(value, AXES, pairs)  17.4 us
    convert_element_type x11, other arithmetic, rounded_sum(): return total.astype(terms[0].dtype)  14 us
    all_to_all x1, starting transfers between devices, body(): lax.all_to_all(packed, AXES, split_axis=0, concat_axis=0, tiled=True)  7.37 us
    unnamed x19, local copies, waits for them, and re-layouts  6.17 us
    pallas_call x1, Pallas kernels, adam_rows(): pl.pallas_call(adam_kernel, grid_spec=pltpu.PrefetchScalarGridSpec(num_sc...  3.37 us
  transfers between devices with their start and end apart: 17, of which 4 were waited for; matrix products, arithmetic and copies ran while one was open for 14% of the time, Pallas kernels for 29%

profile of v2, /device:TPU:0, one launch (start us, length us, event | category | flops | bytes accessed | tf_op | source)
XLA Modules:
  0.0 149.0 jit_solution(14927610943279276201)
XLA Ops:
  7.2 0.0 copy-start
  7.2 0.0 all-gather.3.cloned.1.call-start
  7.2 0.7 all-gather.3.cloned.1.call-update
  8.2 1.5 copy.12
  9.8 0.7 gather_fusion
  10.5 0.1 stack.116
  10.6 0.0 copy-start.7
  10.6 0.6 gather_fusion.1
  11.3 5.7 %weight_gradient.4 = (bf16[4,512,256]{2,1,0:T(8,128)(2,1)}, bf16[4,512,256]{2,1,0:T(8,128)(2,1)S(1)}) custom-call(s32[8]{0:T(128)S(1)} %and_select_fusion.3.order_ref, bf16[1024,8192]{1,0:T(8,128)(2,1)} %refs_3_.7, bf16[1024,8192]{1,0:T(8,128)(2,1)} %refs_3_.7, bf16[1024,8192]{1,0:T(8,128)(2,1)} %refs_3_.7, bf16[1024,8192]{1,0:T(8,128)(2,1)} %refs_3_.7, ...), custom_call_target="tpu_custom_call" | custom-call | flops 2147483648 | bytes 7340032 | tf_op jit(solution)/shard_map/weight_gradient/pallas_call | solution.py:52
  17.0 1.0 copy-done.1
  18.0 0.5 collective-permute-start
  18.5 0.1 stack.125
  18.6 0.7 gather_fusion.2
  19.2 5.7 %weight_gradient.5 = (bf16[4,512,256]{2,1,0:T(8,128)(2,1)}, bf16[4,512,256]{2,1,0:T(8,128)(2,1)S(1)}) custom-call(s32[8]{0:T(128)S(1)} %and_select_fusion.2.order_ref, bf16[1024,8192]{1,0:T(8,128)(2,1)} %refs_3_.7, bf16[1024,8192]{1,0:T(8,128)(2,1)} %refs_3_.7, bf16[1024,8192]{1,0:T(8,128)(2,1)} %refs_3_.7, bf16[1024,8192]{1,0:T(8,128)(2,1)} %refs_3_.7, ...), custom_call_target="tpu_custom_call" | custom-call | flops 2147483648 | bytes 7340032 | tf_op jit(solution)/shard_map/weight_gradient/pallas_call | solution.py:52
  24.9 1.0 copy-done.2
  25.9 0.0 collective-permute-start.4
  26.0 0.1 stack.134
  26.1 0.6 gather_fusion.3
  26.7 5.7 %weight_gradient.6 = (bf16[4,512,256]{2,1,0:T(8,128)(2,1)}, bf16[4,512,256]{2,1,0:T(8,128)(2,1)S(1)}) custom-call(s32[8]{0:T(128)S(1)} %and_select_fusion.1.order_ref, bf16[1024,8192]{1,0:T(8,128)(2,1)} %refs_3_.7, bf16[1024,8192]{1,0:T(8,128)(2,1)} %refs_3_.7, bf16[1024,8192]{1,0:T(8,128)(2,1)} %refs_3_.7, bf16[1024,8192]{1,0:T(8,128)(2,1)} %refs_3_.7, ...), custom_call_target="tpu_custom_call" | custom-call | flops 2147483648 | bytes 7340032 | tf_op jit(solution)/shard_map/weight_gradient/pallas_call | solution.py:52
  32.5 1.0 copy-done.3
  33.5 0.5 collective-permute-start.8
  33.9 0.1 stack.143
  34.0 0.6 gather_fusion.4
  34.7 0.0 copy-start.6
  34.7 5.7 %weight_gradient.7 = (bf16[4,512,256]{2,1,0:T(8,128)(2,1)}, bf16[4,512,256]{2,1,0:T(8,128)(2,1)S(1)}) custom-call(s32[8]{0:T(128)S(1)} %and_select_fusion.order_ref, bf16[1024,8192]{1,0:T(8,128)(2,1)} %refs_3_.7, bf16[1024,8192]{1,0:T(8,128)(2,1)} %refs_3_.7, bf16[1024,8192]{1,0:T(8,128)(2,1)} %refs_3_.7, bf16[1024,8192]{1,0:T(8,128)(2,1)} %refs_3_.7, ...), custom_call_target="tpu_custom_call" | custom-call | flops 2147483648 | bytes 7340032 | tf_op jit(solution)/shard_map/weight_gradient/pallas_call | solution.py:52
  40.4 0.1 collective-permute-start.12
  40.5 2.1 %pack_moments.1 = bf16[32,16,512]{2,1,0:T(8,128)(2,1)} custom-call(s32[32]{0:T(128)} %copy-done.7, f32[256,512]{1,0:T(8,128)} %first_ref.1, f32[256,512]{1,0:T(8,128)} %second_ref.1), custom_call_target="tpu_custom_call" | custom-call | bytes 1572864 | tf_op jit(solution)/shard_map/pack_moments/pallas_call | solution.py:81
  42.5 7.4 %all-to-all-start = ((bf16[32,16,512]{2,1,0:T(8,128)(2,1)}), bf16[32,16,512]{2,1,0:T(8,128)(2,1)S(1)}, u32[]{:S(2)}, u32[]{:S(2)}) async-start(bf16[32,16,512]{2,1,0:T(8,128)(2,1)} %pack_moments.1), calls=%async_computation | async-start | bytes 1048576 | tf_op jit(solution)/shard_map/all_to_all | solution.py:304
  49.9 0.6 dynamic-slice.2
  50.5 0.7 scatter_custom_fusion.inverse_ref
  51.8 1.3 add_convert_fusion.3
  53.2 1.8 %collective-permute-start.1 = (bf16[2,512,256]{2,1,0:T(8,128)(2,1)S(1)}, bf16[2,512,256]{2,1,0:T(8,128)(2,1)S(1)}, u32[]{:S(2)}, u32[]{:S(2)}) collective-permute-start(bf16[2,512,256]{2,1,0:T(8,128)(2,1)S(1)} %add_convert_fusion.3), channel_id=1, source_target_pairs={{0,1},{1,0},{2,3},{3,2},{4,5},{5,4},{6,7},{7,6},{8,24},{9,25},{10,... | collective-permute-start | bytes 1572872 | tf_op jit(solution)/shard_map/ppermute | solution.py:248
  55.0 0.0 collective-permute-done.4
  55.0 1.3 add_convert_fusion.2
  56.3 0.3 collective-permute-start.5
  56.7 1.3 add_convert_fusion.1
  58.0 1.8 %collective-permute-start.9 = (bf16[2,512,256]{2,1,0:T(8,128)(2,1)S(1)}, bf16[2,512,256]{2,1,0:T(8,128)(2,1)S(1)}, u32[]{:S(2)}, u32[]{:S(2)}) collective-permute-start(bf16[2,512,256]{2,1,0:T(8,128)(2,1)S(1)} %add_convert_fusion.1), channel_id=1, source_target_pairs={{0,1},{1,0},{2,3},{3,2},{4,5},{5,4},{6,7},{7,6},{8,24},{9,25},{10,... | collective-permute-start | bytes 1572872 | tf_op jit(solution)/shard_map/ppermute | solution.py:248
  59.8 0.0 collective-permute-done.12.refs_4_
  59.8 0.1 add_convert_fusion
  60.0 0.3 collective-permute-start.13
  60.3 5.3 %collective-permute-done.1 = bf16[2,512,256]{2,1,0:T(8,128)(2,1)S(1)} collective-permute-done((bf16[2,512,256]{2,1,0:T(8,128)(2,1)S(1)}, bf16[2,512,256]{2,1,0:T(8,128)(2,1)S(1)}, u32[]{:S(2)}, u32[]{:S(2)}) %collective-permute-start.1) | collective-permute-done | bytes 524320 | tf_op jit(solution)/shard_map/ppermute | solution.py:248
  65.6 1.1 add_convert_fusion.10
  66.8 1.8 %collective-permute-start.2 = (bf16[1,512,256]{2,1,0:T(8,128)(2,1)S(1)}, bf16[1,512,256]{2,1,0:T(8,128)(2,1)S(1)}, u32[]{:S(2)}, u32[]{:S(2)}) collective-permute-start(bf16[1,512,256]{2,1,0:T(8,128)(2,1)S(1)} %add_convert_fusion.10), channel_id=1, source_target_pairs={{0,16},{1,17},{2,18},{3,19},{4,20},{5,21},{6,22},{7,23},{8,9},{9,8... | collective-permute-start | bytes 786440 | tf_op jit(solution)/shard_map/ppermute | solution.py:248
  68.6 11.2 %collective-permute-done.5 = bf16[2,512,256]{2,1,0:T(8,128)(2,1)S(1)} collective-permute-done((bf16[2,512,256]{2,1,0:T(8,128)(2,1)S(1)}, bf16[2,512,256]{2,1,0:T(8,128)(2,1)S(1)}, u32[]{:S(2)}, u32[]{:S(2)}) %collective-permute-start.5) | collective-permute-done | bytes 524320 | tf_op jit(solution)/shard_map/ppermute | solution.py:248
  79.7 1.1 add_convert_fusion.8
  80.9 1.6 %collective-permute-start.6 = (bf16[1,512,256]{2,1,0:T(8,128)(2,1)S(1)}, bf16[1,512,256]{2,1,0:T(8,128)(2,1)S(1)}, u32[]{:S(2)}, u32[]{:S(2)}) collective-permute-start(bf16[1,512,256]{2,1,0:T(8,128)(2,1)S(1)} %add_convert_fusion.8), channel_id=1, source_target_pairs={{0,16},{1,17},{2,18},{3,19},{4,20},{5,21},{6,22},{7,23},{8,9},{9,8... | collective-permute-start | bytes 786440 | tf_op jit(solution)/shard_map/ppermute | solution.py:248
  82.5 15.3 %collective-permute-done.9 = bf16[2,512,256]{2,1,0:T(8,128)(2,1)S(1)} collective-permute-done((bf16[2,512,256]{2,1,0:T(8,128)(2,1)S(1)}, bf16[2,512,256]{2,1,0:T(8,128)(2,1)S(1)}, u32[]{:S(2)}, u32[]{:S(2)}) %collective-permute-start.9) | collective-permute-done | bytes 524320 | tf_op jit(solution)/shard_map/ppermute | solution.py:248
  97.8 1.1 add_convert_fusion.6
  98.9 1.9 %collective-permute-start.10 = (bf16[1,512,256]{2,1,0:T(8,128)(2,1)S(1)}, bf16[1,512,256]{2,1,0:T(8,128)(2,1)S(1)}, u32[]{:S(2)}, u32[]{:S(2)}) collective-permute-start(bf16[1,512,256]{2,1,0:T(8,128)(2,1)S(1)} %add_convert_fusion.6), channel_id=1, source_target_pairs={{0,16},{1,17},{2,18},{3,19},{4,20},{5,21},{6,22},{7,23},{8,9},{9,8... | collective-permute-start | bytes 786440 | tf_op jit(solution)/shard_map/ppermute | solution.py:248
  100.7 5.1 %collective-permute-done.13.refs_5_ = bf16[2,512,256]{2,1,0:T(8,128)(2,1)S(1)} collective-permute-done((bf16[2,512,256]{2,1,0:T(8,128)(2,1)S(1)}, bf16[2,512,256]{2,1,0:T(8,128)(2,1)S(1)}, u32[]{:S(2)}, u32[]{:S(2)}) %collective-permute-start.13) | collective-permute-done | bytes 524320 | tf_op jit(solution)/shard_map/ppermute | solution.py:248
  105.8 0.8 add_convert_fusion.4
  106.6 1.9 %collective-permute-start.14 = (bf16[1,512,256]{2,1,0:T(8,128)(2,1)}, bf16[1,512,256]{2,1,0:T(8,128)(2,1)S(1)}, u32[]{:S(2)}, u32[]{:S(2)}) collective-permute-start(bf16[1,512,256]{2,1,0:T(8,128)(2,1)} %add_convert_fusion.4), channel_id=1, source_target_pairs={{0,16},{1,17},{2,18},{3,19},{4,20},{5,21},{6,22},{7,23},{8,9},{9,8... | collective-permute-start | bytes 786440 | tf_op jit(solution)/shard_map/ppermute | solution.py:248
  108.5 0.0 collective-permute-done.2
  108.5 1.9 %add_convert_fusion.9 = bf16[1,512,256]{2,1,0:T(8,128)(2,1)} fusion(bf16[1,512,256]{2,1,0:T(8,128)(2,1)S(1)} %collective-permute-done.2, bf16[2,512,256]{2,1,0:T(8,128)(2,1)S(1)} %collective-permute-done.1, bf16[4,512,256]{2,1,0:T(8,128)(2,1)} %collective-permute-done, bf16[4,512,256]{2,1,0:T(8,128)(2,1)} %copy-done.1), kind=kLoop, calls=%fused_computation.15 | loop fusion | flops 1048576 | bytes 1310720 | tf_op jit(solution)/shard_map/convert_element_type | solution.py:255
  110.4 1.1 collective-permute-start.3
  111.4 1.9 %add_convert_fusion.7 = bf16[1,512,256]{2,1,0:T(8,128)(2,1)} fusion(bf16[1,512,256]{2,1,0:T(8,128)(2,1)S(1)} %collective-permute-done.6, bf16[2,512,256]{2,1,0:T(8,128)(2,1)S(1)} %collective-permute-done.5, bf16[4,512,256]{2,1,0:T(8,128)(2,1)} %collective-permute-done.4, bf16[4,512,256]{2,1,0:T(8,128)(2,1)} %copy-done.2), kind=kLoop, calls=%fused_computation.13 | loop fusion | flops 1048576 | bytes 1310720 | tf_op jit(solution)/shard_map/convert_element_type | solution.py:255
  113.3 0.6 collective-permute-start.7
  113.9 1.9 %add_convert_fusion.5 = bf16[1,512,256]{2,1,0:T(8,128)(2,1)} fusion(bf16[1,512,256]{2,1,0:T(8,128)(2,1)S(1)} %collective-permute-done.10, bf16[2,512,256]{2,1,0:T(8,128)(2,1)S(1)} %collective-permute-done.9, bf16[4,512,256]{2,1,0:T(8,128)(2,1)} %collective-permute-done.8, bf16[4,512,256]{2,1,0:T(8,128)(2,1)} %copy-done.3), kind=kLoop, calls=%fused_computation.11 | loop fusion | flops 1048576 | bytes 1310720 | tf_op jit(solution)/shard_map/convert_element_type | solution.py:255
  115.8 3.2 %collective-permute-start.11 = (bf16[1,512,256]{2,1,0:T(8,128)(2,1)}, bf16[1,512,256]{2,1,0:T(8,128)(2,1)}, u32[]{:S(2)}, u32[]{:S(2)}) collective-permute-start(bf16[1,512,256]{2,1,0:T(8,128)(2,1)} %add_convert_fusion.5), channel_id=1, source_target_pairs={{0,6},{1,7},{2,0},{3,1},{4,2},{5,3},{6,4},{7,5},{8,14},{9,15},{10,... | collective-permute-start | bytes 786440 | tf_op jit(solution)/shard_map/ppermute | solution.py:248
  119.0 18.1 %project.1 = (bf16[1024,512]{1,0:T(8,128)(2,1)}, bf16[256,512]{1,0:T(8,128)(2,1)S(1)}) custom-call(s32[32]{0:T(128)S(1)} %copy-done.6, s32[1]{0:T(128)S(6)} %select_n.694.own_ref, bf16[1024,8192]{1,0:T(8,128)(2,1)} %refs_3_.7, bf16[32,256,512]{2,1,0:T(8,128)(2,1)} %bitcast.41), custom_call_target="tpu_custom_call" | custom-call | flops 8589934592 | bytes 26214400 | tf_op jit(solution)/shard_map/project/pallas_call | solution.py:144
  137.1 0.0 copy-start.4
  137.1 0.7 copy-done.4
  137.9 0.9 copy-done.5
  138.8 3.4 %adam_rows.1 = (bf16[256,512]{1,0:T(8,128)(2,1)}, f32[256,512]{1,0:T(8,128)}, f32[256,512]{1,0:T(8,128)}) custom-call(s32[32]{0:T(128)S(1)} %scatter_custom_fusion.inverse_ref, bf16[32,16,512]{2,1,0:T(8,128)(2,1)S(1)} %all-to-all-done.moments_ref, bf16[256,512]{1,0:T(8,128)(2,1)S(1)} %copy-done.5, bf16[1,512,256]{2,1,0:T(8,128)(2,1)} %collective-permute-done.3.refs_0_, ...), custom_call_target="tpu_custom_call" | custom-call | flops 2621440 | bytes 2097152 | tf_op jit(solution)/shard_map/adam_rows/pallas_call | solution.py:204
  (36 shorter events, 0.2 us)
Async XLA Ops:
  7.2 2.6 %copy-start = (s32[8]{0:T(128)S(1)}, s32[8]{0:T(128)}, u32[]{:S(2)}) copy-start(s32[8]{0:T(128)} %param.15) | copy-start | bytes 100
  7.2 111.8 %all-gather.3.cloned.1.call-start = ((), (), s32[]{:S(2)}) async-start(), calls=%async_computation.1 | async-start | bytes 8650752 | tf_op jit(solution)/shard_map/all_gather | solution.py:296
  10.6 23.4 %copy-start.7 = (s32[32]{0:T(128)}, s32[32]{0:T(128)S(1)}, u32[]{:S(2)}) copy-start(s32[32]{0:T(128)S(1)} %fusion.placing_ref) | copy-start | bytes 388
  17.0 1.0 copy-start.1
  18.0 33.8 %collective-permute-start = (bf16[4,512,256]{2,1,0:T(8,128)(2,1)}, bf16[4,512,256]{2,1,0:T(8,128)(2,1)}, u32[]{:S(2)}, u32[]{:S(2)}) collective-permute-start(bf16[4,512,256]{2,1,0:T(8,128)(2,1)} %get-tuple-element.21), channel_id=1, source_target_pairs={{0,8},{1,9},{2,10},{3,11},{4,12},{5,13},{6,14},{7,15},{8,0},{9,1},... | collective-permute-start | bytes 3145736 | tf_op jit(solution)/shard_map/ppermute | solution.py:248
  24.9 1.0 copy-start.2
  25.9 29.1 %collective-permute-start.4 = (bf16[4,512,256]{2,1,0:T(8,128)(2,1)}, bf16[4,512,256]{2,1,0:T(8,128)(2,1)}, u32[]{:S(2)}, u32[]{:S(2)}) collective-permute-start(bf16[4,512,256]{2,1,0:T(8,128)(2,1)} %get-tuple-element.23), channel_id=1, source_target_pairs={{0,8},{1,9},{2,10},{3,11},{4,12},{5,13},{6,14},{7,15},{8,0},{9,1},... | collective-permute-start | bytes 3145736 | tf_op jit(solution)/shard_map/ppermute | solution.py:248
  32.5 1.0 copy-start.3
  33.5 23.2 %collective-permute-start.8 = (bf16[4,512,256]{2,1,0:T(8,128)(2,1)}, bf16[4,512,256]{2,1,0:T(8,128)(2,1)}, u32[]{:S(2)}, u32[]{:S(2)}) collective-permute-start(bf16[4,512,256]{2,1,0:T(8,128)(2,1)} %get-tuple-element.25), channel_id=1, source_target_pairs={{0,8},{1,9},{2,10},{3,11},{4,12},{5,13},{6,14},{7,15},{8,0},{9,1},... | collective-permute-start | bytes 3145736 | tf_op jit(solution)/shard_map/ppermute | solution.py:248
  34.7 15.2 %copy-start.8 = (s32[32]{0:T(128)S(1)}, s32[32]{0:T(128)}, u32[]{:S(2)}) copy-start(s32[32]{0:T(128)} %copy-done.7) | copy-start | bytes 388
  34.7 15.8 %copy-start.6 = (s32[32]{0:T(128)S(1)}, s32[32]{0:T(128)}, u32[]{:S(2)}) copy-start(s32[32]{0:T(128)} %owner_ref.1) | copy-start | bytes 388
  40.4 19.4 %collective-permute-start.12 = (bf16[4,512,256]{2,1,0:T(8,128)(2,1)}, bf16[4,512,256]{2,1,0:T(8,128)(2,1)S(1)}, u32[]{:S(2)}, u32[]{:S(2)}) collective-permute-start(bf16[4,512,256]{2,1,0:T(8,128)(2,1)} %get-tuple-element.27), channel_id=1, source_target_pairs={{0,8},{1,9},{2,10},{3,11},{4,12},{5,13},{6,14},{7,15},{8,0},{9,1},... | collective-permute-start | bytes 3145736 | tf_op jit(solution)/shard_map/ppermute | solution.py:248
  42.5 95.3 %all-to-all-start = ((bf16[32,16,512]{2,1,0:T(8,128)(2,1)}), bf16[32,16,512]{2,1,0:T(8,128)(2,1)S(1)}, u32[]{:S(2)}, u32[]{:S(2)}) async-start(bf16[32,16,512]{2,1,0:T(8,128)(2,1)} %pack_moments.1), calls=%async_computation | async-start | bytes 1048576 | tf_op jit(solution)/shard_map/all_to_all | solution.py:304
  53.2 12.4 %collective-permute-start.1 = (bf16[2,512,256]{2,1,0:T(8,128)(2,1)S(1)}, bf16[2,512,256]{2,1,0:T(8,128)(2,1)S(1)}, u32[]{:S(2)}, u32[]{:S(2)}) collective-permute-start(bf16[2,512,256]{2,1,0:T(8,128)(2,1)S(1)} %add_convert_fusion.3), channel_id=1, source_target_pairs={{0,1},{1,0},{2,3},{3,2},{4,5},{5,4},{6,7},{7,6},{8,24},{9,25},{10,... | collective-permute-start | bytes 1572872 | tf_op jit(solution)/shard_map/ppermute | solution.py:248
  56.3 23.4 %collective-permute-start.5 = (bf16[2,512,256]{2,1,0:T(8,128)(2,1)S(1)}, bf16[2,512,256]{2,1,0:T(8,128)(2,1)S(1)}, u32[]{:S(2)}, u32[]{:S(2)}) collective-permute-start(bf16[2,512,256]{2,1,0:T(8,128)(2,1)S(1)} %add_convert_fusion.2), channel_id=1, source_target_pairs={{0,1},{1,0},{2,3},{3,2},{4,5},{5,4},{6,7},{7,6},{8,24},{9,25},{10,... | collective-permute-start | bytes 1572872 | tf_op jit(solution)/shard_map/ppermute | solution.py:248
  58.0 39.7 %collective-permute-start.9 = (bf16[2,512,256]{2,1,0:T(8,128)(2,1)S(1)}, bf16[2,512,256]{2,1,0:T(8,128)(2,1)S(1)}, u32[]{:S(2)}, u32[]{:S(2)}) collective-permute-start(bf16[2,512,256]{2,1,0:T(8,128)(2,1)S(1)} %add_convert_fusion.1), channel_id=1, source_target_pairs={{0,1},{1,0},{2,3},{3,2},{4,5},{5,4},{6,7},{7,6},{8,24},{9,25},{10,... | collective-permute-start | bytes 1572872 | tf_op jit(solution)/shard_map/ppermute | solution.py:248
  60.0 45.8 %collective-permute-start.13 = (bf16[2,512,256]{2,1,0:T(8,128)(2,1)S(1)}, bf16[2,512,256]{2,1,0:T(8,128)(2,1)S(1)}, u32[]{:S(2)}, u32[]{:S(2)}) collective-permute-start(bf16[2,512,256]{2,1,0:T(8,128)(2,1)S(1)} %add_convert_fusion), channel_id=1, source_target_pairs={{0,1},{1,0},{2,3},{3,2},{4,5},{5,4},{6,7},{7,6},{8,24},{9,25},{10,... | collective-permute-start | bytes 1572872 | tf_op jit(solution)/shard_map/ppermute | solution.py:248
  66.8 41.8 %collective-permute-start.2 = (bf16[1,512,256]{2,1,0:T(8,128)(2,1)S(1)}, bf16[1,512,256]{2,1,0:T(8,128)(2,1)S(1)}, u32[]{:S(2)}, u32[]{:S(2)}) collective-permute-start(bf16[1,512,256]{2,1,0:T(8,128)(2,1)S(1)} %add_convert_fusion.10), channel_id=1, source_target_pairs={{0,16},{1,17},{2,18},{3,19},{4,20},{5,21},{6,22},{7,23},{8,9},{9,8... | collective-permute-start | bytes 786440 | tf_op jit(solution)/shard_map/ppermute | solution.py:248
  80.9 30.6 %collective-permute-start.6 = (bf16[1,512,256]{2,1,0:T(8,128)(2,1)S(1)}, bf16[1,512,256]{2,1,0:T(8,128)(2,1)S(1)}, u32[]{:S(2)}, u32[]{:S(2)}) collective-permute-start(bf16[1,512,256]{2,1,0:T(8,128)(2,1)S(1)} %add_convert_fusion.8), channel_id=1, source_target_pairs={{0,16},{1,17},{2,18},{3,19},{4,20},{5,21},{6,22},{7,23},{8,9},{9,8... | collective-permute-start | bytes 786440 | tf_op jit(solution)/shard_map/ppermute | solution.py:248
  98.9 15.0 %collective-permute-start.10 = (bf16[1,512,256]{2,1,0:T(8,128)(2,1)S(1)}, bf16[1,512,256]{2,1,0:T(8,128)(2,1)S(1)}, u32[]{:S(2)}, u32[]{:S(2)}) collective-permute-start(bf16[1,512,256]{2,1,0:T(8,128)(2,1)S(1)} %add_convert_fusion.6), channel_id=1, source_target_pairs={{0,16},{1,17},{2,18},{3,19},{4,20},{5,21},{6,22},{7,23},{8,9},{9,8... | collective-permute-start | bytes 786440 | tf_op jit(solution)/shard_map/ppermute | solution.py:248
  106.6 31.2 %collective-permute-start.14 = (bf16[1,512,256]{2,1,0:T(8,128)(2,1)}, bf16[1,512,256]{2,1,0:T(8,128)(2,1)S(1)}, u32[]{:S(2)}, u32[]{:S(2)}) collective-permute-start(bf16[1,512,256]{2,1,0:T(8,128)(2,1)} %add_convert_fusion.4), channel_id=1, source_target_pairs={{0,16},{1,17},{2,18},{3,19},{4,20},{5,21},{6,22},{7,23},{8,9},{9,8... | collective-permute-start | bytes 786440 | tf_op jit(solution)/shard_map/ppermute | solution.py:248
  110.4 27.4 %collective-permute-start.3 = (bf16[1,512,256]{2,1,0:T(8,128)(2,1)}, bf16[1,512,256]{2,1,0:T(8,128)(2,1)}, u32[]{:S(2)}, u32[]{:S(2)}) collective-permute-start(bf16[1,512,256]{2,1,0:T(8,128)(2,1)} %add_convert_fusion.9), channel_id=1, source_target_pairs={{0,4},{1,5},{2,6},{3,7},{4,0},{5,1},{6,2},{7,3},{8,12},{9,13},{10,... | collective-permute-start | bytes 786440 | tf_op jit(solution)/shard_map/ppermute | solution.py:248
  113.3 24.5 %collective-permute-start.7 = (bf16[1,512,256]{2,1,0:T(8,128)(2,1)}, bf16[1,512,256]{2,1,0:T(8,128)(2,1)}, u32[]{:S(2)}, u32[]{:S(2)}) collective-permute-start(bf16[1,512,256]{2,1,0:T(8,128)(2,1)} %add_convert_fusion.7), channel_id=1, source_target_pairs={{0,2},{1,3},{2,4},{3,5},{4,6},{5,7},{6,0},{7,1},{8,10},{9,11},{10,... | collective-permute-start | bytes 786440 | tf_op jit(solution)/shard_map/ppermute | solution.py:248
  115.8 22.0 %collective-permute-start.11 = (bf16[1,512,256]{2,1,0:T(8,128)(2,1)}, bf16[1,512,256]{2,1,0:T(8,128)(2,1)}, u32[]{:S(2)}, u32[]{:S(2)}) collective-permute-start(bf16[1,512,256]{2,1,0:T(8,128)(2,1)} %add_convert_fusion.5), channel_id=1, source_target_pairs={{0,6},{1,7},{2,0},{3,1},{4,2},{5,3},{6,4},{7,5},{8,14},{9,15},{10,... | collective-permute-start | bytes 786440 | tf_op jit(solution)/shard_map/ppermute | solution.py:248
  137.1 0.7 copy-start.4
  137.9 1.0 copy-start.5
Sparse Core Ops, SparseCore 0:
  11.0 99.9 all-gather.2

commit v3 on v2

--- a/solution.py
+++ b/solution.py
@@ -1,6 +1,7 @@
 import functools
 import jax
 import jax.numpy as jnp
+import numpy as np
 from jax import lax
 from jax.experimental import pallas as pl
 from jax.experimental.pallas import tpu as pltpu
@@ -23,63 +24,78 @@
     return pl.CostEstimate(flops=flops, bytes_accessed=moved, transcendentals=0)
 
 
-def grad_kernel(order_ref, *refs):
-    per_step = order_ref.shape[0] // pl.num_programs(0)
-    token_refs, turned_ref, out_refs = refs[:per_step], refs[per_step], refs[per_step + 1 :]
+def grad_kernel(per_step, adds, order_ref, *refs):
+    token_refs, turned_ref, refs = refs[:per_step], refs[per_step], refs[per_step + 1 :]
+    out_refs = refs[adds:]
+
+    def write(out_ref):
+        for slot, token_ref in enumerate(token_refs):
+            block = jnp.dot(turned_ref[...], token_ref[...], preferred_element_type=jnp.float32)
+            if adds:
+                block = block + refs[0][slot].astype(jnp.float32)
+            out_ref[slot] = block.astype(out_ref.dtype)
+
+    if len(out_refs) == 1:
+        write(out_refs[0])
+        return
     for step, out_ref in enumerate(out_refs):
-
-        @pl.when(pl.program_id(0) == step)
-        def _():
-            for slot, token_ref in enumerate(token_refs):
-                out_ref[slot] = jnp.dot(
-                    turned_ref[...], token_ref[...], preferred_element_type=jnp.float32
-                ).astype(out_ref.dtype)
-
-
-def grad_blocks(tokens, turned, order, row_block, parts):
+        pl.when(pl.program_id(0) == step)(functools.partial(write, out_ref))
+
+
+def grad_blocks(tokens, turned, order, first, steps, per_step, row_block, addend=None, cut=False):
     rows, features = tokens.shape
     width = turned.shape[0]
-    per_step = order.shape[0] // parts
+    blocks = steps * per_step
     if row_block % 128:
-        whole = jnp.dot(turned, tokens, preferred_element_type=jnp.float32).astype(jnp.bfloat16)
-        cut = jnp.transpose(whole.reshape(width, features // row_block, row_block), (1, 0, 2))
-        return [jnp.take(cut, part, axis=0) for part in order.reshape(parts, per_step)]
+        whole = jnp.dot(turned, tokens, preferred_element_type=jnp.float32)
+        parts = jnp.transpose(whole.reshape(width, features // row_block, row_block), (1, 0, 2))
+        parts = jnp.take(parts, order[first : first + blocks], axis=0)
+        if addend is not None:
+            parts = parts + addend.astype(jnp.float32)
+        parts = parts.astype(jnp.bfloat16)
+        return list(jnp.split(parts, steps)) if cut else [parts]
 
     def token_map(slot):
-        return lambda i, order_ref: (0, order_ref[i * per_step + slot])
-
-    block = (per_step, width, row_block)
+        return lambda i, order_ref: (0, order_ref[first + i * per_step + slot])
+
+    block = pl.BlockSpec((per_step, width, row_block), lambda i, order_ref: (i, 0, 0))
+    fixed = pl.BlockSpec((per_step, width, row_block), lambda i, order_ref: (0, 0, 0))
+    added = [] if addend is None else [addend]
+    outs = steps if cut else 1
     return pl.pallas_call(
-        grad_kernel,
+        functools.partial(grad_kernel, per_step, len(added)),
         grid_spec=pltpu.PrefetchScalarGridSpec(
             num_scalar_prefetch=1,
-            grid=(parts,),
+            grid=(steps,),
             in_specs=[pl.BlockSpec((rows, row_block), token_map(s)) for s in range(per_step)]
-            + [pl.BlockSpec((width, rows), lambda i, order_ref: (0, 0))],
-            out_specs=[pl.BlockSpec(block, lambda i, order_ref: (0, 0, 0))] * parts,
-        ),
-        out_shape=[jax.ShapeDtypeStruct(block, jnp.bfloat16)] * parts,
+            + [pl.BlockSpec((width, rows), lambda i, order_ref: (0, 0))]
+            + [block] * len(added),
+            out_specs=[fixed if cut else block] * outs,
+        ),
+        out_shape=[jax.ShapeDtypeStruct((blocks // outs, width, row_block), jnp.bfloat16)] * outs,
         compiler_params=pltpu.CompilerParams(vmem_limit_bytes=GRANT),
         cost_estimate=cost(
-            2 * rows * width * order.shape[0] * row_block,
-            2 * order.shape[0] * row_block * (rows + width) + 2 * rows * width,
+            2 * rows * width * blocks * row_block,
+            2 * blocks * row_block * (rows + width * (1 + len(added))) + 2 * rows * width,
         ),
         name="weight_gradient",
-    )(order, *([tokens] * per_step), turned)
-
-
-def pack_kernel(placing_ref, first_ref, second_ref, out_ref):
+    )(order, *([tokens] * per_step), turned, *added)
+
+
+def pack_kernel(groups, new_ref, first_ref, second_ref, out_ref):
+    shards = new_ref.shape[0]
     for slot in range(out_ref.shape[0]):
-        rows = pl.ds(pl.multiple_of(placing_ref[slot] * SUB, SUB), SUB)
+        block = new_ref[slot % shards] * groups + slot // shards
+        rows = pl.ds(pl.multiple_of(block * SUB, SUB), SUB)
         pair = jnp.concatenate([first_ref[rows, :], second_ref[rows, :]], axis=0)
         out_ref[slot] = pair.astype(out_ref.dtype)
 
 
-def pack_moments(first, second, placing):
-    devices = placing.shape[0]
+def pack_moments(first, second, new_owner, groups):
+    devices = new_owner.shape[0] * groups
     width = first.shape[1]
     return pl.pallas_call(
-        pack_kernel,
+        functools.partial(pack_kernel, groups),
         in_specs=[
             pl.BlockSpec(memory_space=pltpu.SMEM),
             pl.BlockSpec(memory_space=pltpu.VMEM),
@@ -89,10 +105,10 @@
         out_shape=jax.ShapeDtypeStruct((devices, 2 * SUB, width), jnp.bfloat16),
         cost_estimate=cost(0, 12 * first.size),
         name="pack_moments",
-    )(placing, first, second)
-
-
-def project_kernel(counts, owner_ref, own_ref, token_ref, *refs):
+    )(new_owner, first, second)
+
+
+def project_kernel(counts, owner_ref, order_ref, token_ref, *refs):
     piece_refs = refs[: len(counts)]
     out_ref, rows_ref, held, logical, sems = refs[len(counts) :]
     devices, row_block, _ = held.shape
@@ -100,14 +116,14 @@
     @pl.when(pl.program_id(0) == 0)
     def _():
         copies = []
+        start = 0
         for piece_ref, count in zip(piece_refs, counts):
-            for index in range(count):
-                slot = len(copies)
+            for slot in range(devices):
+                target = held.at[owner_ref[slot], pl.ds(start, count)]
                 copies.append(
-                    pltpu.make_async_copy(
-                        piece_ref.at[index], held.at[owner_ref[slot]], sems.at[slot]
-                    )
+                    pltpu.make_async_copy(piece_ref.at[slot], target, sems.at[len(copies)])
                 )
+            start += count
         for copy in copies:
             copy.start()
         for copy in copies:
@@ -127,7 +143,7 @@
             return carry
 
         lax.fori_loop(0, devices // 2, place, 0)
-        start = pl.multiple_of(own_ref[0] * row_block, row_block)
+        start = pl.multiple_of(order_ref[0] * row_block, row_block)
         rows_ref[...] = logical[pl.ds(start, row_block), :]
 
     out_ref[...] = jnp.dot(
@@ -135,11 +151,11 @@
     ).astype(out_ref.dtype)
 
 
-def project(tokens, pieces, owners, own):
+def project(tokens, pieces, owners, order):
     rows, features = tokens.shape
-    _, row_block, width = pieces[0].shape
-    devices = owners.shape[0]
-    counts = tuple(piece.shape[0] for piece in pieces)
+    devices, _, width = pieces[0].shape
+    counts = tuple(piece.shape[1] for piece in pieces)
+    row_block = sum(counts)
     tile = rows // 4
     return pl.pallas_call(
         functools.partial(project_kernel, counts),
@@ -155,7 +171,7 @@
             scratch_shapes=[
                 pltpu.VMEM((devices, row_block, width), jnp.bfloat16),
                 pltpu.VMEM((features, width), jnp.bfloat16),
-                pltpu.SemaphoreType.DMA((devices,)),
+                pltpu.SemaphoreType.DMA((devices * len(pieces),)),
             ],
         ),
         out_shape=[
@@ -167,7 +183,7 @@
             2 * rows * width * features, 2 * (rows * features + features * width + rows * width)
         ),
         name="project",
-    )(owners, own, tokens, *pieces)
+    )(owners, order, tokens, *pieces)
 
 
 def adam(weight_rows, first_rows, second_rows, gradient):
@@ -180,8 +196,10 @@
     return updated, first_next, second_next
 
 
-def adam_kernel(inverse_ref, moments_ref, weight_ref, *refs):
-    part_refs, (new_ref, first_ref, second_ref, gradient) = refs[:-4], refs[-4:]
+def adam_kernel(owner_ref, moments_ref, weight_ref, *refs):
+    part_refs, (new_ref, first_ref, second_ref, gradient, inverse_ref) = refs[:-5], refs[-5:]
+    for slot in range(moments_ref.shape[0]):
+        inverse_ref[owner_ref[slot]] = slot
     total = part_refs[0][0].astype(jnp.float32)
     for part_ref in part_refs[1:]:
         total = total + part_ref[0].astype(jnp.float32)
@@ -198,7 +216,7 @@
         )
 
 
-def adam_rows(parts, moments, weight_rows, inverse):
+def adam_rows(parts, moments, weight_rows, owners):
     row_block, width = weight_rows.shape
     whole = pl.BlockSpec((row_block, width), lambda i, *_: (0, 0))
     return pl.pallas_call(
@@ -209,7 +227,10 @@
             in_specs=[pl.BlockSpec(moments.shape, lambda i, *_: (0, 0, 0)), whole]
             + [pl.BlockSpec((1, width, row_block), lambda i, *_: (0, 0, 0))] * len(parts),
             out_specs=[whole] * 3,
-            scratch_shapes=[pltpu.VMEM((row_block, width), jnp.float32)],
+            scratch_shapes=[
+                pltpu.VMEM((row_block, width), jnp.float32),
+                pltpu.SMEM((moments.shape[0],), jnp.int32),
+            ],
         ),
         out_shape=[
             jax.ShapeDtypeStruct((row_block, width), jnp.bfloat16),
@@ -219,7 +240,7 @@
         compiler_params=pltpu.CompilerParams(vmem_limit_bytes=GRANT),
         cost_estimate=cost(20 * row_block * width, 16 * row_block * width),
         name="adam_rows",
-    )(inverse, moments, weight_rows, *parts)
+    )(owners, moments, weight_rows, *parts)
 
 
 class Grid:
@@ -255,20 +276,33 @@
     return total.astype(terms[0].dtype)
 
 
+def far_first(grid):
+    return sorted(range(grid.far), key=lambda k: -min(k, grid.far - k))
+
+
+def order_table(grid):
+    steps = [
+        dict(core=core, near=near, side=side, far=far)
+        for far in range(grid.far)
+        for core in range(grid.cores)
+        for near in [*range(1, grid.near), 0]
+        for side in range(grid.side)
+    ]
+    return np.array([[grid.moved(p, **step) for step in steps] for p in range(len(steps))], np.int32)
+
+
 def reduce_rows(grid, blocks_of):
-    near, side = grid.near, grid.side
     last = []
-    for far in sorted(range(grid.far), key=lambda k: -min(k, grid.far - k)):
-        parts = blocks_of(far)
-        terms = [parts[0]]
-        for core in range(1, grid.cores):
-            terms.append(grid.send(parts[core], core=core))
-        kept = list(terms)
-        for step in range(1, near):
-            cut = slice(step * side, (step + 1) * side)
-            kept.append(grid.send(rounded_sum(*[t[cut] for t in terms]), near=step))
+    for far in far_first(grid):
+        addend = None
+        if grid.cores > 1:
+            addend = grid.send(blocks_of(1, far, None, False)[0], core=1)
+        parts = blocks_of(0, far, addend, True)
+        kept = [parts[-1]]
+        for step, part in enumerate(parts[:-1], 1):
+            kept.append(grid.send(part, near=step))
         ends = list(kept)
-        for step in range(1, side):
+        for step in range(1, grid.side):
             cut = slice(step, step + 1)
             ends.append(grid.send(rounded_sum(*[t[cut] for t in kept]), side=step))
         if far:
@@ -287,43 +321,49 @@
     strip = row_block * width // devices
     grid = Grid(groups, shards)
     me = lax.axis_index(AXES)
-    slot_ids = jnp.arange(devices, dtype=jnp.int32)
-    placing = jnp.take(new_owner, slot_ids % shards) * groups + slot_ids // shards
-    inverse = jnp.zeros((devices,), jnp.int32).at[old_owner].set(slot_ids)
-    own_block = jnp.take(placing, me)
     by_tile = row_block == devices * SUB and width % 128 == 0 and devices % 2 == 0
 
-    held = lax.all_gather(old_weight, AXES, axis=0, tiled=False)
+    table = lax.dynamic_index_in_dim(jnp.asarray(order_table(grid)), me, 0, keepdims=False)
+    chosen = (table % shards)[:, None] == jnp.arange(shards, dtype=jnp.int32)
+    order = jnp.sum(jnp.where(chosen, new_owner, 0), axis=1) * groups + table // shards
+    own = (grid.near - 1) * grid.side
+    per_core = grid.near * grid.side
+
     if by_tile:
-        packed = pack_moments(old_first, old_second, placing)
+        half = row_block // 2
+        held = [
+            lax.all_gather(old_weight[start : start + half], AXES, axis=0, tiled=False)
+            for start in (0, half)
+        ]
+        packed = pack_moments(old_first, old_second, new_owner, groups)
     else:
+        held = lax.all_gather(old_weight, AXES, axis=0, tiled=False)
+        slot_ids = jnp.arange(devices, dtype=jnp.int32)
+        placing = jnp.take(new_owner, slot_ids % shards) * groups + slot_ids // shards
         both = jnp.stack([old_first, old_second]).astype(jnp.bfloat16)
         packed = jnp.take(
             jnp.transpose(both.reshape(2, devices, strip), (1, 0, 2)), placing, axis=0
         )
     arrived = lax.all_to_all(packed, AXES, split_axis=0, concat_axis=0, tiled=True)
 
-    cot_turned = cotangent.T
-
-    def blocks_of(far):
-        targets = [
-            grid.moved(me, core, near, side, far)
-            for core in reversed(range(grid.cores))
-            for near in range(grid.near)
-            for side in range(grid.side)
-        ]
-        order = jnp.take(placing, jnp.stack(targets))
-        return grad_blocks(tokens, cot_turned, order, row_block, grid.cores)[::-1]
+    turned = cotangent.T
+
+    def blocks_of(core, far, addend, cut):
+        first = (far * grid.cores + core) * per_core
+        return grad_blocks(
+            tokens, turned, order, first, grid.near, grid.side, row_block, addend, cut
+        )
 
     parts = reduce_rows(grid, blocks_of)
     if by_tile:
-        projected, weight_rows = project(tokens, [held], old_owner, own_block.reshape(1))
-        return (projected, *adam_rows(parts, arrived, weight_rows, inverse))
+        projected, weight_rows = project(tokens, held, old_owner, order[own : own + 1])
+        return (projected, *adam_rows(parts, arrived, weight_rows, old_owner))
+    inverse = jnp.zeros((devices,), jnp.int32).at[old_owner].set(slot_ids)
     logical = jnp.transpose(
         jnp.take(held.reshape(devices, devices, strip), inverse, axis=0), (1, 0, 2)
     ).reshape(features, width)
     projected = jnp.dot(tokens, logical, preferred_element_type=jnp.float32).astype(jnp.bfloat16)
-    weight_rows = lax.dynamic_slice_in_dim(logical, own_block * row_block, row_block, 0)
+    weight_rows = lax.dynamic_slice_in_dim(logical, order[own] * row_block, row_block, 0)
     moved = jnp.transpose(jnp.take(arrived, inverse, axis=0), (1, 0, 2))
     first_rows, second_rows = moved.astype(jnp.float32).reshape(2, row_block, width)
     gradient = sum(part[0].astype(jnp.float32) for part in parts).T

time: 150 us -> 193 us (1.29)
  the two profiles are of different devices: /device:TPU:0 before, /device:TPU:8 now
where the time goes in v3:
time: 193 us; the launch traced here: 191 us
  waiting for transfers between devices  82.3 us (43%)
  Pallas kernels  57.6 us (30%)
  starting transfers between devices  21.3 us (11%)
  between operations  14.2 us (7%)
  other arithmetic  7.93 us (4%)
  local copies, waits for them, and re-layouts  7.62 us (4%)
    all_gather x2, waiting for transfers between devices, body(): lax.all_gather(old_weight[start:start + half], AXES, axis=0, tiled=False)  60.3 us
    pallas_call x8, Pallas kernels, grad_blocks(): pl.pallas_call(functools.partial(grad_kernel, per_step, len(added)), grid...  29.3 us
    pallas_call x1, Pallas kernels, project(): pl.pallas_call(functools.partial(project_kernel, counts), grid_spec=pltpu...  24 us
    ppermute x15, waiting for transfers between devices, send(): return lax.ppermute(value, AXES, pairs)  21.3 us
    ppermute x15, starting transfers between devices, send(): return lax.ppermute(value, AXES, pairs)  15.2 us
    all_to_all x1, starting transfers between devices, body(): lax.all_to_all(packed, AXES, split_axis=0, concat_axis=0, tiled=True)  6.04 us
    convert_element_type x7, other arithmetic, rounded_sum(): return total.astype(terms[0].dtype)  5.78 us
    unnamed x13, local copies, waits for them, and re-layouts  5.3 us
  transfers between devices with their start and end apart: 18, of which 3 were waited for; matrix products, arithmetic and copies ran while one was open for 5% of the time, Pallas kernels for 29%

profile of v3, /device:TPU:8, one launch (start us, length us, event | category | flops | bytes accessed | tf_op | source)
XLA Modules:
  0.0 191.0 jit_solution(4094529157903642120)
XLA Ops:
  7.2 0.0 all-gather.7.cloned.1.call-start
  7.2 1.7 fusion
  8.9 0.0 all-gather.7.cloned.1.call-update
  8.9 0.0 all-gather.5.cloned.1.call-start
  9.0 0.7 all-gather.5.cloned.1.call-update
  9.7 1.5 copy.13
  11.2 0.7 and_select_fusion.1
  11.9 0.7 select_reduce_fusion
  12.6 0.7 multiply_add_fusion.order_ref
  13.3 3.2 %weight_gradient.8 = bf16[4,512,256]{2,1,0:T(8,128)(2,1)S(1)} custom-call(s32[32]{0:T(128)S(1)} %multiply_add_fusion.order_ref, bf16[1024,8192]{1,0:T(8,128)(2,1)} %refs_1_.15, bf16[1024,8192]{1,0:T(8,128)(2,1)} %refs_1_.15, bf16[512,1024]{1,0:T(8,128)(2,1)S(1)} %bitcast.20), custom_call_target="tpu_custom_call" | custom-call | flops 1073741824 | bytes 4194304 | tf_op jit(solution)/shard_map/weight_gradient/pallas_call | solution.py:65
  16.6 0.1 collective-permute-start
  16.6 3.2 %weight_gradient.10 = bf16[4,512,256]{2,1,0:T(8,128)(2,1)S(1)} custom-call(s32[32]{0:T(128)S(1)} %multiply_add_fusion.order_ref, bf16[1024,8192]{1,0:T(8,128)(2,1)} %refs_1_.15, bf16[1024,8192]{1,0:T(8,128)(2,1)} %refs_1_.15, bf16[512,1024]{1,0:T(8,128)(2,1)S(1)} %bitcast.21), custom_call_target="tpu_custom_call" | custom-call | flops 1073741824 | bytes 4194304 | tf_op jit(solution)/shard_map/weight_gradient/pallas_call | solution.py:65
  19.9 0.6 collective-permute-start.4
  20.5 4.0 %weight_gradient.12 = bf16[4,512,256]{2,1,0:T(8,128)(2,1)} custom-call(s32[32]{0:T(128)S(1)} %multiply_add_fusion.order_ref, bf16[1024,8192]{1,0:T(8,128)(2,1)} %refs_1_.15, bf16[1024,8192]{1,0:T(8,128)(2,1)} %refs_1_.15, bf16[512,1024]{1,0:T(8,128)(2,1)S(1)} %bitcast.22), custom_call_target="tpu_custom_call" | custom-call | flops 1073741824 | bytes 4194304 | tf_op jit(solution)/shard_map/weight_gradient/pallas_call | solution.py:65
  24.5 0.0 collective-permute-start.8
  24.5 4.0 %weight_gradient.14 = bf16[4,512,256]{2,1,0:T(8,128)(2,1)} custom-call(s32[32]{0:T(128)S(1)} %multiply_add_fusion.order_ref, bf16[1024,8192]{1,0:T(8,128)(2,1)} %refs_1_.15, bf16[1024,8192]{1,0:T(8,128)(2,1)} %refs_1_.15, bf16[512,1024]{1,0:T(8,128)(2,1)S(1)} %bitcast.23), custom_call_target="tpu_custom_call" | custom-call | flops 1073741824 | bytes 4194304 | tf_op jit(solution)/shard_map/weight_gradient/pallas_call | solution.py:65
  28.6 0.5 collective-permute-start.12
  29.0 0.0 collective-permute-done.refs_3_
  29.1 4.0 %weight_gradient.9 = (bf16[2,512,256]{2,1,0:T(8,128)(2,1)}, bf16[2,512,256]{2,1,0:T(8,128)(2,1)S(1)}) custom-call(s32[32]{0:T(128)S(1)} %multiply_add_fusion.order_ref, bf16[1024,8192]{1,0:T(8,128)(2,1)} %refs_1_.15, bf16[1024,8192]{1,0:T(8,128)(2,1)} %refs_1_.15, bf16[512,1024]{1,0:T(8,128)(2,1)S(1)} %bitcast.24, ...), custom_call_target="tpu_custom_call" | custom-call | flops 1073741824 | bytes 5242880 | tf_op jit(solution)/shard_map/weight_gradient/pallas_call | solution.py:65
  33.1 0.8 copy-done
  33.9 1.5 collective-permute-start.1
  35.3 0.0 collective-permute-done.4.refs_3_
  35.3 4.1 %weight_gradient.11 = (bf16[2,512,256]{2,1,0:T(8,128)(2,1)}, bf16[2,512,256]{2,1,0:T(8,128)(2,1)S(1)}) custom-call(s32[32]{0:T(128)S(1)} %multiply_add_fusion.order_ref, bf16[1024,8192]{1,0:T(8,128)(2,1)} %refs_1_.15, bf16[1024,8192]{1,0:T(8,128)(2,1)} %refs_1_.15, bf16[512,1024]{1,0:T(8,128)(2,1)S(1)} %bitcast.25, ...), custom_call_target="tpu_custom_call" | custom-call | flops 1073741824 | bytes 5242880 | tf_op jit(solution)/shard_map/weight_gradient/pallas_call | solution.py:65
  39.4 0.8 copy-done.2
  40.2 0.5 collective-permute-start.5
  40.8 2.1 %pack_moments.1 = bf16[32,16,512]{2,1,0:T(8,128)(2,1)} custom-call(s32[8]{0:T(128)} %new_ref.1, f32[256,512]{1,0:T(8,128)} %first_ref.1, f32[256,512]{1,0:T(8,128)} %second_ref.1), custom_call_target="tpu_custom_call" | custom-call | bytes 1572864 | tf_op jit(solution)/shard_map/pack_moments/pallas_call | solution.py:97
  42.8 6.0 %all-to-all-start = ((bf16[32,16,512]{2,1,0:T(8,128)(2,1)}), bf16[32,16,512]{2,1,0:T(8,128)(2,1)S(1)}, u32[]{:S(2)}, u32[]{:S(2)}) async-start(bf16[32,16,512]{2,1,0:T(8,128)(2,1)} %pack_moments.1), calls=%async_computation | async-start | bytes 1048576 | tf_op jit(solution)/shard_map/all_to_all | solution.py:347
  48.9 0.6 slice.51.order_ref
  49.5 0.0 collective-permute-done.8.refs_3_
  49.5 3.4 %weight_gradient.13 = (bf16[2,512,256]{2,1,0:T(8,128)(2,1)S(1)}, bf16[2,512,256]{2,1,0:T(8,128)(2,1)S(1)}) custom-call(s32[32]{0:T(128)S(1)} %multiply_add_fusion.order_ref, bf16[1024,8192]{1,0:T(8,128)(2,1)} %refs_1_.15, bf16[1024,8192]{1,0:T(8,128)(2,1)} %refs_1_.15, bf16[512,1024]{1,0:T(8,128)(2,1)S(1)} %bitcast.26, ...), custom_call_target="tpu_custom_call" | custom-call | flops 1073741824 | bytes 5242880 | tf_op jit(solution)/shard_map/weight_gradient/pallas_call | solution.py:65
  53.0 1.5 collective-permute-start.9
  54.5 0.0 collective-permute-done.12.refs_3_
  54.5 3.3 %weight_gradient.15 = (bf16[2,512,256]{2,1,0:T(8,128)(2,1)S(1)}, bf16[2,512,256]{2,1,0:T(8,128)(2,1)S(1)}) custom-call(s32[32]{0:T(128)S(1)} %multiply_add_fusion.order_ref, bf16[1024,8192]{1,0:T(8,128)(2,1)} %refs_1_.15, bf16[1024,8192]{1,0:T(8,128)(2,1)} %refs_1_.15, bf16[512,1024]{1,0:T(8,128)(2,1)S(1)} %bitcast.27, ...), custom_call_target="tpu_custom_call" | custom-call | flops 1073741824 | bytes 5242880 | tf_op jit(solution)/shard_map/weight_gradient/pallas_call | solution.py:65
  57.8 0.0 copy-start.4
  57.8 0.6 collective-permute-start.13
  58.4 0.0 collective-permute-done.1
  58.4 1.0 add_convert_fusion.6
  59.4 1.5 collective-permute-start.2
  61.0 0.0 collective-permute-done.5
  61.0 1.0 add_convert_fusion.4
  62.0 0.6 collective-permute-start.6
  62.6 12.5 %collective-permute-done.9 = bf16[2,512,256]{2,1,0:T(8,128)(2,1)S(1)} collective-permute-done((bf16[2,512,256]{2,1,0:T(8,128)(2,1)S(1)}, bf16[2,512,256]{2,1,0:T(8,128)(2,1)S(1)}, u32[]{:S(2)}, u32[]{:S(2)}) %collective-permute-start.9) | collective-permute-done | bytes 524320 | tf_op jit(solution)/shard_map/ppermute | solution.py:269
  75.1 0.1 add_convert_fusion.2
  75.2 1.5 collective-permute-start.10
  76.7 8.7 %collective-permute-done.13.refs_4_ = bf16[2,512,256]{2,1,0:T(8,128)(2,1)S(1)} collective-permute-done((bf16[2,512,256]{2,1,0:T(8,128)(2,1)S(1)}, bf16[2,512,256]{2,1,0:T(8,128)(2,1)S(1)}, u32[]{:S(2)}, u32[]{:S(2)}) %collective-permute-start.13) | collective-permute-done | bytes 524320 | tf_op jit(solution)/shard_map/ppermute | solution.py:269
  85.4 0.1 add_convert_fusion
  85.5 1.5 collective-permute-start.14
  87.0 0.0 collective-permute-done.2
  87.0 1.1 add_convert_fusion.5
  88.1 2.7 %collective-permute-start.3 = (bf16[1,512,256]{2,1,0:T(8,128)(2,1)S(1)}, bf16[1,512,256]{2,1,0:T(8,128)(2,1)S(1)}, u32[]{:S(2)}, u32[]{:S(2)}) collective-permute-start(bf16[1,512,256]{2,1,0:T(8,128)(2,1)S(1)} %add_convert_fusion.5), channel_id=1, source_target_pairs={{0,4},{1,5},{2,6},{3,7},{4,0},{5,1},{6,2},{7,3},{8,12},{9,13},{10,... | collective-permute-start | bytes 786440 | tf_op jit(solution)/shard_map/ppermute | solution.py:269
  90.8 0.0 collective-permute-done.6
  90.8 1.8 add_convert_fusion.3
  92.5 0.0 collective-permute-start.7
  92.5 0.0 collective-permute-done.10
  92.5 0.8 add_convert_fusion.1
  93.3 2.0 %collective-permute-start.11 = (bf16[1,512,256]{2,1,0:T(8,128)(2,1)}, bf16[1,512,256]{2,1,0:T(8,128)(2,1)S(1)}, u32[]{:S(2)}, u32[]{:S(2)}) collective-permute-start(bf16[1,512,256]{2,1,0:T(8,128)(2,1)} %add_convert_fusion.1), channel_id=1, source_target_pairs={{0,6},{1,7},{2,0},{3,1},{4,2},{5,3},{6,4},{7,5},{8,14},{9,15},{10,... | collective-permute-start | bytes 786440 | tf_op jit(solution)/shard_map/ppermute | solution.py:269
  95.4 60.3 %all-gather.5.cloned.1.call-done = bf16[4096,512]{1,0:T(8,128)(2,1)} async-done(((bf16[128,512]{1,0:T(8,128)(2,1)}), bf16[4096,512]{1,0:T(8,128)(2,1)}) %all-gather.5.cloned.1.call-update) | async-done | bytes 4194320 | tf_op jit(solution)/shard_map/all_gather | solution.py:335
  155.7 2.2 %copy-done.5 = bf16[4096,512]{1,0:T(8,128)(2,1)S(1)} copy-done((bf16[4096,512]{1,0:T(8,128)(2,1)S(1)}, bf16[4096,512]{1,0:T(8,128)(2,1)}, u32[]{:S(2)}) %copy-start.5) | copy-done | bytes 4194328
  157.9 24.0 %project.1 = (bf16[1024,512]{1,0:T(8,128)(2,1)}, bf16[256,512]{1,0:T(8,128)(2,1)S(1)}) custom-call(s32[32]{0:T(128)S(1)} %copy-done.4, s32[1]{0:T(128)} %slice.51.order_ref, bf16[1024,8192]{1,0:T(8,128)(2,1)} %refs_1_.15, bf16[32,128,512]{2,1,0:T(8,128)(2,1)S(1)} %bitcast.28, bf16[32,128,512]{2,1,0:T(8,128)(2,1)} %bitcast.29), custom_call_target="tpu_custom_call" | custom-call | flops 8589934592 | bytes 26214400 | tf_op jit(solution)/shard_map/project/pallas_call | solution.py:160
  181.9 0.0 all-to-all-done.moments_ref
  181.9 0.0 collective-permute-done.14.refs_5_
  181.9 0.0 collective-permute-done.3.refs_0_
  181.9 0.0 collective-permute-done.11.refs_2_
  181.9 2.2 %adam_rows.1 = (bf16[256,512]{1,0:T(8,128)(2,1)}, f32[256,512]{1,0:T(8,128)}, f32[256,512]{1,0:T(8,128)}) custom-call(s32[32]{0:T(128)S(1)} %copy-done.4, bf16[32,16,512]{2,1,0:T(8,128)(2,1)S(1)} %all-to-all-done.moments_ref, bf16[256,512]{1,0:T(8,128)(2,1)S(1)} %get-tuple-element.18.weight_ref, bf16[1,512,256]{2,1,0:T(8,128)(2,1)S(1)} %collective-permute-done.3.refs_0_, ...), custom_call_target="tpu_custom_call" | custom-call | flops 2621440 | bytes 2097152 | tf_op jit(solution)/shard_map/adam_rows/pallas_call | solution.py:222
  (10 shorter events, 0.0 us)
Async XLA Ops:
  7.2 88.2 %all-gather.7.cloned.1.call-start = ((), (), s32[]{:S(2)}) async-start(), calls=%async_computation.2 | async-start | bytes 4325376 | tf_op jit(solution)/shard_map/all_gather | solution.py:335
  8.9 146.8 %all-gather.5.cloned.1.call-start = ((), (), s32[]{:S(2)}) async-start(), calls=%async_computation.1 | async-start | bytes 4325376 | tf_op jit(solution)/shard_map/all_gather | solution.py:335
  16.6 12.5 %collective-permute-start = (bf16[4,512,256]{2,1,0:T(8,128)(2,1)S(1)}, bf16[4,512,256]{2,1,0:T(8,128)(2,1)S(1)}, u32[]{:S(2)}, u32[]{:S(2)}) collective-permute-start(bf16[4,512,256]{2,1,0:T(8,128)(2,1)S(1)} %weight_gradient.8), channel_id=1, source_target_pairs={{0,8},{1,9},{2,10},{3,11},{4,12},{5,13},{6,14},{7,15},{8,0},{9,1},... | collective-permute-start | bytes 3145736 | tf_op jit(solution)/shard_map/ppermute | solution.py:269
  19.9 15.4 %collective-permute-start.4 = (bf16[4,512,256]{2,1,0:T(8,128)(2,1)S(1)}, bf16[4,512,256]{2,1,0:T(8,128)(2,1)S(1)}, u32[]{:S(2)}, u32[]{:S(2)}) collective-permute-start(bf16[4,512,256]{2,1,0:T(8,128)(2,1)S(1)} %weight_gradient.10), channel_id=1, source_target_pairs={{0,8},{1,9},{2,10},{3,11},{4,12},{5,13},{6,14},{7,15},{8,0},{9,1},... | collective-permute-start | bytes 3145736 | tf_op jit(solution)/shard_map/ppermute | solution.py:269
  24.5 25.0 %collective-permute-start.8 = (bf16[4,512,256]{2,1,0:T(8,128)(2,1)}, bf16[4,512,256]{2,1,0:T(8,128)(2,1)}, u32[]{:S(2)}, u32[]{:S(2)}) collective-permute-start(bf16[4,512,256]{2,1,0:T(8,128)(2,1)} %weight_gradient.12), channel_id=1, source_target_pairs={{0,8},{1,9},{2,10},{3,11},{4,12},{5,13},{6,14},{7,15},{8,0},{9,1},... | collective-permute-start | bytes 3145736 | tf_op jit(solution)/shard_map/ppermute | solution.py:269
  28.6 26.0 %collective-permute-start.12 = (bf16[4,512,256]{2,1,0:T(8,128)(2,1)}, bf16[4,512,256]{2,1,0:T(8,128)(2,1)S(1)}, u32[]{:S(2)}, u32[]{:S(2)}) collective-permute-start(bf16[4,512,256]{2,1,0:T(8,128)(2,1)} %weight_gradient.14), channel_id=1, source_target_pairs={{0,8},{1,9},{2,10},{3,11},{4,12},{5,13},{6,14},{7,15},{8,0},{9,1},... | collective-permute-start | bytes 3145736 | tf_op jit(solution)/shard_map/ppermute | solution.py:269
  33.1 0.8 copy-start
  33.9 24.6 %collective-permute-start.1 = (bf16[2,512,256]{2,1,0:T(8,128)(2,1)}, bf16[2,512,256]{2,1,0:T(8,128)(2,1)}, u32[]{:S(2)}, u32[]{:S(2)}) collective-permute-start(bf16[2,512,256]{2,1,0:T(8,128)(2,1)} %get-tuple-element.20), channel_id=1, source_target_pairs={{0,1},{1,0},{2,3},{3,2},{4,5},{5,4},{6,7},{7,6},{8,24},{9,25},{10,... | collective-permute-start | bytes 1572872 | tf_op jit(solution)/shard_map/ppermute | solution.py:269
  39.4 0.8 copy-start.2
  40.2 20.7 %collective-permute-start.5 = (bf16[2,512,256]{2,1,0:T(8,128)(2,1)}, bf16[2,512,256]{2,1,0:T(8,128)(2,1)}, u32[]{:S(2)}, u32[]{:S(2)}) collective-permute-start(bf16[2,512,256]{2,1,0:T(8,128)(2,1)} %get-tuple-element.22), channel_id=1, source_target_pairs={{0,1},{1,0},{2,3},{3,2},{4,5},{5,4},{6,7},{7,6},{8,24},{9,25},{10,... | collective-permute-start | bytes 1572872 | tf_op jit(solution)/shard_map/ppermute | solution.py:269
  42.8 139.0 %all-to-all-start = ((bf16[32,16,512]{2,1,0:T(8,128)(2,1)}), bf16[32,16,512]{2,1,0:T(8,128)(2,1)S(1)}, u32[]{:S(2)}, u32[]{:S(2)}) async-start(bf16[32,16,512]{2,1,0:T(8,128)(2,1)} %pack_moments.1), calls=%async_computation | async-start | bytes 1048576 | tf_op jit(solution)/shard_map/all_to_all | solution.py:347
  53.0 5.5 %copy-start.1 = (bf16[2,512,256]{2,1,0:T(8,128)(2,1)S(1)}, bf16[2,512,256]{2,1,0:T(8,128)(2,1)}, u32[]{:S(2)}) copy-start(bf16[2,512,256]{2,1,0:T(8,128)(2,1)} %copy-done) | copy-start | bytes 1572868
  53.0 8.0 %copy-start.3 = (bf16[2,512,256]{2,1,0:T(8,128)(2,1)S(1)}, bf16[2,512,256]{2,1,0:T(8,128)(2,1)}, u32[]{:S(2)}) copy-start(bf16[2,512,256]{2,1,0:T(8,128)(2,1)} %copy-done.2) | copy-start | bytes 1572868
  53.0 22.1 %collective-permute-start.9 = (bf16[2,512,256]{2,1,0:T(8,128)(2,1)S(1)}, bf16[2,512,256]{2,1,0:T(8,128)(2,1)S(1)}, u32[]{:S(2)}, u32[]{:S(2)}) collective-permute-start(bf16[2,512,256]{2,1,0:T(8,128)(2,1)S(1)} %get-tuple-element.24), channel_id=1, source_target_pairs={{0,1},{1,0},{2,3},{3,2},{4,5},{5,4},{6,7},{7,6},{8,24},{9,25},{10,... | collective-permute-start | bytes 1572872 | tf_op jit(solution)/shard_map/ppermute | solution.py:269
  57.8 97.9 %copy-start.4 = (s32[32]{0:T(128)S(1)}, s32[32]{0:T(128)}, u32[]{:S(2)}) copy-start(s32[32]{0:T(128)} %owner_ref.3) | copy-start | bytes 388
  57.8 27.6 %collective-permute-start.13 = (bf16[2,512,256]{2,1,0:T(8,128)(2,1)S(1)}, bf16[2,512,256]{2,1,0:T(8,128)(2,1)S(1)}, u32[]{:S(2)}, u32[]{:S(2)}) collective-permute-start(bf16[2,512,256]{2,1,0:T(8,128)(2,1)S(1)} %get-tuple-element.26), channel_id=1, source_target_pairs={{0,1},{1,0},{2,3},{3,2},{4,5},{5,4},{6,7},{7,6},{8,24},{9,25},{10,... | collective-permute-start | bytes 1572872 | tf_op jit(solution)/shard_map/ppermute | solution.py:269
  59.4 27.6 %collective-permute-start.2 = (bf16[1,512,256]{2,1,0:T(8,128)(2,1)S(1)}, bf16[1,512,256]{2,1,0:T(8,128)(2,1)S(1)}, u32[]{:S(2)}, u32[]{:S(2)}) collective-permute-start(bf16[1,512,256]{2,1,0:T(8,128)(2,1)S(1)} %add_convert_fusion.6), channel_id=1, source_target_pairs={{0,16},{1,17},{2,18},{3,19},{4,20},{5,21},{6,22},{7,23},{8,9},{9,8... | collective-permute-start | bytes 786440 | tf_op jit(solution)/shard_map/ppermute | solution.py:269
  62.0 28.8 %collective-permute-start.6 = (bf16[1,512,256]{2,1,0:T(8,128)(2,1)S(1)}, bf16[1,512,256]{2,1,0:T(8,128)(2,1)S(1)}, u32[]{:S(2)}, u32[]{:S(2)}) collective-permute-start(bf16[1,512,256]{2,1,0:T(8,128)(2,1)S(1)} %add_convert_fusion.4), channel_id=1, source_target_pairs={{0,16},{1,17},{2,18},{3,19},{4,20},{5,21},{6,22},{7,23},{8,9},{9,8... | collective-permute-start | bytes 786440 | tf_op jit(solution)/shard_map/ppermute | solution.py:269
  75.2 17.4 %collective-permute-start.10 = (bf16[1,512,256]{2,1,0:T(8,128)(2,1)S(1)}, bf16[1,512,256]{2,1,0:T(8,128)(2,1)S(1)}, u32[]{:S(2)}, u32[]{:S(2)}) collective-permute-start(bf16[1,512,256]{2,1,0:T(8,128)(2,1)S(1)} %add_convert_fusion.2), channel_id=1, source_target_pairs={{0,16},{1,17},{2,18},{3,19},{4,20},{5,21},{6,22},{7,23},{8,9},{9,8... | collective-permute-start | bytes 786440 | tf_op jit(solution)/shard_map/ppermute | solution.py:269
  85.5 96.4 %collective-permute-start.14 = (bf16[1,512,256]{2,1,0:T(8,128)(2,1)S(1)}, bf16[1,512,256]{2,1,0:T(8,128)(2,1)S(1)}, u32[]{:S(2)}, u32[]{:S(2)}) collective-permute-start(bf16[1,512,256]{2,1,0:T(8,128)(2,1)S(1)} %add_convert_fusion), channel_id=1, source_target_pairs={{0,16},{1,17},{2,18},{3,19},{4,20},{5,21},{6,22},{7,23},{8,9},{9,8... | collective-permute-start | bytes 786440 | tf_op jit(solution)/shard_map/ppermute | solution.py:269
  88.1 93.8 %collective-permute-start.3 = (bf16[1,512,256]{2,1,0:T(8,128)(2,1)S(1)}, bf16[1,512,256]{2,1,0:T(8,128)(2,1)S(1)}, u32[]{:S(2)}, u32[]{:S(2)}) collective-permute-start(bf16[1,512,256]{2,1,0:T(8,128)(2,1)S(1)} %add_convert_fusion.5), channel_id=1, source_target_pairs={{0,4},{1,5},{2,6},{3,7},{4,0},{5,1},{6,2},{7,3},{8,12},{9,13},{10,... | collective-permute-start | bytes 786440 | tf_op jit(solution)/shard_map/ppermute | solution.py:269
  92.5 89.4 %collective-permute-start.7 = (bf16[1,512,256]{2,1,0:T(8,128)(2,1)}, bf16[1,512,256]{2,1,0:T(8,128)(2,1)S(1)}, u32[]{:S(2)}, u32[]{:S(2)}) collective-permute-start(bf16[1,512,256]{2,1,0:T(8,128)(2,1)} %add_convert_fusion.3), channel_id=1, source_target_pairs={{0,2},{1,3},{2,4},{3,5},{4,6},{5,7},{6,0},{7,1},{8,10},{9,11},{10,... | collective-permute-start | bytes 786440 | tf_op jit(solution)/shard_map/ppermute | solution.py:269
  93.3 88.6 %collective-permute-start.11 = (bf16[1,512,256]{2,1,0:T(8,128)(2,1)}, bf16[1,512,256]{2,1,0:T(8,128)(2,1)S(1)}, u32[]{:S(2)}, u32[]{:S(2)}) collective-permute-start(bf16[1,512,256]{2,1,0:T(8,128)(2,1)} %add_convert_fusion.1), channel_id=1, source_target_pairs={{0,6},{1,7},{2,0},{3,1},{4,2},{5,3},{6,4},{7,5},{8,14},{9,15},{10,... | collective-permute-start | bytes 786440 | tf_op jit(solution)/shard_map/ppermute | solution.py:269
  155.7 2.2 %copy-start.5 = (bf16[4096,512]{1,0:T(8,128)(2,1)S(1)}, bf16[4096,512]{1,0:T(8,128)(2,1)}, u32[]{:S(2)}) copy-start(bf16[4096,512]{1,0:T(8,128)(2,1)} %all-gather.5.cloned.1.call-done) | copy-start | bytes 12582916
Sparse Core Ops, SparseCore 0:
  11.0 72.7 all-gather.6
  86.7 68.8 all-gather.4

commit v4 on v3

--- a/solution.py
+++ b/solution.py
@@ -24,7 +24,12 @@
     return pl.CostEstimate(flops=flops, bytes_accessed=moved, transcendentals=0)
 
 
-def grad_kernel(per_step, adds, order_ref, *refs):
+def block_at(new_ref, groups, position):
+    shards = new_ref.shape[0]
+    return new_ref[lax.rem(position, shards)] * groups + lax.div(position, shards)
+
+
+def grad_kernel(per_step, adds, row_ref, new_ref, *refs):
     token_refs, turned_ref, refs = refs[:per_step], refs[per_step], refs[per_step + 1 :]
     out_refs = refs[adds:]
 
@@ -42,33 +47,42 @@
         pl.when(pl.program_id(0) == step)(functools.partial(write, out_ref))
 
 
-def grad_blocks(tokens, turned, order, first, steps, per_step, row_block, addend=None, cut=False):
+def grad_blocks(tokens, turned, row, new_owner, first, steps, per_step, addend=None, cut=False):
     rows, features = tokens.shape
     width = turned.shape[0]
     blocks = steps * per_step
+    groups = lax.axis_size("rep")
+    row_block = features // (groups * new_owner.shape[0])
     if row_block % 128:
+        chosen = row[first : first + blocks]
+        chosen = jnp.take(new_owner, chosen % new_owner.shape[0]) * groups + (
+            chosen // new_owner.shape[0]
+        )
         whole = jnp.dot(turned, tokens, preferred_element_type=jnp.float32)
         parts = jnp.transpose(whole.reshape(width, features // row_block, row_block), (1, 0, 2))
-        parts = jnp.take(parts, order[first : first + blocks], axis=0)
+        parts = jnp.take(parts, chosen, axis=0)
         if addend is not None:
             parts = parts + addend.astype(jnp.float32)
         parts = parts.astype(jnp.bfloat16)
         return list(jnp.split(parts, steps)) if cut else [parts]
 
     def token_map(slot):
-        return lambda i, order_ref: (0, order_ref[first + i * per_step + slot])
-
-    block = pl.BlockSpec((per_step, width, row_block), lambda i, order_ref: (i, 0, 0))
-    fixed = pl.BlockSpec((per_step, width, row_block), lambda i, order_ref: (0, 0, 0))
+        return lambda i, row_ref, new_ref: (
+            0,
+            block_at(new_ref, groups, row_ref[first + i * per_step + slot]),
+        )
+
+    block = pl.BlockSpec((per_step, width, row_block), lambda i, *_: (i, 0, 0))
+    fixed = pl.BlockSpec((per_step, width, row_block), lambda i, *_: (0, 0, 0))
     added = [] if addend is None else [addend]
     outs = steps if cut else 1
     return pl.pallas_call(
         functools.partial(grad_kernel, per_step, len(added)),
         grid_spec=pltpu.PrefetchScalarGridSpec(
-            num_scalar_prefetch=1,
+            num_scalar_prefetch=2,
             grid=(steps,),
             in_specs=[pl.BlockSpec((rows, row_block), token_map(s)) for s in range(per_step)]
-            + [pl.BlockSpec((width, rows), lambda i, order_ref: (0, 0))]
+            + [pl.BlockSpec((width, rows), lambda i, *_: (0, 0))]
             + [block] * len(added),
             out_specs=[fixed if cut else block] * outs,
         ),
@@ -79,13 +93,12 @@
             2 * blocks * row_block * (rows + width * (1 + len(added))) + 2 * rows * width,
         ),
         name="weight_gradient",
-    )(order, *([tokens] * per_step), turned, *added)
+    )(row, new_owner, *([tokens] * per_step), turned, *added)
 
 
 def pack_kernel(groups, new_ref, first_ref, second_ref, out_ref):
-    shards = new_ref.shape[0]
     for slot in range(out_ref.shape[0]):
-        block = new_ref[slot % shards] * groups + slot // shards
+        block = block_at(new_ref, groups, slot)
         rows = pl.ds(pl.multiple_of(block * SUB, SUB), SUB)
         pair = jnp.concatenate([first_ref[rows, :], second_ref[rows, :]], axis=0)
         out_ref[slot] = pair.astype(out_ref.dtype)
@@ -108,22 +121,18 @@
     )(new_owner, first, second)
 
 
-def project_kernel(counts, owner_ref, order_ref, token_ref, *refs):
-    piece_refs = refs[: len(counts)]
-    out_ref, rows_ref, held, logical, sems = refs[len(counts) :]
+def project_kernel(groups, first, own, row_ref, old_ref, new_ref, token_ref, *refs):
+    piece_refs, (out_ref, rows_ref, held, logical, sems) = refs[:-5], refs[-5:]
     devices, row_block, _ = held.shape
 
     @pl.when(pl.program_id(0) == 0)
     def _():
         copies = []
-        start = 0
-        for piece_ref, count in zip(piece_refs, counts):
-            for slot in range(devices):
-                target = held.at[owner_ref[slot], pl.ds(start, count)]
-                copies.append(
-                    pltpu.make_async_copy(piece_ref.at[slot], target, sems.at[len(copies)])
-                )
-            start += count
+        for piece_ref in piece_refs:
+            for index in range(piece_ref.shape[0]):
+                slot = len(copies)
+                target = held.at[old_ref[row_ref[first + slot]]]
+                copies.append(pltpu.make_async_copy(piece_ref.at[index], target, sems.at[slot]))
         for copy in copies:
             copy.start()
         for copy in copies:
@@ -143,7 +152,8 @@
             return carry
 
         lax.fori_loop(0, devices // 2, place, 0)
-        start = pl.multiple_of(order_ref[0] * row_block, row_block)
+        start = block_at(new_ref, groups, row_ref[own]) * row_block
+        start = pl.multiple_of(start, row_block)
         rows_ref[...] = logical[pl.ds(start, row_block), :]
 
     out_ref[...] = jnp.dot(
@@ -151,16 +161,15 @@
     ).astype(out_ref.dtype)
 
 
-def project(tokens, pieces, owners, order):
+def project(tokens, pieces, row, first, own, old_owner, new_owner):
     rows, features = tokens.shape
-    devices, _, width = pieces[0].shape
-    counts = tuple(piece.shape[1] for piece in pieces)
-    row_block = sum(counts)
+    _, row_block, width = pieces[0].shape
+    devices = old_owner.shape[0]
     tile = rows // 4
     return pl.pallas_call(
-        functools.partial(project_kernel, counts),
+        functools.partial(project_kernel, devices // new_owner.shape[0], first, own),
         grid_spec=pltpu.PrefetchScalarGridSpec(
-            num_scalar_prefetch=2,
+            num_scalar_prefetch=3,
             grid=(rows // tile,),
             in_specs=[pl.BlockSpec((tile, features), lambda i, *_: (i, 0))]
             + [pl.BlockSpec(memory_space=pl.ANY)] * len(pieces),
@@ -171,7 +180,7 @@
             scratch_shapes=[
                 pltpu.VMEM((devices, row_block, width), jnp.bfloat16),
                 pltpu.VMEM((features, width), jnp.bfloat16),
-                pltpu.SemaphoreType.DMA((devices * len(pieces),)),
+                pltpu.SemaphoreType.DMA((devices,)),
             ],
         ),
         out_shape=[
@@ -183,7 +192,7 @@
             2 * rows * width * features, 2 * (rows * features + features * width + rows * width)
         ),
         name="project",
-    )(owners, order, tokens, *pieces)
+    )(row, old_owner, new_owner, tokens, *pieces)
 
 
 def adam(weight_rows, first_rows, second_rows, gradient):
@@ -276,40 +285,75 @@
     return total.astype(terms[0].dtype)
 
 
-def far_first(grid):
-    return sorted(range(grid.far), key=lambda k: -min(k, grid.far - k))
-
-
-def order_table(grid):
-    steps = [
+def chunks(grid):
+    half = grid.far // 2
+    return [sorted({d, (grid.far - d) % grid.far}) for d in range(half + 1)]
+
+
+def tables(grid, devices):
+    sums = [
         dict(core=core, near=near, side=side, far=far)
-        for far in range(grid.far)
+        for chunk in chunks(grid)
         for core in range(grid.cores)
         for near in [*range(1, grid.near), 0]
         for side in range(grid.side)
+        for far in chunk
     ]
-    return np.array([[grid.moved(p, **step) for step in steps] for p in range(len(steps))], np.int32)
+    shards = [
+        dict(core=-core, near=-near, side=-side, far=-far)
+        for chunk in chunks(grid)
+        for core in range(grid.cores)
+        for near in range(grid.near)
+        for side in range(grid.side)
+        for far in chunk
+    ]
+    return np.array(
+        [[grid.moved(p, **step) for step in sums + shards] for p in range(devices)], np.int32
+    )
 
 
 def reduce_rows(grid, blocks_of):
     last = []
-    for far in far_first(grid):
+    start = grid.far
+    for chunk in reversed(chunks(grid)):
+        count = len(chunk)
+        start -= count
         addend = None
         if grid.cores > 1:
-            addend = grid.send(blocks_of(1, far, None, False)[0], core=1)
-        parts = blocks_of(0, far, addend, True)
+            addend = grid.send(blocks_of(1, start, count, None, False)[0], core=1)
+        parts = blocks_of(0, start, count, addend, True)
         kept = [parts[-1]]
         for step, part in enumerate(parts[:-1], 1):
             kept.append(grid.send(part, near=step))
         ends = list(kept)
         for step in range(1, grid.side):
-            cut = slice(step, step + 1)
+            cut = slice(step * count, (step + 1) * count)
             ends.append(grid.send(rounded_sum(*[t[cut] for t in kept]), side=step))
-        if far:
-            last.append(grid.send(rounded_sum(*[t[:1] for t in ends]), far=far))
-        else:
+        if chunk == [0]:
             last.extend(ends)
+            continue
+        for index, far in enumerate(chunk):
+            cut = slice(index, index + 1)
+            last.append(grid.send(rounded_sum(*[t[cut] for t in ends]), far=far))
     return last
+
+
+def gather_shards(grid, own):
+    arrived = {far: grid.send(own, far=far) for far in range(1, grid.far)}
+    arrived[0] = own
+    pieces = []
+    for chunk in chunks(grid):
+        base = joined([arrived[far] for far in chunk])
+        plane = joined([base] + [grid.send(base, side=step) for step in range(1, grid.side)])
+        both = [plane] + [grid.send(plane, near=step) for step in range(1, grid.near)]
+        pieces += both
+        for core in range(1, grid.cores):
+            pieces += [grid.send(part, core=core) for part in both]
+    return pieces
+
+
+def joined(arrays):
+    return arrays[0] if len(arrays) == 1 else jnp.concatenate(arrays, axis=0)
 
 
 def body(tokens, cotangent, old_weight, old_first, old_second, old_owner, new_owner):
@@ -323,21 +367,14 @@
     me = lax.axis_index(AXES)
     by_tile = row_block == devices * SUB and width % 128 == 0 and devices % 2 == 0
 
-    table = lax.dynamic_index_in_dim(jnp.asarray(order_table(grid)), me, 0, keepdims=False)
-    chosen = (table % shards)[:, None] == jnp.arange(shards, dtype=jnp.int32)
-    order = jnp.sum(jnp.where(chosen, new_owner, 0), axis=1) * groups + table // shards
+    row = lax.dynamic_index_in_dim(jnp.asarray(tables(grid, devices)), me, 0, keepdims=False)
+    per_far = grid.near * grid.side
     own = (grid.near - 1) * grid.side
-    per_core = grid.near * grid.side
-
+
+    pieces = gather_shards(grid, old_weight[None])
     if by_tile:
-        half = row_block // 2
-        held = [
-            lax.all_gather(old_weight[start : start + half], AXES, axis=0, tiled=False)
-            for start in (0, half)
-        ]
         packed = pack_moments(old_first, old_second, new_owner, groups)
     else:
-        held = lax.all_gather(old_weight, AXES, axis=0, tiled=False)
         slot_ids = jnp.arange(devices, dtype=jnp.int32)
         placing = jnp.take(new_owner, slot_ids % shards) * groups + slot_ids // shards
         both = jnp.stack([old_first, old_second]).astype(jnp.bfloat16)
@@ -348,22 +385,26 @@
 
     turned = cotangent.T
 
-    def blocks_of(core, far, addend, cut):
-        first = (far * grid.cores + core) * per_core
+    def blocks_of(core, start, count, addend, cut):
+        first = (start * grid.cores + core * count) * per_far
+        per_step = grid.side * count
         return grad_blocks(
-            tokens, turned, order, first, grid.near, grid.side, row_block, addend, cut
+            tokens, turned, row, new_owner, first, grid.near, per_step, addend, cut
         )
 
     parts = reduce_rows(grid, blocks_of)
     if by_tile:
-        projected, weight_rows = project(tokens, held, old_owner, order[own : own + 1])
+        projected, weight_rows = project(tokens, pieces, row, devices, own, old_owner, new_owner)
         return (projected, *adam_rows(parts, arrived, weight_rows, old_owner))
     inverse = jnp.zeros((devices,), jnp.int32).at[old_owner].set(slot_ids)
-    logical = jnp.transpose(
-        jnp.take(held.reshape(devices, devices, strip), inverse, axis=0), (1, 0, 2)
-    ).reshape(features, width)
+    held = jnp.zeros((devices, devices, strip), jnp.bfloat16)
+    held = held.at[jnp.take(old_owner, row[devices:])].set(
+        joined(pieces).reshape(devices, devices, strip)
+    )
+    logical = jnp.transpose(held, (1, 0, 2)).reshape(features, width)
     projected = jnp.dot(tokens, logical, preferred_element_type=jnp.float32).astype(jnp.bfloat16)
-    weight_rows = lax.dynamic_slice_in_dim(logical, order[own] * row_block, row_block, 0)
+    own_block = jnp.take(placing, me)
+    weight_rows = lax.dynamic_slice_in_dim(logical, own_block * row_block, row_block, 0)
     moved = jnp.transpose(jnp.take(arrived, inverse, axis=0), (1, 0, 2))
     first_rows, second_rows = moved.astype(jnp.float32).reshape(2, row_block, width)
     gradient = sum(part[0].astype(jnp.float32) for part in parts).T

time: 193 us -> 133 us (0.69)
  waiting for transfers between devices: 82.3 us -> 48.3 us
  between operations: 14.2 us -> 0.95 us
  Pallas kernels: 57.6 us -> 45.2 us
  starting transfers between devices: 21.3 us -> 26.7 us
  local copies, waits for them, and re-layouts: 7.62 us -> 5.33 us
    all_gather x2 -> x0, waiting for transfers between devices: 60.3 us -> none  [body(): lax.all_gather(old_weight[start:start + half], AXES, axis=0, tiled=False)]
    ppermute x15 -> x27, waiting for transfers between devices: 21.3 us -> 48.3 us  [send(): return lax.ppermute(value, AXES, pairs)]
    pallas_call x1, Pallas kernels: 24 us -> 16.9 us  [project(): pl.pallas_call(functools.partial(project_kernel, devices // new_owner.sha...]
    ppermute x15 -> x27, starting transfers between devices: 15.2 us -> 22 us  [send(): return lax.ppermute(value, AXES, pairs)]
    pallas_call x8 -> x6, Pallas kernels: 29.3 us -> 24 us  [grad_blocks(): pl.pallas_call(functools.partial(grad_kernel, per_step, len(added)), grid...]
    slice x2 -> x0, local copies, waits for them, and re-layouts: 2.32 us -> none  [the longest x1 1.68 us: body(): old_weight[start:start + half]]
    unnamed x13 -> x34, local copies, waits for them, and re-layouts: 5.3 us -> 3.78 us
    convert_element_type x7 -> x5, other arithmetic: 5.78 us -> 5.99 us  [rounded_sum(): return total.astype(terms[0].dtype)]
  transfers between devices with their start and end apart: 18 -> 28, of which waited for: 3 -> 10; matrix products, arithmetic and copies ran while one was open for 5% -> 6% of each run, Pallas kernels for 29% -> 29%
where the time goes in v4:
time: 133 us
  waiting for transfers between devices  48.3 us (36%)
  Pallas kernels  45.2 us (34%)
  starting transfers between devices  26.7 us (20%)
  other arithmetic  6.09 us (5%)
  local copies, waits for them, and re-layouts  5.33 us (4%)
    ppermute x27, waiting for transfers between devices, send(): return lax.ppermute(value, AXES, pairs)  48.3 us
    pallas_call x6, Pallas kernels, grad_blocks(): pl.pallas_call(functools.partial(grad_kernel, per_step, len(added)), grid...  24 us
    ppermute x27, starting transfers between devices, send(): return lax.ppermute(value, AXES, pairs)  22 us
    pallas_call x1, Pallas kernels, project(): pl.pallas_call(functools.partial(project_kernel, devices // new_owner.sha...  16.9 us
    convert_element_type x5, other arithmetic, rounded_sum(): return total.astype(terms[0].dtype)  5.99 us
    all_to_all x1, starting transfers between devices, body(): lax.all_to_all(packed, AXES, split_axis=0, concat_axis=0, tiled=True)  4.73 us
    unnamed x34, local copies, waits for them, and re-layouts  3.78 us
  transfers between devices with their start and end apart: 28, of which 10 were waited for; matrix products, arithmetic and copies ran while one was open for 6% of the time, Pallas kernels for 29%

profile of v4, /device:TPU:8, one launch (start us, length us, event | category | flops | bytes accessed | tf_op | source)
XLA Modules:
  0.0 132.6 jit_solution(4379816228000597355)
XLA Ops:
  0.6 0.0 copy-start.3
  0.6 1.5 %copy.12 = bf16[1024,512]{0,1:T(8,128)(2,1)S(1)} copy(bf16[1024,512]{1,0:T(8,128)(2,1)} %param.9) | data formatting | bytes 2097152 | tf_op args[1]
  2.1 0.7 dynamic-slice_bitcast_fusion.row_ref
  2.8 4.9 %weight_gradient.8 = bf16[8,512,256]{2,1,0:T(8,128)(2,1)S(1)} custom-call(s32[64]{0:T(128)S(1)} %dynamic-slice_bitcast_fusion.row_ref, s32[8]{0:T(128)S(1)} %copy-done.3, bf16[1024,8192]{1,0:T(8,128)(2,1)} %refs_1_.11, bf16[1024,8192]{1,0:T(8,128)(2,1)} %refs_1_.11, bf16[1024,8192]{1,0:T(8,128)(2,1)} %refs_1_.11, bf16[1024,8192]{1,0:T(8,128)(2,1)} %refs_1_.11, ...), custom_call_target="tpu_custom_call" | custom-call | flops 2147483648 | bytes 7340032 | tf_op jit(solution)/shard_map/weight_gradient/pallas_call | solution.py:79
  7.7 0.1 collective-permute-start.19
  7.8 1.6 %collective-permute-start.4 = (bf16[1,256,512]{2,1,0:T(8,128)(2,1)S(1)}, bf16[1,256,512]{2,1,0:T(8,128)(2,1)S(1)}, u32[]{:S(2)}, u32[]{:S(2)}) collective-permute-start(bf16[1,256,512]{2,1,0:T(8,128)(2,1)S(1)} %bitcast.10), channel_id=1, source_target_pairs={{0,2},{1,3},{2,4},{3,5},{4,6},{5,7},{6,0},{7,1},{8,10},{9,11},{10,... | collective-permute-start | bytes 786440 | tf_op jit(solution)/shard_map/ppermute | solution.py:278
  9.5 0.4 collective-permute-start.5
  9.9 3.3 %weight_gradient.6 = bf16[4,512,256]{2,1,0:T(8,128)(2,1)S(1)} custom-call(s32[64]{0:T(128)S(1)} %dynamic-slice_bitcast_fusion.row_ref, s32[8]{0:T(128)S(1)} %copy-done.3, bf16[1024,8192]{1,0:T(8,128)(2,1)} %refs_1_.11, bf16[1024,8192]{1,0:T(8,128)(2,1)} %refs_1_.11, bf16[512,1024]{1,0:T(8,128)(2,1)S(1)} %bitcast.5), custom_call_target="tpu_custom_call" | custom-call | flops 1073741824 | bytes 4194304 | tf_op jit(solution)/shard_map/weight_gradient/pallas_call | solution.py:79
  13.3 0.1 collective-permute-start.15
  13.3 3.7 %collective-permute-done.4 = bf16[1,256,512]{2,1,0:T(8,128)(2,1)S(1)} collective-permute-done((bf16[1,256,512]{2,1,0:T(8,128)(2,1)S(1)}, bf16[1,256,512]{2,1,0:T(8,128)(2,1)S(1)}, u32[]{:S(2)}, u32[]{:S(2)}) %collective-permute-start.4) | collective-permute-done | bytes 262176 | tf_op jit(solution)/shard_map/ppermute | solution.py:278
  17.0 6.0 %collective-permute-done.5 = bf16[1,256,512]{2,1,0:T(8,128)(2,1)S(1)} collective-permute-done((bf16[1,256,512]{2,1,0:T(8,128)(2,1)S(1)}, bf16[1,256,512]{2,1,0:T(8,128)(2,1)S(1)}, u32[]{:S(2)}, u32[]{:S(2)}) %collective-permute-start.5) | collective-permute-done | bytes 262176 | tf_op jit(solution)/shard_map/ppermute | solution.py:278
  23.0 0.1 pad_maximum_fusion.1
  23.0 1.6 %collective-permute-start.6 = (bf16[2,256,512]{2,1,0:T(8,128)(2,1)S(1)}, bf16[2,256,512]{2,1,0:T(8,128)(2,1)S(1)}, u32[]{:S(2)}, u32[]{:S(2)}) collective-permute-start(bf16[2,256,512]{2,1,0:T(8,128)(2,1)S(1)} %pad_maximum_fusion.1), channel_id=1, source_target_pairs={{0,16},{1,17},{2,18},{3,19},{4,20},{5,21},{6,22},{7,23},{8,9},{9,8... | collective-permute-start | bytes 1572872 | tf_op jit(solution)/shard_map/ppermute | solution.py:278
  24.6 3.3 %weight_gradient.10 = bf16[4,512,256]{2,1,0:T(8,128)(2,1)S(1)} custom-call(s32[64]{0:T(128)S(1)} %dynamic-slice_bitcast_fusion.row_ref, s32[8]{0:T(128)S(1)} %copy-done.3, bf16[1024,8192]{1,0:T(8,128)(2,1)} %refs_1_.11, bf16[1024,8192]{1,0:T(8,128)(2,1)} %refs_1_.11, bf16[512,1024]{1,0:T(8,128)(2,1)S(1)} %bitcast.6), custom_call_target="tpu_custom_call" | custom-call | flops 1073741824 | bytes 4194304 | tf_op jit(solution)/shard_map/weight_gradient/pallas_call | solution.py:79
  28.0 0.1 collective-permute-start.24
  28.1 1.2 collective-permute-start
  29.3 0.0 collective-permute-done.19.refs_5_
  29.3 4.9 %weight_gradient.9 = (bf16[4,512,256]{2,1,0:T(8,128)(2,1)S(1)}, bf16[4,512,256]{2,1,0:T(8,128)(2,1)S(1)}) custom-call(s32[64]{0:T(128)S(1)} %dynamic-slice_bitcast_fusion.row_ref, s32[8]{0:T(128)S(1)} %copy-done.3, bf16[1024,8192]{1,0:T(8,128)(2,1)} %refs_1_.11, bf16[1024,8192]{1,0:T(8,128)(2,1)} %refs_1_.11, bf16[1024,8192]{1,0:T(8,128)(2,1)} %refs_1_.11, ...), custom_call_target="tpu_custom_call" | custom-call | flops 2147483648 | bytes 9437184 | tf_op jit(solution)/shard_map/weight_gradient/pallas_call | solution.py:79
  34.2 0.9 collective-permute-start.20
  35.1 0.7 constant_dynamic-update-slice_fusion.2
  35.8 0.0 collective-permute-done.6
  35.8 1.7 %collective-permute-start.10 = (bf16[1,256,512]{2,1,0:T(8,128)(2,1)S(1)}, bf16[1,256,512]{2,1,0:T(8,128)(2,1)S(1)}, u32[]{:S(2)}, u32[]{:S(2)}) collective-permute-start(bf16[1,256,512]{2,1,0:T(8,128)(2,1)S(1)} %bitcast.13), channel_id=1, source_target_pairs={{0,4},{1,5},{2,6},{3,7},{4,0},{5,1},{6,2},{7,3},{8,12},{9,13},{10,... | collective-permute-start | bytes 786440 | tf_op jit(solution)/shard_map/ppermute | solution.py:278
  37.6 0.7 constant_dynamic-update-slice_fusion.1
  38.3 0.8 constant_dynamic-update-slice_fusion.refs_4_
  39.1 0.6 collective-permute-start.7
  39.7 8.9 %collective-permute-done.10 = bf16[1,256,512]{2,1,0:T(8,128)(2,1)S(1)} collective-permute-done((bf16[1,256,512]{2,1,0:T(8,128)(2,1)S(1)}, bf16[1,256,512]{2,1,0:T(8,128)(2,1)S(1)}, u32[]{:S(2)}, u32[]{:S(2)}) %collective-permute-start.10) | collective-permute-done | bytes 262176 | tf_op jit(solution)/shard_map/ppermute | solution.py:278
  48.7 1.6 %collective-permute-start.11 = (bf16[1,256,512]{2,1,0:T(8,128)(2,1)S(1)}, bf16[1,256,512]{2,1,0:T(8,128)(2,1)S(1)}, u32[]{:S(2)}, u32[]{:S(2)}) collective-permute-start(bf16[1,256,512]{2,1,0:T(8,128)(2,1)S(1)} %collective-permute-done.10), channel_id=1, source_target_pairs={{0,16},{1,17},{2,18},{3,19},{4,20},{5,21},{6,22},{7,23},{8,9},{9,8... | collective-permute-start | bytes 786440 | tf_op jit(solution)/shard_map/ppermute | solution.py:278
  50.3 0.1 pad_maximum_fusion.refs_0_
  50.3 0.6 collective-permute-start.1
  50.9 3.3 %weight_gradient.7 = (bf16[2,512,256]{2,1,0:T(8,128)(2,1)S(1)}, bf16[2,512,256]{2,1,0:T(8,128)(2,1)S(1)}) custom-call(s32[64]{0:T(128)S(1)} %dynamic-slice_bitcast_fusion.row_ref, s32[8]{0:T(128)S(1)} %copy-done.3, bf16[1024,8192]{1,0:T(8,128)(2,1)} %refs_1_.11, bf16[1024,8192]{1,0:T(8,128)(2,1)} %refs_1_.11, bf16[512,1024]{1,0:T(8,128)(2,1)S(1)} %bitcast.8, ...), custom_call_target="tpu_custom_call" | custom-call | flops 1073741824 | bytes 5242880 | tf_op jit(solution)/shard_map/weight_gradient/pallas_call | solution.py:79
  54.3 3.6 %collective-permute-done.11 = bf16[1,256,512]{2,1,0:T(8,128)(2,1)S(1)} collective-permute-done((bf16[1,256,512]{2,1,0:T(8,128)(2,1)S(1)}, bf16[1,256,512]{2,1,0:T(8,128)(2,1)S(1)}, u32[]{:S(2)}, u32[]{:S(2)}) %collective-permute-start.11) | collective-permute-done | bytes 262176 | tf_op jit(solution)/shard_map/ppermute | solution.py:278
  57.9 0.5 collective-permute-start.16
  58.5 4.1 %weight_gradient.11 = (bf16[2,512,256]{2,1,0:T(8,128)(2,1)}, bf16[2,512,256]{2,1,0:T(8,128)(2,1)S(1)}) custom-call(s32[64]{0:T(128)S(1)} %dynamic-slice_bitcast_fusion.row_ref, s32[8]{0:T(128)S(1)} %copy-done.3, bf16[1024,8192]{1,0:T(8,128)(2,1)} %refs_1_.11, bf16[1024,8192]{1,0:T(8,128)(2,1)} %refs_1_.11, bf16[512,1024]{1,0:T(8,128)(2,1)S(1)} %bitcast.9, ...), custom_call_target="tpu_custom_call" | custom-call | flops 1073741824 | bytes 5242880 | tf_op jit(solution)/shard_map/weight_gradient/pallas_call | solution.py:79
  62.7 6.1 %collective-permute-done.1.refs_1_ = bf16[2,256,512]{2,1,0:T(8,128)(2,1)S(1)} collective-permute-done((bf16[2,256,512]{2,1,0:T(8,128)(2,1)S(1)}, bf16[2,256,512]{2,1,0:T(8,128)(2,1)S(1)}, u32[]{:S(2)}, u32[]{:S(2)}) %collective-permute-start.1) | collective-permute-done | bytes 524320 | tf_op jit(solution)/shard_map/ppermute | solution.py:278
  68.7 0.8 collective-permute-start.12
  69.6 1.2 collective-permute-start.25
  70.8 1.0 add_convert_fusion
  71.8 0.9 collective-permute-start.21
  72.6 2.4 %collective-permute-done.16 = bf16[2,512,256]{2,1,0:T(8,128)(2,1)S(1)} collective-permute-done((bf16[2,512,256]{2,1,0:T(8,128)(2,1)S(1)}, bf16[2,512,256]{2,1,0:T(8,128)(2,1)S(1)}, u32[]{:S(2)}, u32[]{:S(2)}) %collective-permute-start.16) | collective-permute-done | bytes 524320 | tf_op jit(solution)/shard_map/ppermute | solution.py:278
  75.0 0.5 collective-permute-start.9
  75.5 0.1 add_convert_fusion.5
  75.6 10.0 %collective-permute-done.12.refs_9_ = bf16[2,256,512]{2,1,0:T(8,128)(2,1)S(1)} collective-permute-done((bf16[2,256,512]{2,1,0:T(8,128)(2,1)S(1)}, bf16[2,256,512]{2,1,0:T(8,128)(2,1)S(1)}, u32[]{:S(2)}, u32[]{:S(2)}) %collective-permute-start.12) | collective-permute-done | bytes 524320 | tf_op jit(solution)/shard_map/ppermute | solution.py:278
  85.6 0.8 copy-done.10
  86.4 0.9 collective-permute-start.17
  87.3 2.1 %pack_moments.1 = bf16[32,16,512]{2,1,0:T(8,128)(2,1)} custom-call(s32[8]{0:T(128)} %new_ref.15, f32[256,512]{1,0:T(8,128)} %first_ref.1, f32[256,512]{1,0:T(8,128)} %second_ref.1), custom_call_target="tpu_custom_call" | custom-call | bytes 1572864 | tf_op jit(solution)/shard_map/pack_moments/pallas_call | solution.py:110
  89.4 4.7 %all-to-all-start = ((bf16[32,16,512]{2,1,0:T(8,128)(2,1)}), bf16[32,16,512]{2,1,0:T(8,128)(2,1)S(1)}, u32[]{:S(2)}, u32[]{:S(2)}) async-start(bf16[32,16,512]{2,1,0:T(8,128)(2,1)} %pack_moments.1), calls=%async_computation | async-start | bytes 1048576 | tf_op jit(solution)/shard_map/all_to_all | solution.py:384
  94.1 0.0 copy-start.4
  94.1 0.0 copy-start.5
  94.1 0.0 copy-start.7
  94.1 0.0 copy-start.9
  94.2 0.2 collective-permute-start.13
  94.4 0.4 collective-permute-start.3
  94.8 0.1 collective-permute-start.14
  94.9 0.8 add_convert_fusion.1
  95.7 1.9 %add_convert_fusion.4 = bf16[1,512,256]{2,1,0:T(8,128)(2,1)} fusion(bf16[1,512,256]{2,1,0:T(8,128)(2,1)} %collective-permute-done.17, bf16[2,512,256]{2,1,0:T(8,128)(2,1)} %copy-done.13, bf16[2,512,256]{2,1,0:T(8,128)(2,1)} %copy-done), kind=kLoop, calls=%fused_computation.6 | loop fusion | flops 786432 | bytes 1048576 | tf_op jit(solution)/shard_map/convert_element_type | solution.py:285
  97.6 2.2 %add_convert_fusion.2 = (bf16[1,512,256]{2,1,0:T(8,128)(2,1)}, bf16[1,512,256]{2,1,0:T(8,128)(2,1)}) fusion(bf16[2,512,256]{2,1,0:T(8,128)(2,1)} %collective-permute-done.21, bf16[4,512,256]{2,1,0:T(8,128)(2,1)} %copy-done.12, bf16[4,512,256]{2,1,0:T(8,128)(2,1)S(1)} %get-tuple-element.19), kind=kLoop, calls=%fused_computation.4 | loop fusion | flops 1572864 | bytes 2097152 | tf_op jit(solution)/shard_map/convert_element_type | solution.py:285
  99.8 1.5 %collective-permute-start.26 = (bf16[1,512,256]{2,1,0:T(8,128)(2,1)}, bf16[1,512,256]{2,1,0:T(8,128)(2,1)S(1)}, u32[]{:S(2)}, u32[]{:S(2)}) collective-permute-start(bf16[1,512,256]{2,1,0:T(8,128)(2,1)} %add_convert_fusion.1), channel_id=1, source_target_pairs={{0,16},{1,17},{2,18},{3,19},{4,20},{5,21},{6,22},{7,23},{8,9},{9,8... | collective-permute-start | bytes 786440 | tf_op jit(solution)/shard_map/ppermute | solution.py:278
  101.3 2.4 %collective-permute-start.18 = (bf16[1,512,256]{2,1,0:T(8,128)(2,1)}, bf16[1,512,256]{2,1,0:T(8,128)(2,1)S(1)}, u32[]{:S(2)}, u32[]{:S(2)}) collective-permute-start(bf16[1,512,256]{2,1,0:T(8,128)(2,1)} %add_convert_fusion.4), channel_id=1, source_target_pairs={{0,4},{1,5},{2,6},{3,7},{4,0},{5,1},{6,2},{7,3},{8,12},{9,13},{10,... | collective-permute-start | bytes 786440 | tf_op jit(solution)/shard_map/ppermute | solution.py:278
  103.8 2.0 %collective-permute-start.23 = (bf16[1,512,256]{2,1,0:T(8,128)(2,1)}, bf16[1,512,256]{2,1,0:T(8,128)(2,1)S(1)}, u32[]{:S(2)}, u32[]{:S(2)}) collective-permute-start(bf16[1,512,256]{2,1,0:T(8,128)(2,1)} %get-tuple-element.26), channel_id=1, source_target_pairs={{0,6},{1,7},{2,0},{3,1},{4,2},{5,3},{6,4},{7,5},{8,14},{9,15},{10,... | collective-permute-start | bytes 786440 | tf_op jit(solution)/shard_map/ppermute | solution.py:278
  105.8 16.9 %project.1 = (bf16[1024,512]{1,0:T(8,128)(2,1)}, bf16[256,512]{1,0:T(8,128)(2,1)S(1)}) custom-call(s32[64]{0:T(128)S(1)} %dynamic-slice_bitcast_fusion.row_ref, s32[32]{0:T(128)S(1)} %copy-done.5, s32[8]{0:T(128)S(1)} %copy-done.4, bf16[1024,8192]{1,0:T(8,128)(2,1)} %refs_1_.11, bf16[2,256,512]{2,1,0:T(8,128)(2,1)S(1)} %pad_maximum_fusion.refs_0_, ...), custom_call_target="tpu_custom_call" | custom-call | flops 8589934592 | bytes 26214400 | tf_op jit(solution)/shard_map/project/pallas_call | solution.py:169
  122.8 0.2 collective-permute-done.18.refs_0_
  123.0 5.4 %collective-permute-done.22.refs_1_ = bf16[1,512,256]{2,1,0:T(8,128)(2,1)S(1)} collective-permute-done((bf16[1,512,256]{2,1,0:T(8,128)(2,1)}, bf16[1,512,256]{2,1,0:T(8,128)(2,1)S(1)}, u32[]{:S(2)}, u32[]{:S(2)}) %collective-permute-start.22) | collective-permute-done | bytes 262176 | tf_op jit(solution)/shard_map/ppermute | solution.py:278
  128.4 2.0 %collective-permute-done.23.refs_2_ = bf16[1,512,256]{2,1,0:T(8,128)(2,1)S(1)} collective-permute-done((bf16[1,512,256]{2,1,0:T(8,128)(2,1)}, bf16[1,512,256]{2,1,0:T(8,128)(2,1)S(1)}, u32[]{:S(2)}, u32[]{:S(2)}) %collective-permute-start.23) | collective-permute-done | bytes 262176 | tf_op jit(solution)/shard_map/ppermute | solution.py:278
  130.4 2.2 %adam_rows.1 = (bf16[256,512]{1,0:T(8,128)(2,1)}, f32[256,512]{1,0:T(8,128)}, f32[256,512]{1,0:T(8,128)}) custom-call(s32[32]{0:T(128)S(1)} %copy-done.5, bf16[32,16,512]{2,1,0:T(8,128)(2,1)S(1)} %all-to-all-done.moments_ref, bf16[256,512]{1,0:T(8,128)(2,1)S(1)} %get-tuple-element.16.weight_ref, bf16[1,512,256]{2,1,0:T(8,128)(2,1)S(1)} %collective-permute-done.18.refs_0_, ...), custom_call_target="tpu_custom_call" | custom-call | flops 2621440 | bytes 2097152 | tf_op jit(solution)/shard_map/adam_rows/pallas_call | solution.py:231
  (45 shorter events, 0.1 us)
Async XLA Ops:
  0.6 2.2 %copy-start.3 = (s32[8]{0:T(128)S(1)}, s32[8]{0:T(128)}, u32[]{:S(2)}) copy-start(s32[8]{0:T(128)} %new_ref.15) | copy-start | bytes 100
  2.8 5.0 %copy-start.14 = (bf16[256,512]{1,0:T(8,128)(2,1)S(1)}, bf16[256,512]{1,0:T(8,128)(2,1)}, u32[]{:S(2)}) copy-start(bf16[256,512]{1,0:T(8,128)(2,1)} %param.10) | copy-start | bytes 786436
  7.7 21.6 %collective-permute-start.19 = (bf16[8,512,256]{2,1,0:T(8,128)(2,1)S(1)}, bf16[8,512,256]{2,1,0:T(8,128)(2,1)S(1)}, u32[]{:S(2)}, u32[]{:S(2)}) collective-permute-start(bf16[8,512,256]{2,1,0:T(8,128)(2,1)S(1)} %weight_gradient.8), channel_id=1, source_target_pairs={{0,8},{1,9},{2,10},{3,11},{4,12},{5,13},{6,14},{7,15},{8,0},{9,1},... | collective-permute-start | bytes 6291464 | tf_op jit(solution)/shard_map/ppermute | solution.py:278
  7.8 9.2 %collective-permute-start.4 = (bf16[1,256,512]{2,1,0:T(8,128)(2,1)S(1)}, bf16[1,256,512]{2,1,0:T(8,128)(2,1)S(1)}, u32[]{:S(2)}, u32[]{:S(2)}) collective-permute-start(bf16[1,256,512]{2,1,0:T(8,128)(2,1)S(1)} %bitcast.10), channel_id=1, source_target_pairs={{0,2},{1,3},{2,4},{3,5},{4,6},{5,7},{6,0},{7,1},{8,10},{9,11},{10,... | collective-permute-start | bytes 786440 | tf_op jit(solution)/shard_map/ppermute | solution.py:278
  9.5 13.5 %collective-permute-start.5 = (bf16[1,256,512]{2,1,0:T(8,128)(2,1)S(1)}, bf16[1,256,512]{2,1,0:T(8,128)(2,1)S(1)}, u32[]{:S(2)}, u32[]{:S(2)}) collective-permute-start(bf16[1,256,512]{2,1,0:T(8,128)(2,1)S(1)} %bitcast.11), channel_id=1, source_target_pairs={{0,6},{1,7},{2,0},{3,1},{4,2},{5,3},{6,4},{7,5},{8,14},{9,15},{10,... | collective-permute-start | bytes 786440 | tf_op jit(solution)/shard_map/ppermute | solution.py:278
  13.3 37.1 %collective-permute-start.15 = (bf16[4,512,256]{2,1,0:T(8,128)(2,1)S(1)}, bf16[4,512,256]{2,1,0:T(8,128)(2,1)S(1)}, u32[]{:S(2)}, u32[]{:S(2)}) collective-permute-start(bf16[4,512,256]{2,1,0:T(8,128)(2,1)S(1)} %weight_gradient.6), channel_id=1, source_target_pairs={{0,8},{1,9},{2,10},{3,11},{4,12},{5,13},{6,14},{7,15},{8,0},{9,1},... | collective-permute-start | bytes 3145736 | tf_op jit(solution)/shard_map/ppermute | solution.py:278
  23.0 12.8 %collective-permute-start.6 = (bf16[2,256,512]{2,1,0:T(8,128)(2,1)S(1)}, bf16[2,256,512]{2,1,0:T(8,128)(2,1)S(1)}, u32[]{:S(2)}, u32[]{:S(2)}) collective-permute-start(bf16[2,256,512]{2,1,0:T(8,128)(2,1)S(1)} %pad_maximum_fusion.1), channel_id=1, source_target_pairs={{0,16},{1,17},{2,18},{3,19},{4,20},{5,21},{6,22},{7,23},{8,9},{9,8... | collective-permute-start | bytes 1572872 | tf_op jit(solution)/shard_map/ppermute | solution.py:278
  28.0 30.0 %collective-permute-start.24 = (bf16[4,512,256]{2,1,0:T(8,128)(2,1)S(1)}, bf16[4,512,256]{2,1,0:T(8,128)(2,1)S(1)}, u32[]{:S(2)}, u32[]{:S(2)}) collective-permute-start(bf16[4,512,256]{2,1,0:T(8,128)(2,1)S(1)} %weight_gradient.10), channel_id=1, source_target_pairs={{0,8},{1,9},{2,10},{3,11},{4,12},{5,13},{6,14},{7,15},{8,0},{9,1},... | collective-permute-start | bytes 3145736 | tf_op jit(solution)/shard_map/ppermute | solution.py:278
  28.1 11.1 %collective-permute-start = (bf16[1,256,512]{2,1,0:T(8,128)(2,1)S(1)}, bf16[1,256,512]{2,1,0:T(8,128)(2,1)S(1)}, u32[]{:S(2)}, u32[]{:S(2)}) collective-permute-start(bf16[1,256,512]{2,1,0:T(8,128)(2,1)S(1)} %bitcast.12), channel_id=1, source_target_pairs={{0,16},{1,17},{2,18},{3,19},{4,20},{5,21},{6,22},{7,23},{8,9},{9,8... | collective-permute-start | bytes 786440 | tf_op jit(solution)/shard_map/ppermute | solution.py:278
  34.2 35.4 %collective-permute-start.20 = (bf16[4,512,256]{2,1,0:T(8,128)(2,1)S(1)}, bf16[4,512,256]{2,1,0:T(8,128)(2,1)S(1)}, u32[]{:S(2)}, u32[]{:S(2)}) collective-permute-start(bf16[4,512,256]{2,1,0:T(8,128)(2,1)S(1)} %get-tuple-element.20), channel_id=1, source_target_pairs={{0,1},{1,0},{2,3},{3,2},{4,5},{5,4},{6,7},{7,6},{8,24},{9,25},{10,... | collective-permute-start | bytes 3145736 | tf_op jit(solution)/shard_map/ppermute | solution.py:278
  35.8 12.9 %collective-permute-start.10 = (bf16[1,256,512]{2,1,0:T(8,128)(2,1)S(1)}, bf16[1,256,512]{2,1,0:T(8,128)(2,1)S(1)}, u32[]{:S(2)}, u32[]{:S(2)}) collective-permute-start(bf16[1,256,512]{2,1,0:T(8,128)(2,1)S(1)} %bitcast.13), channel_id=1, source_target_pairs={{0,4},{1,5},{2,6},{3,7},{4,0},{5,1},{6,2},{7,3},{8,12},{9,13},{10,... | collective-permute-start | bytes 786440 | tf_op jit(solution)/shard_map/ppermute | solution.py:278
  39.1 35.9 %collective-permute-start.7 = (bf16[4,256,512]{2,1,0:T(8,128)(2,1)}, bf16[4,256,512]{2,1,0:T(8,128)(2,1)}, u32[]{:S(2)}, u32[]{:S(2)}) collective-permute-start(bf16[4,256,512]{2,1,0:T(8,128)(2,1)} %constant_dynamic-update-slice_fusion.refs_4_), channel_id=1, source_target_pairs={{0,1},{1,0},{2,3},{3,2},{4,5},{5,4},{6,7},{7,6},{8,24},{9,25},{10,... | collective-permute-start | bytes 3145736 | tf_op jit(solution)/shard_map/ppermute | solution.py:278
  48.7 9.2 %collective-permute-start.11 = (bf16[1,256,512]{2,1,0:T(8,128)(2,1)S(1)}, bf16[1,256,512]{2,1,0:T(8,128)(2,1)S(1)}, u32[]{:S(2)}, u32[]{:S(2)}) collective-permute-start(bf16[1,256,512]{2,1,0:T(8,128)(2,1)S(1)} %collective-permute-done.10), channel_id=1, source_target_pairs={{0,16},{1,17},{2,18},{3,19},{4,20},{5,21},{6,22},{7,23},{8,9},{9,8... | collective-permute-start | bytes 786440 | tf_op jit(solution)/shard_map/ppermute | solution.py:278
  50.3 18.4 %collective-permute-start.1 = (bf16[2,256,512]{2,1,0:T(8,128)(2,1)S(1)}, bf16[2,256,512]{2,1,0:T(8,128)(2,1)S(1)}, u32[]{:S(2)}, u32[]{:S(2)}) collective-permute-start(bf16[2,256,512]{2,1,0:T(8,128)(2,1)S(1)} %pad_maximum_fusion.refs_0_), channel_id=1, source_target_pairs={{0,1},{1,0},{2,3},{3,2},{4,5},{5,4},{6,7},{7,6},{8,24},{9,25},{10,... | collective-permute-start | bytes 1572872 | tf_op jit(solution)/shard_map/ppermute | solution.py:278
  54.3 21.2 %copy-start = (bf16[2,512,256]{2,1,0:T(8,128)(2,1)}, bf16[2,512,256]{2,1,0:T(8,128)(2,1)S(1)}, u32[]{:S(2)}) copy-start(bf16[2,512,256]{2,1,0:T(8,128)(2,1)S(1)} %get-tuple-element.17) | copy-start | bytes 1572868
  57.9 13.8 %collective-permute-start.2 = (bf16[2,256,512]{2,1,0:T(8,128)(2,1)S(1)}, bf16[2,256,512]{2,1,0:T(8,128)(2,1)S(1)}, u32[]{:S(2)}, u32[]{:S(2)}) collective-permute-start(bf16[2,256,512]{2,1,0:T(8,128)(2,1)S(1)} %pad_maximum_fusion.refs_0_), channel_id=1, source_target_pairs={{0,8},{1,9},{2,10},{3,11},{4,12},{5,13},{6,14},{7,15},{8,0},{9,1},... | collective-permute-start | bytes 1572872 | tf_op jit(solution)/shard_map/ppermute | solution.py:278
  57.9 17.1 %collective-permute-start.16 = (bf16[2,512,256]{2,1,0:T(8,128)(2,1)S(1)}, bf16[2,512,256]{2,1,0:T(8,128)(2,1)S(1)}, u32[]{:S(2)}, u32[]{:S(2)}) collective-permute-start(bf16[2,512,256]{2,1,0:T(8,128)(2,1)S(1)} %get-tuple-element.18), channel_id=1, source_target_pairs={{0,1},{1,0},{2,3},{3,2},{4,5},{5,4},{6,7},{7,6},{8,24},{9,25},{10,... | collective-permute-start | bytes 1572872 | tf_op jit(solution)/shard_map/ppermute | solution.py:278
  58.5 10.2 %copy-start.1 = (bf16[2,256,512]{2,1,0:T(8,128)(2,1)}, bf16[2,256,512]{2,1,0:T(8,128)(2,1)S(1)}, u32[]{:S(2)}) copy-start(bf16[2,256,512]{2,1,0:T(8,128)(2,1)S(1)} %constant_dynamic-update-slice_fusion.3.refs_8_) | copy-start | bytes 1572868
  68.7 16.9 %copy-start.6 = (bf16[2,256,512]{2,1,0:T(8,128)(2,1)}, bf16[2,256,512]{2,1,0:T(8,128)(2,1)S(1)}, u32[]{:S(2)}) copy-start(bf16[2,256,512]{2,1,0:T(8,128)(2,1)S(1)} %collective-permute-done.1.refs_1_) | copy-start | bytes 1572868
  68.7 16.8 %collective-permute-start.12 = (bf16[2,256,512]{2,1,0:T(8,128)(2,1)S(1)}, bf16[2,256,512]{2,1,0:T(8,128)(2,1)S(1)}, u32[]{:S(2)}, u32[]{:S(2)}) collective-permute-start(bf16[2,256,512]{2,1,0:T(8,128)(2,1)S(1)} %constant_dynamic-update-slice_fusion.3.refs_8_), channel_id=1, source_target_pairs={{0,1},{1,0},{2,3},{3,2},{4,5},{5,4},{6,7},{7,6},{8,24},{9,25},{10,... | collective-permute-start | bytes 1572872 | tf_op jit(solution)/shard_map/ppermute | solution.py:278
  69.6 16.0 %copy-start.12 = (bf16[4,512,256]{2,1,0:T(8,128)(2,1)}, bf16[4,512,256]{2,1,0:T(8,128)(2,1)S(1)}, u32[]{:S(2)}) copy-start(bf16[4,512,256]{2,1,0:T(8,128)(2,1)S(1)} %collective-permute-done.20) | copy-start | bytes 3145732
  69.6 24.6 %collective-permute-start.25 = (bf16[2,512,256]{2,1,0:T(8,128)(2,1)}, bf16[2,512,256]{2,1,0:T(8,128)(2,1)S(1)}, u32[]{:S(2)}, u32[]{:S(2)}) collective-permute-start(bf16[2,512,256]{2,1,0:T(8,128)(2,1)} %get-tuple-element.22), channel_id=1, source_target_pairs={{0,1},{1,0},{2,3},{3,2},{4,5},{5,4},{6,7},{7,6},{8,24},{9,25},{10,... | collective-permute-start | bytes 1572872 | tf_op jit(solution)/shard_map/ppermute | solution.py:278
  71.8 13.8 %copy-start.8 = (bf16[2,256,512]{2,1,0:T(8,128)(2,1)}, bf16[2,256,512]{2,1,0:T(8,128)(2,1)S(1)}, u32[]{:S(2)}) copy-start(bf16[2,256,512]{2,1,0:T(8,128)(2,1)S(1)} %collective-permute-done.2.refs_2_) | copy-start | bytes 1572868
  71.8 23.0 %collective-permute-start.21 = (bf16[2,512,256]{2,1,0:T(8,128)(2,1)}, bf16[2,512,256]{2,1,0:T(8,128)(2,1)}, u32[]{:S(2)}, u32[]{:S(2)}) collective-permute-start(bf16[2,512,256]{2,1,0:T(8,128)(2,1)} %add_convert_fusion), channel_id=1, source_target_pairs={{0,16},{1,17},{2,18},{3,19},{4,20},{5,21},{6,22},{7,23},{8,9},{9,8... | collective-permute-start | bytes 1572872 | tf_op jit(solution)/shard_map/ppermute | solution.py:278
  75.0 10.6 %copy-start.13 = (bf16[2,512,256]{2,1,0:T(8,128)(2,1)}, bf16[2,512,256]{2,1,0:T(8,128)(2,1)S(1)}, u32[]{:S(2)}) copy-start(bf16[2,512,256]{2,1,0:T(8,128)(2,1)S(1)} %collective-permute-done.16) | copy-start | bytes 1572868
  75.0 28.8 %collective-permute-start.8 = (bf16[4,256,512]{2,1,0:T(8,128)(2,1)}, bf16[4,256,512]{2,1,0:T(8,128)(2,1)}, u32[]{:S(2)}, u32[]{:S(2)}) collective-permute-start(bf16[4,256,512]{2,1,0:T(8,128)(2,1)} %constant_dynamic-update-slice_fusion.refs_4_), channel_id=1, source_target_pairs={{0,8},{1,9},{2,10},{3,11},{4,12},{5,13},{6,14},{7,15},{8,0},{9,1},... | collective-permute-start | bytes 3145736 | tf_op jit(solution)/shard_map/ppermute | solution.py:278
  75.0 30.8 %collective-permute-start.9 = (bf16[4,256,512]{2,1,0:T(8,128)(2,1)}, bf16[4,256,512]{2,1,0:T(8,128)(2,1)}, u32[]{:S(2)}, u32[]{:S(2)}) collective-permute-start(bf16[4,256,512]{2,1,0:T(8,128)(2,1)} %collective-permute-done.7.refs_5_), channel_id=1, source_target_pairs={{0,8},{1,9},{2,10},{3,11},{4,12},{5,13},{6,14},{7,15},{8,0},{9,1},... | collective-permute-start | bytes 3145736 | tf_op jit(solution)/shard_map/ppermute | solution.py:278
  85.6 0.8 copy-start.10
  86.4 8.0 %collective-permute-start.17 = (bf16[1,512,256]{2,1,0:T(8,128)(2,1)S(1)}, bf16[1,512,256]{2,1,0:T(8,128)(2,1)}, u32[]{:S(2)}, u32[]{:S(2)}) collective-permute-start(bf16[1,512,256]{2,1,0:T(8,128)(2,1)S(1)} %add_convert_fusion.5), channel_id=1, source_target_pairs={{0,16},{1,17},{2,18},{3,19},{4,20},{5,21},{6,22},{7,23},{8,9},{9,8... | collective-permute-start | bytes 786440 | tf_op jit(solution)/shard_map/ppermute | solution.py:278
  89.4 33.5 %all-to-all-start = ((bf16[32,16,512]{2,1,0:T(8,128)(2,1)}), bf16[32,16,512]{2,1,0:T(8,128)(2,1)S(1)}, u32[]{:S(2)}, u32[]{:S(2)}) async-start(bf16[32,16,512]{2,1,0:T(8,128)(2,1)} %pack_moments.1), calls=%async_computation | async-start | bytes 1048576 | tf_op jit(solution)/shard_map/all_to_all | solution.py:384
  94.1 11.7 %copy-start.2 = (bf16[2,256,512]{2,1,0:T(8,128)(2,1)S(1)}, bf16[2,256,512]{2,1,0:T(8,128)(2,1)}, u32[]{:S(2)}) copy-start(bf16[2,256,512]{2,1,0:T(8,128)(2,1)} %copy-done.1) | copy-start | bytes 1572868
  94.1 11.7 %copy-start.4 = (s32[8]{0:T(128)S(1)}, s32[8]{0:T(128)}, u32[]{:S(2)}) copy-start(s32[8]{0:T(128)} %new_ref.15) | copy-start | bytes 100
  94.1 11.7 %copy-start.5 = (s32[32]{0:T(128)S(1)}, s32[32]{0:T(128)}, u32[]{:S(2)}) copy-start(s32[32]{0:T(128)} %owner_ref.1) | copy-start | bytes 388
  94.1 11.7 %copy-start.7 = (bf16[2,256,512]{2,1,0:T(8,128)(2,1)S(1)}, bf16[2,256,512]{2,1,0:T(8,128)(2,1)}, u32[]{:S(2)}) copy-start(bf16[2,256,512]{2,1,0:T(8,128)(2,1)} %copy-done.6) | copy-start | bytes 1572868
  94.1 11.7 %copy-start.9 = (bf16[2,256,512]{2,1,0:T(8,128)(2,1)S(1)}, bf16[2,256,512]{2,1,0:T(8,128)(2,1)}, u32[]{:S(2)}) copy-start(bf16[2,256,512]{2,1,0:T(8,128)(2,1)} %copy-done.8) | copy-start | bytes 1572868
  94.2 11.7 %copy-start.11 = (bf16[2,256,512]{2,1,0:T(8,128)(2,1)S(1)}, bf16[2,256,512]{2,1,0:T(8,128)(2,1)}, u32[]{:S(2)}) copy-start(bf16[2,256,512]{2,1,0:T(8,128)(2,1)} %copy-done.10) | copy-start | bytes 1572868
  94.2 5.7 %collective-permute-start.13 = (bf16[2,256,512]{2,1,0:T(8,128)(2,1)}, bf16[2,256,512]{2,1,0:T(8,128)(2,1)S(1)}, u32[]{:S(2)}, u32[]{:S(2)}) collective-permute-start(bf16[2,256,512]{2,1,0:T(8,128)(2,1)} %copy-done.1), channel_id=1, source_target_pairs={{0,8},{1,9},{2,10},{3,11},{4,12},{5,13},{6,14},{7,15},{8,0},{9,1},... | collective-permute-start | bytes 1572872 | tf_op jit(solution)/shard_map/ppermute | solution.py:278
  94.4 6.9 %collective-permute-start.3 = (bf16[2,256,512]{2,1,0:T(8,128)(2,1)}, bf16[2,256,512]{2,1,0:T(8,128)(2,1)S(1)}, u32[]{:S(2)}, u32[]{:S(2)}) collective-permute-start(bf16[2,256,512]{2,1,0:T(8,128)(2,1)} %copy-done.6), channel_id=1, source_target_pairs={{0,8},{1,9},{2,10},{3,11},{4,12},{5,13},{6,14},{7,15},{8,0},{9,1},... | collective-permute-start | bytes 1572872 | tf_op jit(solution)/shard_map/ppermute | solution.py:278
  94.8 9.0 %collective-permute-start.14 = (bf16[2,256,512]{2,1,0:T(8,128)(2,1)}, bf16[2,256,512]{2,1,0:T(8,128)(2,1)S(1)}, u32[]{:S(2)}, u32[]{:S(2)}) collective-permute-start(bf16[2,256,512]{2,1,0:T(8,128)(2,1)} %copy-done.10), channel_id=1, source_target_pairs={{0,8},{1,9},{2,10},{3,11},{4,12},{5,13},{6,14},{7,15},{8,0},{9,1},... | collective-permute-start | bytes 1572872 | tf_op jit(solution)/shard_map/ppermute | solution.py:278
  99.8 23.0 %collective-permute-start.26 = (bf16[1,512,256]{2,1,0:T(8,128)(2,1)}, bf16[1,512,256]{2,1,0:T(8,128)(2,1)S(1)}, u32[]{:S(2)}, u32[]{:S(2)}) collective-permute-start(bf16[1,512,256]{2,1,0:T(8,128)(2,1)} %add_convert_fusion.1), channel_id=1, source_target_pairs={{0,16},{1,17},{2,18},{3,19},{4,20},{5,21},{6,22},{7,23},{8,9},{9,8... | collective-permute-start | bytes 786440 | tf_op jit(solution)/shard_map/ppermute | solution.py:278
  101.3 21.7 %collective-permute-start.18 = (bf16[1,512,256]{2,1,0:T(8,128)(2,1)}, bf16[1,512,256]{2,1,0:T(8,128)(2,1)S(1)}, u32[]{:S(2)}, u32[]{:S(2)}) collective-permute-start(bf16[1,512,256]{2,1,0:T(8,128)(2,1)} %add_convert_fusion.4), channel_id=1, source_target_pairs={{0,4},{1,5},{2,6},{3,7},{4,0},{5,1},{6,2},{7,3},{8,12},{9,13},{10,... | collective-permute-start | bytes 786440 | tf_op jit(solution)/shard_map/ppermute | solution.py:278
  103.8 24.6 %collective-permute-start.22 = (bf16[1,512,256]{2,1,0:T(8,128)(2,1)}, bf16[1,512,256]{2,1,0:T(8,128)(2,1)S(1)}, u32[]{:S(2)}, u32[]{:S(2)}) collective-permute-start(bf16[1,512,256]{2,1,0:T(8,128)(2,1)} %get-tuple-element.27), channel_id=1, source_target_pairs={{0,2},{1,3},{2,4},{3,5},{4,6},{5,7},{6,0},{7,1},{8,10},{9,11},{10,... | collective-permute-start | bytes 786440 | tf_op jit(solution)/shard_map/ppermute | solution.py:278
  103.8 26.6 %collective-permute-start.23 = (bf16[1,512,256]{2,1,0:T(8,128)(2,1)}, bf16[1,512,256]{2,1,0:T(8,128)(2,1)S(1)}, u32[]{:S(2)}, u32[]{:S(2)}) collective-permute-start(bf16[1,512,256]{2,1,0:T(8,128)(2,1)} %get-tuple-element.26), channel_id=1, source_target_pairs={{0,6},{1,7},{2,0},{3,1},{4,2},{5,3},{6,4},{7,5},{8,14},{9,15},{10,... | collective-permute-start | bytes 786440 | tf_op jit(solution)/shard_map/ppermute | solution.py:278

commit v5 on v4

--- a/solution.py
+++ b/solution.py
@@ -16,7 +16,7 @@
 correction_two = 1.0 - 0.95**10
 
 AXES = ("rep", "fsdp")
-GRANT = 48 * 1024 * 1024
+MIB = 1024 * 1024
 SUB = 8
 
 
@@ -29,25 +29,28 @@
     return new_ref[lax.rem(position, shards)] * groups + lax.div(position, shards)
 
 
-def grad_kernel(per_step, adds, row_ref, new_ref, *refs):
+def grad_kernel(per_step, adds, outs, row_ref, new_ref, *refs):
     token_refs, turned_ref, refs = refs[:per_step], refs[per_step], refs[per_step + 1 :]
-    out_refs = refs[adds:]
-
-    def write(out_ref):
+    out_refs = refs[-outs:]
+    step = pl.program_id(0)
+
+    def write(out_ref, start):
         for slot, token_ref in enumerate(token_refs):
             block = jnp.dot(turned_ref[...], token_ref[...], preferred_element_type=jnp.float32)
             if adds:
-                block = block + refs[0][slot].astype(jnp.float32)
-            out_ref[slot] = block.astype(out_ref.dtype)
-
-    if len(out_refs) == 1:
-        write(out_refs[0])
+                block = block + refs[0][step * per_step + slot].astype(jnp.float32)
+            out_ref[start + slot] = block.astype(out_ref.dtype)
+
+    if outs == 1:
+        write(out_refs[0], step * per_step)
         return
-    for step, out_ref in enumerate(out_refs):
-        pl.when(pl.program_id(0) == step)(functools.partial(write, out_ref))
-
-
-def grad_blocks(tokens, turned, row, new_owner, first, steps, per_step, addend=None, cut=False):
+    for part, out_ref in enumerate(out_refs):
+        pl.when(step == part)(functools.partial(write, out_ref, 0))
+
+
+def grad_blocks(
+    tokens, turned, row, new_owner, first, steps, per_step, addend=None, cut=False, after=()
+):
     rows, features = tokens.shape
     width = turned.shape[0]
     blocks = steps * per_step
@@ -72,28 +75,27 @@
             block_at(new_ref, groups, row_ref[first + i * per_step + slot]),
         )
 
-    block = pl.BlockSpec((per_step, width, row_block), lambda i, *_: (i, 0, 0))
-    fixed = pl.BlockSpec((per_step, width, row_block), lambda i, *_: (0, 0, 0))
+    whole = pl.BlockSpec(memory_space=pltpu.VMEM)
     added = [] if addend is None else [addend]
     outs = steps if cut else 1
     return pl.pallas_call(
-        functools.partial(grad_kernel, per_step, len(added)),
+        functools.partial(grad_kernel, per_step, len(added), outs),
         grid_spec=pltpu.PrefetchScalarGridSpec(
             num_scalar_prefetch=2,
             grid=(steps,),
             in_specs=[pl.BlockSpec((rows, row_block), token_map(s)) for s in range(per_step)]
-            + [pl.BlockSpec((width, rows), lambda i, *_: (0, 0))]
-            + [block] * len(added),
-            out_specs=[fixed if cut else block] * outs,
+            + [whole] * (1 + len(added))
+            + [pl.BlockSpec(memory_space=pl.ANY)] * len(after),
+            out_specs=[whole] * outs,
         ),
         out_shape=[jax.ShapeDtypeStruct((blocks // outs, width, row_block), jnp.bfloat16)] * outs,
-        compiler_params=pltpu.CompilerParams(vmem_limit_bytes=GRANT),
+        compiler_params=pltpu.CompilerParams(vmem_limit_bytes=46 * MIB),
         cost_estimate=cost(
             2 * rows * width * blocks * row_block,
             2 * blocks * row_block * (rows + width * (1 + len(added))) + 2 * rows * width,
         ),
         name="weight_gradient",
-    )(row, new_owner, *([tokens] * per_step), turned, *added)
+    )(row, new_owner, *([tokens] * per_step), turned, *added, *after)
 
 
 def pack_kernel(groups, new_ref, first_ref, second_ref, out_ref):
@@ -187,7 +189,7 @@
             jax.ShapeDtypeStruct((rows, width), jnp.bfloat16),
             jax.ShapeDtypeStruct((row_block, width), jnp.bfloat16),
         ],
-        compiler_params=pltpu.CompilerParams(vmem_limit_bytes=GRANT),
+        compiler_params=pltpu.CompilerParams(vmem_limit_bytes=46 * MIB),
         cost_estimate=cost(
             2 * rows * width * features, 2 * (rows * features + features * width + rows * width)
         ),
@@ -227,26 +229,21 @@
 
 def adam_rows(parts, moments, weight_rows, owners):
     row_block, width = weight_rows.shape
-    whole = pl.BlockSpec((row_block, width), lambda i, *_: (0, 0))
+    whole = pl.BlockSpec(memory_space=pltpu.VMEM)
     return pl.pallas_call(
         adam_kernel,
-        grid_spec=pltpu.PrefetchScalarGridSpec(
-            num_scalar_prefetch=1,
-            grid=(1,),
-            in_specs=[pl.BlockSpec(moments.shape, lambda i, *_: (0, 0, 0)), whole]
-            + [pl.BlockSpec((1, width, row_block), lambda i, *_: (0, 0, 0))] * len(parts),
-            out_specs=[whole] * 3,
-            scratch_shapes=[
-                pltpu.VMEM((row_block, width), jnp.float32),
-                pltpu.SMEM((moments.shape[0],), jnp.int32),
-            ],
-        ),
+        in_specs=[pl.BlockSpec(memory_space=pltpu.SMEM)] + [whole] * (2 + len(parts)),
+        out_specs=[whole] * 3,
+        scratch_shapes=[
+            pltpu.VMEM((row_block, width), jnp.float32),
+            pltpu.SMEM((moments.shape[0],), jnp.int32),
+        ],
         out_shape=[
             jax.ShapeDtypeStruct((row_block, width), jnp.bfloat16),
             jax.ShapeDtypeStruct((row_block, width), jnp.float32),
             jax.ShapeDtypeStruct((row_block, width), jnp.float32),
         ],
-        compiler_params=pltpu.CompilerParams(vmem_limit_bytes=GRANT),
+        compiler_params=pltpu.CompilerParams(vmem_limit_bytes=12 * MIB),
         cost_estimate=cost(20 * row_block * width, 16 * row_block * width),
         name="adam_rows",
     )(owners, moments, weight_rows, *parts)
@@ -278,11 +275,30 @@
         return lax.ppermute(value, AXES, pairs)
 
 
-def rounded_sum(*terms):
-    total = terms[0].astype(jnp.float32)
-    for term in terms[1:]:
-        total = total + term.astype(jnp.float32)
-    return total.astype(terms[0].dtype)
+def sum_kernel(start, count, terms, *refs):
+    out_ref = refs[-1]
+    total = refs[0][start : start + count].astype(jnp.float32)
+    for ref in refs[1:terms]:
+        total = total + ref[start : start + count].astype(jnp.float32)
+    out_ref[...] = total.astype(out_ref.dtype)
+
+
+def rounded_sum(terms, start, count, after=()):
+    shape = (count, *terms[0].shape[1:])
+    if shape[-1] % 128:
+        total = sum(term[start : start + count].astype(jnp.float32) for term in terms)
+        return total.astype(terms[0].dtype)
+    whole = pl.BlockSpec(memory_space=pltpu.VMEM)
+    size = count * shape[1] * shape[2]
+    return pl.pallas_call(
+        functools.partial(sum_kernel, start, count, len(terms)),
+        in_specs=[whole] * len(terms) + [pl.BlockSpec(memory_space=pl.ANY)] * len(after),
+        out_specs=whole,
+        out_shape=jax.ShapeDtypeStruct(shape, terms[0].dtype),
+        compiler_params=pltpu.CompilerParams(vmem_limit_bytes=12 * MIB),
+        cost_estimate=cost(size * len(terms), 2 * size * (len(terms) + 1)),
+        name="add_blocks",
+    )(*terms, *after)
 
 
 def chunks(grid):
@@ -312,44 +328,58 @@
     )
 
 
-def reduce_rows(grid, blocks_of):
+def reduce_rows(grid, blocks_of, project_now):
+    plan = []
+    start = 0
+    for number, chunk in enumerate(chunks(grid)):
+        plan.insert(0, (number, chunk, start))
+        start += len(chunk)
+    addends = {}
+    if grid.cores > 1:
+        for number, chunk, start in plan:
+            block = blocks_of(1, number, start, len(chunk), None, False)[0]
+            addends[number] = grid.send(block, core=1)
+    held = {}
+    for number, chunk, start in plan:
+        parts = blocks_of(0, number, start, len(chunk), addends.get(number), True)
+        held[number] = [parts[-1]]
+        for step, part in enumerate(parts[:-1], 1):
+            held[number].append(grid.send(part, near=step))
+    projection = project_now()
     last = []
-    start = grid.far
-    for chunk in reversed(chunks(grid)):
+    for number, chunk, _ in plan:
         count = len(chunk)
-        start -= count
-        addend = None
-        if grid.cores > 1:
-            addend = grid.send(blocks_of(1, start, count, None, False)[0], core=1)
-        parts = blocks_of(0, start, count, addend, True)
-        kept = [parts[-1]]
-        for step, part in enumerate(parts[:-1], 1):
-            kept.append(grid.send(part, near=step))
+        kept = held[number]
         ends = list(kept)
         for step in range(1, grid.side):
-            cut = slice(step * count, (step + 1) * count)
-            ends.append(grid.send(rounded_sum(*[t[cut] for t in kept]), side=step))
+            part = rounded_sum(kept, step * count, count, projection[1:])
+            ends.append(grid.send(part, side=step))
+        held[number] = ends
+    for number, chunk, _ in plan:
+        ends = held[number]
         if chunk == [0]:
             last.extend(ends)
             continue
         for index, far in enumerate(chunk):
-            cut = slice(index, index + 1)
-            last.append(grid.send(rounded_sum(*[t[cut] for t in ends]), far=far))
-    return last
+            last.append(grid.send(rounded_sum(ends, index, 1), far=far))
+    return last, projection
 
 
 def gather_shards(grid, own):
     arrived = {far: grid.send(own, far=far) for far in range(1, grid.far)}
     arrived[0] = own
-    pieces = []
+    pieces, marks = [], []
     for chunk in chunks(grid):
         base = joined([arrived[far] for far in chunk])
-        plane = joined([base] + [grid.send(base, side=step) for step in range(1, grid.side)])
-        both = [plane] + [grid.send(plane, near=step) for step in range(1, grid.near)]
+        sides = [grid.send(base, side=step) for step in range(1, grid.side)]
+        plane = joined([base] + sides)
+        nears = [grid.send(plane, near=step) for step in range(1, grid.near)]
+        both = [plane] + nears
+        marks.append((sides, nears, [arrived[far] for far in chunk]))
         pieces += both
         for core in range(1, grid.cores):
             pieces += [grid.send(part, core=core) for part in both]
-    return pieces
+    return pieces, marks
 
 
 def joined(arrays):
@@ -371,7 +401,7 @@
     per_far = grid.near * grid.side
     own = (grid.near - 1) * grid.side
 
-    pieces = gather_shards(grid, old_weight[None])
+    pieces, marks = gather_shards(grid, old_weight[None])
     if by_tile:
         packed = pack_moments(old_first, old_second, new_owner, groups)
     else:
@@ -385,16 +415,35 @@
 
     turned = cotangent.T
 
-    def blocks_of(core, start, count, addend, cut):
+    waits = {
+        (1, 2): [packed, *marks[0][0]],
+        (1, 1): marks[1][2],
+        (1, 0): [*marks[1][0], *marks[2][2]],
+        (0, 2): [*marks[0][1], *marks[2][0]],
+        (0, 0): [*marks[1][1], arrived],
+    }
+    if not by_tile:
+        waits = {}
+    done = []
+
+    def blocks_of(core, chunk, start, count, addend, cut):
         first = (start * grid.cores + core * count) * per_far
         per_step = grid.side * count
-        return grad_blocks(
-            tokens, turned, row, new_owner, first, grid.near, per_step, addend, cut
+        after = [*waits.get((core, chunk), ()), *done[-1:]]
+        blocks = grad_blocks(
+            tokens, turned, row, new_owner, first, grid.near, per_step, addend, cut, after
         )
-
-    parts = reduce_rows(grid, blocks_of)
+        done.append(blocks[0])
+        return blocks
+
+    def project_now():
+        if by_tile:
+            return project(tokens, pieces, row, devices, own, old_owner, new_owner)
+        return ()
+
+    parts, projection = reduce_rows(grid, blocks_of, project_now)
     if by_tile:
-        projected, weight_rows = project(tokens, pieces, row, devices, own, old_owner, new_owner)
+        projected, weight_rows = projection
         return (projected, *adam_rows(parts, arrived, weight_rows, old_owner))
     inverse = jnp.zeros((devices,), jnp.int32).at[old_owner].set(slot_ids)
     held = jnp.zeros((devices, devices, strip), jnp.bfloat16)

time: 133 us -> 149 us (1.12)
  local copies, waits for them, and re-layouts: 5.33 us -> 13.9 us
  other arithmetic: 6.09 us -> 0.1 us
  Pallas kernels: 45.2 us -> 50.4 us
  waiting for transfers between devices: 48.3 us -> 52.7 us
  starting transfers between devices: 26.7 us -> 29.7 us
    unnamed x34 -> x46, local copies, waits for them, and re-layouts: 3.78 us -> 11.6 us
    convert_element_type x5 -> x0, other arithmetic: 5.99 us -> none  [rounded_sum(): return total.astype(terms[0].dtype)]
    pallas_call x7 -> x13, Pallas kernels: 26.2 us -> 30.7 us  [the longest x6 27.4 us: grad_blocks(): pl.pallas_call(functools.partial(grad_kernel, per_step, len(added), outs)...]
    ppermute x27, waiting for transfers between devices: 48.3 us -> 52.1 us  [send(): return lax.ppermute(value, AXES, pairs)]
    ppermute x27, starting transfers between devices: 22 us -> 24.6 us  [send(): return lax.ppermute(value, AXES, pairs)]
  transfers between devices with their start and end apart: 28 -> 28, of which waited for: 10 -> 8; matrix products, arithmetic and copies ran while one was open for 6% -> 5% of each run, Pallas kernels for 29% -> 32%
where the time goes in v5:
time: 149 us; the launch traced here: 148 us
  waiting for transfers between devices  52.7 us (35%)
  Pallas kernels  50.4 us (34%)
  starting transfers between devices  29.7 us (20%)
  local copies, waits for them, and re-layouts  13.9 us (9%)
    ppermute x27, waiting for transfers between devices, send(): return lax.ppermute(value, AXES, pairs)  52.1 us
    pallas_call x6, Pallas kernels, grad_blocks(): pl.pallas_call(functools.partial(grad_kernel, per_step, len(added), outs)...  27.4 us
    ppermute x27, starting transfers between devices, send(): return lax.ppermute(value, AXES, pairs)  24.6 us
    pallas_call x1, Pallas kernels, project(): pl.pallas_call(functools.partial(project_kernel, devices // new_owner.sha...  17.7 us
    unnamed x46, local copies, waits for them, and re-layouts  11.6 us
    all_to_all x1, starting transfers between devices, body(): lax.all_to_all(packed, AXES, split_axis=0, concat_axis=0, tiled=True)  5.04 us
  transfers between devices with their start and end apart: 28, of which 8 were waited for; matrix products, arithmetic and copies ran while one was open for 5% of the time, Pallas kernels for 32%

profile of v5, /device:TPU:8, one launch (start us, length us, event | category | flops | bytes accessed | tf_op | source)
XLA Modules:
  0.0 147.8 jit_solution(17725894307811338675)
XLA Ops:
  0.6 1.6 %collective-permute-start.4 = (bf16[1,256,512]{2,1,0:T(8,128)(2,1)}, bf16[1,256,512]{2,1,0:T(8,128)(2,1)S(1)}, u32[]{:S(2)}, u32[]{:S(2)}) collective-permute-start(bf16[1,256,512]{2,1,0:T(8,128)(2,1)} %bitcast.10), channel_id=1, source_target_pairs={{0,2},{1,3},{2,4},{3,5},{4,6},{5,7},{6,0},{7,1},{8,10},{9,11},{10,... | collective-permute-start | bytes 786440 | tf_op jit(solution)/shard_map/ppermute | solution.py:275
  2.3 0.4 collective-permute-start.5
  2.7 1.5 %collective-permute-start = (bf16[1,256,512]{2,1,0:T(8,128)(2,1)}, bf16[1,256,512]{2,1,0:T(8,128)(2,1)S(1)}, u32[]{:S(2)}, u32[]{:S(2)}) collective-permute-start(bf16[1,256,512]{2,1,0:T(8,128)(2,1)} %bitcast.12), channel_id=1, source_target_pairs={{0,16},{1,17},{2,18},{3,19},{4,20},{5,21},{6,22},{7,23},{8,9},{9,8... | collective-permute-start | bytes 786440 | tf_op jit(solution)/shard_map/ppermute | solution.py:275
  4.2 2.6 %collective-permute-start.10 = (bf16[1,256,512]{2,1,0:T(8,128)(2,1)}, bf16[1,256,512]{2,1,0:T(8,128)(2,1)}, u32[]{:S(2)}, u32[]{:S(2)}) collective-permute-start(bf16[1,256,512]{2,1,0:T(8,128)(2,1)} %bitcast.13), channel_id=1, source_target_pairs={{0,4},{1,5},{2,6},{3,7},{4,0},{5,1},{6,2},{7,3},{8,12},{9,13},{10,... | collective-permute-start | bytes 786440 | tf_op jit(solution)/shard_map/ppermute | solution.py:275
  6.8 1.5 %copy.12 = bf16[1024,512]{0,1:T(8,128)(2,1)S(1)} copy(bf16[1024,512]{1,0:T(8,128)(2,1)} %param.9) | data formatting | bytes 2097152 | tf_op args[1]
  8.3 2.1 %pack_moments.1.refs_3_ = bf16[32,16,512]{2,1,0:T(8,128)(2,1)} custom-call(s32[8]{0:T(128)} %new_ref.15, f32[256,512]{1,0:T(8,128)} %first_ref.1, f32[256,512]{1,0:T(8,128)} %second_ref.1), custom_call_target="tpu_custom_call" | custom-call | bytes 1572864 | tf_op jit(solution)/shard_map/pack_moments/pallas_call | solution.py:112
  10.4 0.7 dynamic-slice_bitcast_fusion.row_ref
  11.1 9.4 %collective-permute-done.4.refs_5_ = bf16[1,256,512]{2,1,0:T(8,128)(2,1)S(1)} collective-permute-done((bf16[1,256,512]{2,1,0:T(8,128)(2,1)}, bf16[1,256,512]{2,1,0:T(8,128)(2,1)S(1)}, u32[]{:S(2)}, u32[]{:S(2)}) %collective-permute-start.4) | collective-permute-done | bytes 262176 | tf_op jit(solution)/shard_map/ppermute | solution.py:275
  20.6 1.6 %collective-permute-start.6 = (bf16[2,256,512]{2,1,0:T(8,128)(2,1)S(1)}, bf16[2,256,512]{2,1,0:T(8,128)(2,1)S(1)}, u32[]{:S(2)}, u32[]{:S(2)}) collective-permute-start(bf16[2,256,512]{2,1,0:T(8,128)(2,1)S(1)} %pad_maximum_fusion.1), channel_id=1, source_target_pairs={{0,16},{1,17},{2,18},{3,19},{4,20},{5,21},{6,22},{7,23},{8,9},{9,8... | collective-permute-start | bytes 1572872 | tf_op jit(solution)/shard_map/ppermute | solution.py:275
  22.2 0.7 copy-done.7
  22.9 1.0 copy-done
  23.9 0.9 copy-done.8
  24.9 4.3 %weight_gradient.6.refs_7_ = bf16[4,512,256]{2,1,0:T(8,128)(2,1)} custom-call(s32[64]{0:T(128)S(1)} %dynamic-slice_bitcast_fusion.row_ref, s32[8]{0:T(128)S(1)} %copy-done.14, bf16[1024,8192]{1,0:T(8,128)(2,1)} %refs_1_.11, bf16[1024,8192]{1,0:T(8,128)(2,1)} %refs_1_.11, bf16[512,1024]{1,0:T(8,128)(2,1)S(1)} %bitcast.4, bf16[32,16,512]{2,1,0:T(8,128)(2,1)S(1)} %copy-done, ...), custom_call_target="tpu_custom_call" | custom-call | flops 1073741824 | bytes 4194304 | tf_op jit(solution)/shard_map/weight_gradient/pallas_call | solution.py:81
  29.1 0.9 copy-done.2
  30.1 4.9 %weight_gradient.7.refs_5_ = bf16[8,512,256]{2,1,0:T(8,128)(2,1)S(1)} custom-call(s32[64]{0:T(128)S(1)} %dynamic-slice_bitcast_fusion.row_ref, s32[8]{0:T(128)S(1)} %copy-done.14, bf16[1024,8192]{1,0:T(8,128)(2,1)} %refs_1_.11, bf16[1024,8192]{1,0:T(8,128)(2,1)} %refs_1_.11, bf16[1024,8192]{1,0:T(8,128)(2,1)} %refs_1_.11, bf16[1024,8192]{1,0:T(8,128)(2,1)} %refs_1_.11, ...), custom_call_target="tpu_custom_call" | custom-call | flops 2147483648 | bytes 7340032 | tf_op jit(solution)/shard_map/weight_gradient/pallas_call | solution.py:81
  35.0 0.1 collective-permute-start.19
  35.1 0.1 pad_maximum_fusion.refs_0_
  35.1 1.6 %collective-permute-start.1 = (bf16[2,256,512]{2,1,0:T(8,128)(2,1)S(1)}, bf16[2,256,512]{2,1,0:T(8,128)(2,1)}, u32[]{:S(2)}, u32[]{:S(2)}) collective-permute-start(bf16[2,256,512]{2,1,0:T(8,128)(2,1)S(1)} %pad_maximum_fusion.refs_0_), channel_id=1, source_target_pairs={{0,1},{1,0},{2,3},{3,2},{4,5},{5,4},{6,7},{7,6},{8,24},{9,25},{10,... | collective-permute-start | bytes 1572872 | tf_op jit(solution)/shard_map/ppermute | solution.py:275
  36.7 0.7 collective-permute-start.11
  37.4 0.7 constant_dynamic-update-slice_fusion.2
  38.2 0.7 constant_dynamic-update-slice_fusion.1
  38.9 0.8 constant_dynamic-update-slice_fusion.refs_4_
  39.7 1.5 %collective-permute-start.7 = (bf16[4,256,512]{2,1,0:T(8,128)(2,1)}, bf16[4,256,512]{2,1,0:T(8,128)(2,1)}, u32[]{:S(2)}, u32[]{:S(2)}) collective-permute-start(bf16[4,256,512]{2,1,0:T(8,128)(2,1)} %constant_dynamic-update-slice_fusion.refs_4_), channel_id=1, source_target_pairs={{0,1},{1,0},{2,3},{3,2},{4,5},{5,4},{6,7},{7,6},{8,24},{9,25},{10,... | collective-permute-start | bytes 3145736 | tf_op jit(solution)/shard_map/ppermute | solution.py:275
  41.2 1.6 %constant_dynamic-update-slice_fusion.4 = bf16[2,256,512]{2,1,0:T(8,128)(2,1)} fusion(bf16[1,256,512]{2,1,0:T(8,128)(2,1)} %collective-permute-done.10.refs_4_), kind=kLoop, calls=%fused_computation.6 | loop fusion | bytes 524288
  42.9 3.3 %collective-permute-done.11.refs_5_ = bf16[1,256,512]{2,1,0:T(8,128)(2,1)S(1)} collective-permute-done((bf16[1,256,512]{2,1,0:T(8,128)(2,1)}, bf16[1,256,512]{2,1,0:T(8,128)(2,1)S(1)}, u32[]{:S(2)}, u32[]{:S(2)}) %collective-permute-start.11) | collective-permute-done | bytes 262176 | tf_op jit(solution)/shard_map/ppermute | solution.py:275
  46.2 0.8 constant_dynamic-update-slice_fusion.3.refs_8_
  46.9 0.7 collective-permute-start.12
  47.7 0.8 copy-done.16
  48.4 0.5 collective-permute-start.13
  48.9 4.2 %weight_gradient.8.refs_6_ = bf16[4,512,256]{2,1,0:T(8,128)(2,1)} custom-call(s32[64]{0:T(128)S(1)} %dynamic-slice_bitcast_fusion.row_ref, s32[8]{0:T(128)S(1)} %copy-done.14, bf16[1024,8192]{1,0:T(8,128)(2,1)} %refs_1_.11, bf16[1024,8192]{1,0:T(8,128)(2,1)} %refs_1_.11, bf16[512,1024]{1,0:T(8,128)(2,1)S(1)} %bitcast.6, ...), custom_call_target="tpu_custom_call" | custom-call | flops 1073741824 | bytes 4194304 | tf_op jit(solution)/shard_map/weight_gradient/pallas_call | solution.py:81
  53.2 10.9 %collective-permute-done.12.refs_9_ = bf16[2,256,512]{2,1,0:T(8,128)(2,1)S(1)} collective-permute-done((bf16[2,256,512]{2,1,0:T(8,128)(2,1)}, bf16[2,256,512]{2,1,0:T(8,128)(2,1)S(1)}, u32[]{:S(2)}, u32[]{:S(2)}) %collective-permute-start.12) | collective-permute-done | bytes 524320 | tf_op jit(solution)/shard_map/ppermute | solution.py:275
  64.1 0.8 copy-done.18
  64.9 5.0 %all-to-all-start = ((bf16[32,16,512]{2,1,0:T(8,128)(2,1)}), bf16[32,16,512]{2,1,0:T(8,128)(2,1)}, u32[]{:S(2)}, u32[]{:S(2)}) async-start(bf16[32,16,512]{2,1,0:T(8,128)(2,1)} %pack_moments.1.refs_3_), calls=%async_computation | async-start | bytes 1048576 | tf_op jit(solution)/shard_map/all_to_all | solution.py:414
  69.9 0.2 collective-permute-start.8
  70.1 0.4 collective-permute-start.9
  70.5 0.1 collective-permute-start.3
  70.7 0.4 collective-permute-start.14
  71.0 0.9 copy-done.6
  72.0 3.7 %weight_gradient.9 = (bf16[2,512,256]{2,1,0:T(8,128)(2,1)S(1)}, bf16[2,512,256]{2,1,0:T(8,128)(2,1)S(1)}) custom-call(s32[64]{0:T(128)S(1)} %dynamic-slice_bitcast_fusion.row_ref, s32[8]{0:T(128)S(1)} %copy-done.14, bf16[1024,8192]{1,0:T(8,128)(2,1)} %refs_1_.11, bf16[1024,8192]{1,0:T(8,128)(2,1)} %refs_1_.11, bf16[512,1024]{1,0:T(8,128)(2,1)S(1)} %bitcast.7, ...), custom_call_target="tpu_custom_call" | custom-call | flops 1073741824 | bytes 5242880 | tf_op jit(solution)/shard_map/weight_gradient/pallas_call | solution.py:81
  75.7 0.8 copy-done.3
  76.5 6.6 %weight_gradient.10 = (bf16[4,512,256]{2,1,0:T(8,128)(2,1)}, bf16[4,512,256]{2,1,0:T(8,128)(2,1)S(1)}) custom-call(s32[64]{0:T(128)S(1)} %dynamic-slice_bitcast_fusion.row_ref, s32[8]{0:T(128)S(1)} %copy-done.14, bf16[1024,8192]{1,0:T(8,128)(2,1)} %refs_1_.11, bf16[1024,8192]{1,0:T(8,128)(2,1)} %refs_1_.11, bf16[1024,8192]{1,0:T(8,128)(2,1)} %refs_1_.11, ...), custom_call_target="tpu_custom_call" | custom-call | flops 2147483648 | bytes 9437184 | tf_op jit(solution)/shard_map/weight_gradient/pallas_call | solution.py:81
  83.1 1.5 %collective-permute-start.20 = (bf16[4,512,256]{2,1,0:T(8,128)(2,1)}, bf16[4,512,256]{2,1,0:T(8,128)(2,1)S(1)}, u32[]{:S(2)}, u32[]{:S(2)}) collective-permute-start(bf16[4,512,256]{2,1,0:T(8,128)(2,1)} %get-tuple-element.20.refs_6_), channel_id=1, source_target_pairs={{0,1},{1,0},{2,3},{3,2},{4,5},{5,4},{6,7},{7,6},{8,24},{9,25},{10,... | collective-permute-start | bytes 3145736 | tf_op jit(solution)/shard_map/ppermute | solution.py:275
  84.6 0.6 all-to-all-done.refs_5_.moments_ref
  85.2 3.8 %weight_gradient.11 = (bf16[2,512,256]{2,1,0:T(8,128)(2,1)S(1)}, bf16[2,512,256]{2,1,0:T(8,128)(2,1)S(1)}) custom-call(s32[64]{0:T(128)S(1)} %dynamic-slice_bitcast_fusion.row_ref, s32[8]{0:T(128)S(1)} %copy-done.14, bf16[1024,8192]{1,0:T(8,128)(2,1)} %refs_1_.11, bf16[1024,8192]{1,0:T(8,128)(2,1)} %refs_1_.11, bf16[512,1024]{1,0:T(8,128)(2,1)S(1)} %bitcast.9, ...), custom_call_target="tpu_custom_call" | custom-call | flops 1073741824 | bytes 5242880 | tf_op jit(solution)/shard_map/weight_gradient/pallas_call | solution.py:81
  89.0 0.1 collective-permute-start.16
  89.1 2.0 %collective-permute-start.25 = (bf16[2,512,256]{2,1,0:T(8,128)(2,1)S(1)}, bf16[2,512,256]{2,1,0:T(8,128)(2,1)S(1)}, u32[]{:S(2)}, u32[]{:S(2)}) collective-permute-start(bf16[2,512,256]{2,1,0:T(8,128)(2,1)S(1)} %get-tuple-element.22), channel_id=1, source_target_pairs={{0,1},{1,0},{2,3},{3,2},{4,5},{5,4},{6,7},{7,6},{8,24},{9,25},{10,... | collective-permute-start | bytes 1572872 | tf_op jit(solution)/shard_map/ppermute | solution.py:275
  91.2 17.7 %project.1 = (bf16[1024,512]{1,0:T(8,128)(2,1)}, bf16[256,512]{1,0:T(8,128)(2,1)S(1)}) custom-call(s32[64]{0:T(128)S(1)} %dynamic-slice_bitcast_fusion.row_ref, s32[32]{0:T(128)S(1)} %copy-done.15, s32[8]{0:T(128)S(1)} %copy-done.14, bf16[1024,8192]{1,0:T(8,128)(2,1)} %refs_1_.11, bf16[2,256,512]{2,1,0:T(8,128)(2,1)S(1)} %copy-done.13, ...), custom_call_target="tpu_custom_call" | custom-call | flops 8589934592 | bytes 26214400 | tf_op jit(solution)/shard_map/project/pallas_call | solution.py:171
  108.9 0.1 add_blocks.8
  109.0 0.9 collective-permute-start.21
  109.9 0.1 add_blocks.6
  110.0 1.2 collective-permute-start.17
  111.2 0.1 add_blocks.11
  111.3 0.9 collective-permute-start.26
  112.2 8.8 %collective-permute-done.17.refs_2_ = bf16[1,512,256]{2,1,0:T(8,128)(2,1)S(1)} collective-permute-done((bf16[1,512,256]{2,1,0:T(8,128)(2,1)S(1)}, bf16[1,512,256]{2,1,0:T(8,128)(2,1)S(1)}, u32[]{:S(2)}, u32[]{:S(2)}) %collective-permute-start.17) | collective-permute-done | bytes 262176 | tf_op jit(solution)/shard_map/ppermute | solution.py:275
  121.1 0.1 add_blocks.7
  121.2 1.9 %collective-permute-start.18 = (bf16[1,512,256]{2,1,0:T(8,128)(2,1)S(1)}, bf16[1,512,256]{2,1,0:T(8,128)(2,1)S(1)}, u32[]{:S(2)}, u32[]{:S(2)}) collective-permute-start(bf16[1,512,256]{2,1,0:T(8,128)(2,1)S(1)} %add_blocks.7), channel_id=1, source_target_pairs={{0,4},{1,5},{2,6},{3,7},{4,0},{5,1},{6,2},{7,3},{8,12},{9,13},{10,... | collective-permute-start | bytes 786440 | tf_op jit(solution)/shard_map/ppermute | solution.py:275
  123.1 0.1 add_blocks.9
  123.2 1.0 collective-permute-start.22
  124.2 0.1 add_blocks.10
  124.3 1.1 collective-permute-start.23
  125.4 9.8 %collective-permute-done.18.refs_0_ = bf16[1,512,256]{2,1,0:T(8,128)(2,1)S(1)} collective-permute-done((bf16[1,512,256]{2,1,0:T(8,128)(2,1)S(1)}, bf16[1,512,256]{2,1,0:T(8,128)(2,1)S(1)}, u32[]{:S(2)}, u32[]{:S(2)}) %collective-permute-start.18) | collective-permute-done | bytes 262176 | tf_op jit(solution)/shard_map/ppermute | solution.py:275
  135.2 8.9 %collective-permute-done.22.refs_1_ = bf16[1,512,256]{2,1,0:T(8,128)(2,1)S(1)} collective-permute-done((bf16[1,512,256]{2,1,0:T(8,128)(2,1)S(1)}, bf16[1,512,256]{2,1,0:T(8,128)(2,1)S(1)}, u32[]{:S(2)}, u32[]{:S(2)}) %collective-permute-start.22) | collective-permute-done | bytes 262176 | tf_op jit(solution)/shard_map/ppermute | solution.py:275
  144.1 1.0 collective-permute-done.23.refs_2_
  145.1 2.7 %adam_rows.1 = (bf16[256,512]{1,0:T(8,128)(2,1)}, f32[256,512]{1,0:T(8,128)}, f32[256,512]{1,0:T(8,128)}) custom-call(s32[32]{0:T(128)S(1)} %copy-done.15, bf16[32,16,512]{2,1,0:T(8,128)(2,1)} %all-to-all-done.refs_5_.moments_ref, bf16[256,512]{1,0:T(8,128)(2,1)S(1)} %get-tuple-element.16.refs_2_.weight_ref, ...), custom_call_target="tpu_custom_call" | custom-call | flops 2621440 | bytes 2097152 | tf_op jit(solution)/shard_map/adam_rows/pallas_call | solution.py:233
  (58 shorter events, 0.2 us)
Async XLA Ops:
  0.6 19.9 %collective-permute-start.4 = (bf16[1,256,512]{2,1,0:T(8,128)(2,1)}, bf16[1,256,512]{2,1,0:T(8,128)(2,1)S(1)}, u32[]{:S(2)}, u32[]{:S(2)}) collective-permute-start(bf16[1,256,512]{2,1,0:T(8,128)(2,1)} %bitcast.10), channel_id=1, source_target_pairs={{0,2},{1,3},{2,4},{3,5},{4,6},{5,7},{6,0},{7,1},{8,10},{9,11},{10,... | collective-permute-start | bytes 786440 | tf_op jit(solution)/shard_map/ppermute | solution.py:275
  2.3 18.3 %collective-permute-start.5 = (bf16[1,256,512]{2,1,0:T(8,128)(2,1)}, bf16[1,256,512]{2,1,0:T(8,128)(2,1)S(1)}, u32[]{:S(2)}, u32[]{:S(2)}) collective-permute-start(bf16[1,256,512]{2,1,0:T(8,128)(2,1)} %bitcast.11), channel_id=1, source_target_pairs={{0,6},{1,7},{2,0},{3,1},{4,2},{5,3},{6,4},{7,5},{8,14},{9,15},{10,... | collective-permute-start | bytes 786440 | tf_op jit(solution)/shard_map/ppermute | solution.py:275
  2.7 19.5 %collective-permute-start = (bf16[1,256,512]{2,1,0:T(8,128)(2,1)}, bf16[1,256,512]{2,1,0:T(8,128)(2,1)S(1)}, u32[]{:S(2)}, u32[]{:S(2)}) collective-permute-start(bf16[1,256,512]{2,1,0:T(8,128)(2,1)} %bitcast.12), channel_id=1, source_target_pairs={{0,16},{1,17},{2,18},{3,19},{4,20},{5,21},{6,22},{7,23},{8,9},{9,8... | collective-permute-start | bytes 786440 | tf_op jit(solution)/shard_map/ppermute | solution.py:275
  4.2 32.5 %collective-permute-start.10 = (bf16[1,256,512]{2,1,0:T(8,128)(2,1)}, bf16[1,256,512]{2,1,0:T(8,128)(2,1)}, u32[]{:S(2)}, u32[]{:S(2)}) collective-permute-start(bf16[1,256,512]{2,1,0:T(8,128)(2,1)} %bitcast.13), channel_id=1, source_target_pairs={{0,4},{1,5},{2,6},{3,7},{4,0},{5,1},{6,2},{7,3},{8,12},{9,13},{10,... | collective-permute-start | bytes 786440 | tf_op jit(solution)/shard_map/ppermute | solution.py:275
  6.8 16.1 %copy-start.14 = (s32[8]{0:T(128)S(1)}, s32[8]{0:T(128)}, u32[]{:S(2)}) copy-start(s32[8]{0:T(128)} %new_ref.15) | copy-start | bytes 100
  20.5 2.4 %copy-start.1 = (bf16[1,256,512]{2,1,0:T(8,128)(2,1)}, bf16[1,256,512]{2,1,0:T(8,128)(2,1)S(1)}, u32[]{:S(2)}) copy-start(bf16[1,256,512]{2,1,0:T(8,128)(2,1)S(1)} %collective-permute-done.5.refs_6_) | copy-start | bytes 786436
  20.6 18.3 %collective-permute-start.6 = (bf16[2,256,512]{2,1,0:T(8,128)(2,1)S(1)}, bf16[2,256,512]{2,1,0:T(8,128)(2,1)S(1)}, u32[]{:S(2)}, u32[]{:S(2)}) collective-permute-start(bf16[2,256,512]{2,1,0:T(8,128)(2,1)S(1)} %pad_maximum_fusion.1), channel_id=1, source_target_pairs={{0,16},{1,17},{2,18},{3,19},{4,20},{5,21},{6,22},{7,23},{8,9},{9,8... | collective-permute-start | bytes 1572872 | tf_op jit(solution)/shard_map/ppermute | solution.py:275
  22.2 0.7 copy-start.7
  22.9 1.0 copy-start
  23.9 0.9 copy-start.8
  29.1 0.9 copy-start.2
  30.1 5.0 %copy-start.9 = (bf16[1,256,512]{2,1,0:T(8,128)(2,1)S(1)}, bf16[1,256,512]{2,1,0:T(8,128)(2,1)}, u32[]{:S(2)}) copy-start(bf16[1,256,512]{2,1,0:T(8,128)(2,1)} %copy-done.7) | copy-start | bytes 786436
  30.1 5.0 %copy-start.20 = (bf16[256,512]{1,0:T(8,128)(2,1)S(1)}, bf16[256,512]{1,0:T(8,128)(2,1)}, u32[]{:S(2)}) copy-start(bf16[256,512]{1,0:T(8,128)(2,1)} %param.10) | copy-start | bytes 786436
  35.0 35.7 %collective-permute-start.19 = (bf16[8,512,256]{2,1,0:T(8,128)(2,1)S(1)}, bf16[8,512,256]{2,1,0:T(8,128)(2,1)}, u32[]{:S(2)}, u32[]{:S(2)}) collective-permute-start(bf16[8,512,256]{2,1,0:T(8,128)(2,1)S(1)} %weight_gradient.7.refs_5_), channel_id=1, source_target_pairs={{0,8},{1,9},{2,10},{3,11},{4,12},{5,13},{6,14},{7,15},{8,0},{9,1},... | collective-permute-start | bytes 6291464 | tf_op jit(solution)/shard_map/ppermute | solution.py:275
  35.1 11.0 %copy-start.12 = (bf16[2,256,512]{2,1,0:T(8,128)(2,1)}, bf16[2,256,512]{2,1,0:T(8,128)(2,1)S(1)}, u32[]{:S(2)}) copy-start(bf16[2,256,512]{2,1,0:T(8,128)(2,1)S(1)} %pad_maximum_fusion.refs_0_) | copy-start | bytes 1572868
  35.1 12.5 %collective-permute-start.1 = (bf16[2,256,512]{2,1,0:T(8,128)(2,1)S(1)}, bf16[2,256,512]{2,1,0:T(8,128)(2,1)}, u32[]{:S(2)}, u32[]{:S(2)}) collective-permute-start(bf16[2,256,512]{2,1,0:T(8,128)(2,1)S(1)} %pad_maximum_fusion.refs_0_), channel_id=1, source_target_pairs={{0,1},{1,0},{2,3},{3,2},{4,5},{5,4},{6,7},{7,6},{8,24},{9,25},{10,... | collective-permute-start | bytes 1572872 | tf_op jit(solution)/shard_map/ppermute | solution.py:275
  36.7 10.9 %collective-permute-start.2 = (bf16[2,256,512]{2,1,0:T(8,128)(2,1)S(1)}, bf16[2,256,512]{2,1,0:T(8,128)(2,1)S(1)}, u32[]{:S(2)}, u32[]{:S(2)}) collective-permute-start(bf16[2,256,512]{2,1,0:T(8,128)(2,1)S(1)} %pad_maximum_fusion.refs_0_), channel_id=1, source_target_pairs={{0,8},{1,9},{2,10},{3,11},{4,12},{5,13},{6,14},{7,15},{8,0},{9,1},... | collective-permute-start | bytes 1572872 | tf_op jit(solution)/shard_map/ppermute | solution.py:275
  36.7 9.5 %collective-permute-start.11 = (bf16[1,256,512]{2,1,0:T(8,128)(2,1)}, bf16[1,256,512]{2,1,0:T(8,128)(2,1)S(1)}, u32[]{:S(2)}, u32[]{:S(2)}) collective-permute-start(bf16[1,256,512]{2,1,0:T(8,128)(2,1)} %collective-permute-done.10.refs_4_), channel_id=1, source_target_pairs={{0,16},{1,17},{2,18},{3,19},{4,20},{5,21},{6,22},{7,23},{8,9},{9,8... | collective-permute-start | bytes 786440 | tf_op jit(solution)/shard_map/ppermute | solution.py:275
  39.7 30.4 %collective-permute-start.7 = (bf16[4,256,512]{2,1,0:T(8,128)(2,1)}, bf16[4,256,512]{2,1,0:T(8,128)(2,1)}, u32[]{:S(2)}, u32[]{:S(2)}) collective-permute-start(bf16[4,256,512]{2,1,0:T(8,128)(2,1)} %constant_dynamic-update-slice_fusion.refs_4_), channel_id=1, source_target_pairs={{0,1},{1,0},{2,3},{3,2},{4,5},{5,4},{6,7},{7,6},{8,24},{9,25},{10,... | collective-permute-start | bytes 3145736 | tf_op jit(solution)/shard_map/ppermute | solution.py:275
  46.2 7.0 %copy-start.5 = (bf16[1,256,512]{2,1,0:T(8,128)(2,1)}, bf16[1,256,512]{2,1,0:T(8,128)(2,1)S(1)}, u32[]{:S(2)}) copy-start(bf16[1,256,512]{2,1,0:T(8,128)(2,1)S(1)} %collective-permute-done.11.refs_5_) | copy-start | bytes 786436
  46.9 17.1 %collective-permute-start.12 = (bf16[2,256,512]{2,1,0:T(8,128)(2,1)}, bf16[2,256,512]{2,1,0:T(8,128)(2,1)S(1)}, u32[]{:S(2)}, u32[]{:S(2)}) collective-permute-start(bf16[2,256,512]{2,1,0:T(8,128)(2,1)} %constant_dynamic-update-slice_fusion.3.refs_8_), channel_id=1, source_target_pairs={{0,1},{1,0},{2,3},{3,2},{4,5},{5,4},{6,7},{7,6},{8,24},{9,25},{10,... | collective-permute-start | bytes 1572872 | tf_op jit(solution)/shard_map/ppermute | solution.py:275
  47.6 22.9 %collective-permute-start.15 = (bf16[4,512,256]{2,1,0:T(8,128)(2,1)}, bf16[4,512,256]{2,1,0:T(8,128)(2,1)}, u32[]{:S(2)}, u32[]{:S(2)}) collective-permute-start(bf16[4,512,256]{2,1,0:T(8,128)(2,1)} %weight_gradient.6.refs_7_), channel_id=1, source_target_pairs={{0,8},{1,9},{2,10},{3,11},{4,12},{5,13},{6,14},{7,15},{8,0},{9,1},... | collective-permute-start | bytes 3145736 | tf_op jit(solution)/shard_map/ppermute | solution.py:275
  47.6 0.8 copy-start.16
  48.4 21.5 %collective-permute-start.13 = (bf16[2,256,512]{2,1,0:T(8,128)(2,1)}, bf16[2,256,512]{2,1,0:T(8,128)(2,1)}, u32[]{:S(2)}, u32[]{:S(2)}) collective-permute-start(bf16[2,256,512]{2,1,0:T(8,128)(2,1)} %constant_dynamic-update-slice_fusion.3.refs_8_), channel_id=1, source_target_pairs={{0,8},{1,9},{2,10},{3,11},{4,12},{5,13},{6,14},{7,15},{8,0},{9,1},... | collective-permute-start | bytes 1572872 | tf_op jit(solution)/shard_map/ppermute | solution.py:275
  64.1 0.8 copy-start.18
  64.9 18.2 %collective-permute-start.24 = (bf16[4,512,256]{2,1,0:T(8,128)(2,1)}, bf16[4,512,256]{2,1,0:T(8,128)(2,1)}, u32[]{:S(2)}, u32[]{:S(2)}) collective-permute-start(bf16[4,512,256]{2,1,0:T(8,128)(2,1)} %weight_gradient.8.refs_6_), channel_id=1, source_target_pairs={{0,8},{1,9},{2,10},{3,11},{4,12},{5,13},{6,14},{7,15},{8,0},{9,1},... | collective-permute-start | bytes 3145736 | tf_op jit(solution)/shard_map/ppermute | solution.py:275
  64.9 20.4 %all-to-all-start = ((bf16[32,16,512]{2,1,0:T(8,128)(2,1)}), bf16[32,16,512]{2,1,0:T(8,128)(2,1)}, u32[]{:S(2)}, u32[]{:S(2)}) async-start(bf16[32,16,512]{2,1,0:T(8,128)(2,1)} %pack_moments.1.refs_3_), calls=%async_computation | async-start | bytes 1048576 | tf_op jit(solution)/shard_map/all_to_all | solution.py:414
  69.9 21.2 %collective-permute-start.8 = (bf16[4,256,512]{2,1,0:T(8,128)(2,1)}, bf16[4,256,512]{2,1,0:T(8,128)(2,1)}, u32[]{:S(2)}, u32[]{:S(2)}) collective-permute-start(bf16[4,256,512]{2,1,0:T(8,128)(2,1)} %constant_dynamic-update-slice_fusion.refs_4_), channel_id=1, source_target_pairs={{0,8},{1,9},{2,10},{3,11},{4,12},{5,13},{6,14},{7,15},{8,0},{9,1},... | collective-permute-start | bytes 3145736 | tf_op jit(solution)/shard_map/ppermute | solution.py:275
  70.1 21.0 %collective-permute-start.9 = (bf16[4,256,512]{2,1,0:T(8,128)(2,1)}, bf16[4,256,512]{2,1,0:T(8,128)(2,1)}, u32[]{:S(2)}, u32[]{:S(2)}) collective-permute-start(bf16[4,256,512]{2,1,0:T(8,128)(2,1)} %collective-permute-done.7.refs_5_.refs_4_), channel_id=1, source_target_pairs={{0,8},{1,9},{2,10},{3,11},{4,12},{5,13},{6,14},{7,15},{8,0},{9,1},... | collective-permute-start | bytes 3145736 | tf_op jit(solution)/shard_map/ppermute | solution.py:275
  70.5 18.5 %collective-permute-start.3 = (bf16[2,256,512]{2,1,0:T(8,128)(2,1)}, bf16[2,256,512]{2,1,0:T(8,128)(2,1)}, u32[]{:S(2)}, u32[]{:S(2)}) collective-permute-start(bf16[2,256,512]{2,1,0:T(8,128)(2,1)} %collective-permute-done.1.refs_1_.refs_4_), channel_id=1, source_target_pairs={{0,8},{1,9},{2,10},{3,11},{4,12},{5,13},{6,14},{7,15},{8,0},{9,1},... | collective-permute-start | bytes 1572872 | tf_op jit(solution)/shard_map/ppermute | solution.py:275
  70.7 18.5 %collective-permute-start.14 = (bf16[2,256,512]{2,1,0:T(8,128)(2,1)}, bf16[2,256,512]{2,1,0:T(8,128)(2,1)}, u32[]{:S(2)}, u32[]{:S(2)}) collective-permute-start(bf16[2,256,512]{2,1,0:T(8,128)(2,1)} %copy-done.18), channel_id=1, source_target_pairs={{0,8},{1,9},{2,10},{3,11},{4,12},{5,13},{6,14},{7,15},{8,0},{9,1},... | collective-permute-start | bytes 1572872 | tf_op jit(solution)/shard_map/ppermute | solution.py:275
  71.0 0.9 copy-start.6
  75.7 0.8 copy-start.3
  76.5 6.6 %copy-start.10 = (bf16[2,512,256]{2,1,0:T(8,128)(2,1)}, bf16[2,512,256]{2,1,0:T(8,128)(2,1)S(1)}, u32[]{:S(2)}) copy-start(bf16[2,512,256]{2,1,0:T(8,128)(2,1)S(1)} %get-tuple-element.18.refs_6_) | copy-start | bytes 1572868
  83.1 8.0 %copy-start.15 = (s32[32]{0:T(128)S(1)}, s32[32]{0:T(128)}, u32[]{:S(2)}) copy-start(s32[32]{0:T(128)} %owner_ref.1) | copy-start | bytes 388
  83.1 25.8 %collective-permute-start.20 = (bf16[4,512,256]{2,1,0:T(8,128)(2,1)}, bf16[4,512,256]{2,1,0:T(8,128)(2,1)S(1)}, u32[]{:S(2)}, u32[]{:S(2)}) collective-permute-start(bf16[4,512,256]{2,1,0:T(8,128)(2,1)} %get-tuple-element.20.refs_6_), channel_id=1, source_target_pairs={{0,1},{1,0},{2,3},{3,2},{4,5},{5,4},{6,7},{7,6},{8,24},{9,25},{10,... | collective-permute-start | bytes 3145736 | tf_op jit(solution)/shard_map/ppermute | solution.py:275
  85.2 3.8 %copy-start.11 = (bf16[2,512,256]{2,1,0:T(8,128)(2,1)S(1)}, bf16[2,512,256]{2,1,0:T(8,128)(2,1)}, u32[]{:S(2)}) copy-start(bf16[2,512,256]{2,1,0:T(8,128)(2,1)} %copy-done.10) | copy-start | bytes 1572868
  85.2 5.9 %copy-start.13 = (bf16[2,256,512]{2,1,0:T(8,128)(2,1)S(1)}, bf16[2,256,512]{2,1,0:T(8,128)(2,1)}, u32[]{:S(2)}) copy-start(bf16[2,256,512]{2,1,0:T(8,128)(2,1)} %copy-done.12) | copy-start | bytes 1572868
  85.2 5.9 %copy-start.17 = (bf16[2,256,512]{2,1,0:T(8,128)(2,1)S(1)}, bf16[2,256,512]{2,1,0:T(8,128)(2,1)}, u32[]{:S(2)}) copy-start(bf16[2,256,512]{2,1,0:T(8,128)(2,1)} %copy-done.16) | copy-start | bytes 1572868
  85.2 5.9 %copy-start.19 = (bf16[2,256,512]{2,1,0:T(8,128)(2,1)S(1)}, bf16[2,256,512]{2,1,0:T(8,128)(2,1)}, u32[]{:S(2)}) copy-start(bf16[2,256,512]{2,1,0:T(8,128)(2,1)} %copy-done.18) | copy-start | bytes 1572868
  89.0 20.9 %collective-permute-start.16 = (bf16[2,512,256]{2,1,0:T(8,128)(2,1)S(1)}, bf16[2,512,256]{2,1,0:T(8,128)(2,1)S(1)}, u32[]{:S(2)}, u32[]{:S(2)}) collective-permute-start(bf16[2,512,256]{2,1,0:T(8,128)(2,1)S(1)} %copy-done.11), channel_id=1, source_target_pairs={{0,1},{1,0},{2,3},{3,2},{4,5},{5,4},{6,7},{7,6},{8,24},{9,25},{10,... | collective-permute-start | bytes 1572872 | tf_op jit(solution)/shard_map/ppermute | solution.py:275
  89.1 22.1 %collective-permute-start.25 = (bf16[2,512,256]{2,1,0:T(8,128)(2,1)S(1)}, bf16[2,512,256]{2,1,0:T(8,128)(2,1)S(1)}, u32[]{:S(2)}, u32[]{:S(2)}) collective-permute-start(bf16[2,512,256]{2,1,0:T(8,128)(2,1)S(1)} %get-tuple-element.22), channel_id=1, source_target_pairs={{0,1},{1,0},{2,3},{3,2},{4,5},{5,4},{6,7},{7,6},{8,24},{9,25},{10,... | collective-permute-start | bytes 1572872 | tf_op jit(solution)/shard_map/ppermute | solution.py:275
  108.9 1.1 copy-start.4
  109.0 14.1 %collective-permute-start.21 = (bf16[2,512,256]{2,1,0:T(8,128)(2,1)S(1)}, bf16[2,512,256]{2,1,0:T(8,128)(2,1)S(1)}, u32[]{:S(2)}, u32[]{:S(2)}) collective-permute-start(bf16[2,512,256]{2,1,0:T(8,128)(2,1)S(1)} %add_blocks.8), channel_id=1, source_target_pairs={{0,16},{1,17},{2,18},{3,19},{4,20},{5,21},{6,22},{7,23},{8,9},{9,8... | collective-permute-start | bytes 1572872 | tf_op jit(solution)/shard_map/ppermute | solution.py:275
  110.0 11.0 %collective-permute-start.17 = (bf16[1,512,256]{2,1,0:T(8,128)(2,1)S(1)}, bf16[1,512,256]{2,1,0:T(8,128)(2,1)S(1)}, u32[]{:S(2)}, u32[]{:S(2)}) collective-permute-start(bf16[1,512,256]{2,1,0:T(8,128)(2,1)S(1)} %add_blocks.6), channel_id=1, source_target_pairs={{0,16},{1,17},{2,18},{3,19},{4,20},{5,21},{6,22},{7,23},{8,9},{9,8... | collective-permute-start | bytes 786440 | tf_op jit(solution)/shard_map/ppermute | solution.py:275
  111.3 14.1 %collective-permute-start.26 = (bf16[1,512,256]{2,1,0:T(8,128)(2,1)S(1)}, bf16[1,512,256]{2,1,0:T(8,128)(2,1)S(1)}, u32[]{:S(2)}, u32[]{:S(2)}) collective-permute-start(bf16[1,512,256]{2,1,0:T(8,128)(2,1)S(1)} %add_blocks.11), channel_id=1, source_target_pairs={{0,16},{1,17},{2,18},{3,19},{4,20},{5,21},{6,22},{7,23},{8,9},{9,8... | collective-permute-start | bytes 786440 | tf_op jit(solution)/shard_map/ppermute | solution.py:275
  121.2 14.1 %collective-permute-start.18 = (bf16[1,512,256]{2,1,0:T(8,128)(2,1)S(1)}, bf16[1,512,256]{2,1,0:T(8,128)(2,1)S(1)}, u32[]{:S(2)}, u32[]{:S(2)}) collective-permute-start(bf16[1,512,256]{2,1,0:T(8,128)(2,1)S(1)} %add_blocks.7), channel_id=1, source_target_pairs={{0,4},{1,5},{2,6},{3,7},{4,0},{5,1},{6,2},{7,3},{8,12},{9,13},{10,... | collective-permute-start | bytes 786440 | tf_op jit(solution)/shard_map/ppermute | solution.py:275
  123.2 20.9 %collective-permute-start.22 = (bf16[1,512,256]{2,1,0:T(8,128)(2,1)S(1)}, bf16[1,512,256]{2,1,0:T(8,128)(2,1)S(1)}, u32[]{:S(2)}, u32[]{:S(2)}) collective-permute-start(bf16[1,512,256]{2,1,0:T(8,128)(2,1)S(1)} %add_blocks.9), channel_id=1, source_target_pairs={{0,2},{1,3},{2,4},{3,5},{4,6},{5,7},{6,0},{7,1},{8,10},{9,11},{10,... | collective-permute-start | bytes 786440 | tf_op jit(solution)/shard_map/ppermute | solution.py:275
  124.3 20.8 %collective-permute-start.23 = (bf16[1,512,256]{2,1,0:T(8,128)(2,1)S(1)}, bf16[1,512,256]{2,1,0:T(8,128)(2,1)S(1)}, u32[]{:S(2)}, u32[]{:S(2)}) collective-permute-start(bf16[1,512,256]{2,1,0:T(8,128)(2,1)S(1)} %add_blocks.10), channel_id=1, source_target_pairs={{0,6},{1,7},{2,0},{3,1},{4,2},{5,3},{6,4},{7,5},{8,14},{9,15},{10,... | collective-permute-start | bytes 786440 | tf_op jit(solution)/shard_map/ppermute | solution.py:275

commit v6 on v4

--- a/solution.py
+++ b/solution.py
@@ -34,8 +34,11 @@
     out_refs = refs[adds:]
 
     def write(out_ref):
-        for slot, token_ref in enumerate(token_refs):
-            block = jnp.dot(turned_ref[...], token_ref[...], preferred_element_type=jnp.float32)
+        wide = jnp.concatenate([token_ref[...] for token_ref in token_refs], axis=1)
+        blocks = jnp.dot(turned_ref[...], wide, preferred_element_type=jnp.float32)
+        row_block = out_ref.shape[2]
+        for slot in range(per_step):
+            block = blocks[:, slot * row_block : (slot + 1) * row_block]
             if adds:
                 block = block + refs[0][slot].astype(jnp.float32)
             out_ref[slot] = block.astype(out_ref.dtype)

time: 133 us -> 133 us (level)
  no operation moved by 1% of the time
where the time goes in v6:
time: 133 us
  waiting for transfers between devices  48.4 us (36%)
  Pallas kernels  45.2 us (34%)
  starting transfers between devices  26.7 us (20%)
  other arithmetic  6.09 us (5%)
  local copies, waits for them, and re-layouts  5.33 us (4%)
    ppermute x27, waiting for transfers between devices, send(): return lax.ppermute(value, AXES, pairs)  48.4 us
    pallas_call x6, Pallas kernels, grad_blocks(): pl.pallas_call(functools.partial(grad_kernel, per_step, len(added)), grid...  23.9 us
    ppermute x27, starting transfers between devices, send(): return lax.ppermute(value, AXES, pairs)  21.9 us
    pallas_call x1, Pallas kernels, project(): pl.pallas_call(functools.partial(project_kernel, devices // new_owner.sha...  16.9 us
    convert_element_type x5, other arithmetic, rounded_sum(): return total.astype(terms[0].dtype)  5.99 us
    all_to_all x1, starting transfers between devices, body(): lax.all_to_all(packed, AXES, split_axis=0, concat_axis=0, tiled=True)  4.72 us
    unnamed x34, local copies, waits for them, and re-layouts  3.78 us
  transfers between devices with their start and end apart: 28, of which 10 were waited for; matrix products, arithmetic and copies ran while one was open for 6% of the time, Pallas kernels for 29%

profile of v6, /device:TPU:8, one launch (start us, length us, event | category | flops | bytes accessed | tf_op | source)
XLA Modules:
  0.0 132.5 jit_solution(12683676659299838784)
XLA Ops:
  0.6 0.0 copy-start.3
  0.6 1.5 %copy.12 = bf16[1024,512]{0,1:T(8,128)(2,1)S(1)} copy(bf16[1024,512]{1,0:T(8,128)(2,1)} %param.9) | data formatting | bytes 2097152 | tf_op args[1]
  2.1 0.7 dynamic-slice_bitcast_fusion.row_ref
  2.8 4.9 %weight_gradient.8 = bf16[8,512,256]{2,1,0:T(8,128)(2,1)S(1)} custom-call(s32[64]{0:T(128)S(1)} %dynamic-slice_bitcast_fusion.row_ref, s32[8]{0:T(128)S(1)} %copy-done.3, bf16[1024,8192]{1,0:T(8,128)(2,1)} %refs_1_.11, bf16[1024,8192]{1,0:T(8,128)(2,1)} %refs_1_.11, bf16[1024,8192]{1,0:T(8,128)(2,1)} %refs_1_.11, bf16[1024,8192]{1,0:T(8,128)(2,1)} %refs_1_.11, ...), custom_call_target="tpu_custom_call" | custom-call | flops 2147483648 | bytes 7340032 | tf_op jit(solution)/shard_map/weight_gradient/pallas_call | solution.py:82
  7.7 0.1 collective-permute-start.19
  7.8 1.6 %collective-permute-start.4 = (bf16[1,256,512]{2,1,0:T(8,128)(2,1)S(1)}, bf16[1,256,512]{2,1,0:T(8,128)(2,1)S(1)}, u32[]{:S(2)}, u32[]{:S(2)}) collective-permute-start(bf16[1,256,512]{2,1,0:T(8,128)(2,1)S(1)} %bitcast.10), channel_id=1, source_target_pairs={{0,2},{1,3},{2,4},{3,5},{4,6},{5,7},{6,0},{7,1},{8,10},{9,11},{10,... | collective-permute-start | bytes 786440 | tf_op jit(solution)/shard_map/ppermute | solution.py:281
  9.4 0.5 collective-permute-start.5
  9.9 3.3 %weight_gradient.6 = bf16[4,512,256]{2,1,0:T(8,128)(2,1)S(1)} custom-call(s32[64]{0:T(128)S(1)} %dynamic-slice_bitcast_fusion.row_ref, s32[8]{0:T(128)S(1)} %copy-done.3, bf16[1024,8192]{1,0:T(8,128)(2,1)} %refs_1_.11, bf16[1024,8192]{1,0:T(8,128)(2,1)} %refs_1_.11, bf16[512,1024]{1,0:T(8,128)(2,1)S(1)} %bitcast.5), custom_call_target="tpu_custom_call" | custom-call | flops 1073741824 | bytes 4194304 | tf_op jit(solution)/shard_map/weight_gradient/pallas_call | solution.py:82
  13.2 0.1 collective-permute-start.15
  13.3 3.7 %collective-permute-done.4 = bf16[1,256,512]{2,1,0:T(8,128)(2,1)S(1)} collective-permute-done((bf16[1,256,512]{2,1,0:T(8,128)(2,1)S(1)}, bf16[1,256,512]{2,1,0:T(8,128)(2,1)S(1)}, u32[]{:S(2)}, u32[]{:S(2)}) %collective-permute-start.4) | collective-permute-done | bytes 262176 | tf_op jit(solution)/shard_map/ppermute | solution.py:281
  17.0 6.0 %collective-permute-done.5 = bf16[1,256,512]{2,1,0:T(8,128)(2,1)S(1)} collective-permute-done((bf16[1,256,512]{2,1,0:T(8,128)(2,1)S(1)}, bf16[1,256,512]{2,1,0:T(8,128)(2,1)S(1)}, u32[]{:S(2)}, u32[]{:S(2)}) %collective-permute-start.5) | collective-permute-done | bytes 262176 | tf_op jit(solution)/shard_map/ppermute | solution.py:281
  23.0 0.1 pad_maximum_fusion.1
  23.0 1.6 %collective-permute-start.6 = (bf16[2,256,512]{2,1,0:T(8,128)(2,1)S(1)}, bf16[2,256,512]{2,1,0:T(8,128)(2,1)S(1)}, u32[]{:S(2)}, u32[]{:S(2)}) collective-permute-start(bf16[2,256,512]{2,1,0:T(8,128)(2,1)S(1)} %pad_maximum_fusion.1), channel_id=1, source_target_pairs={{0,16},{1,17},{2,18},{3,19},{4,20},{5,21},{6,22},{7,23},{8,9},{9,8... | collective-permute-start | bytes 1572872 | tf_op jit(solution)/shard_map/ppermute | solution.py:281
  24.6 3.3 %weight_gradient.10 = bf16[4,512,256]{2,1,0:T(8,128)(2,1)S(1)} custom-call(s32[64]{0:T(128)S(1)} %dynamic-slice_bitcast_fusion.row_ref, s32[8]{0:T(128)S(1)} %copy-done.3, bf16[1024,8192]{1,0:T(8,128)(2,1)} %refs_1_.11, bf16[1024,8192]{1,0:T(8,128)(2,1)} %refs_1_.11, bf16[512,1024]{1,0:T(8,128)(2,1)S(1)} %bitcast.6), custom_call_target="tpu_custom_call" | custom-call | flops 1073741824 | bytes 4194304 | tf_op jit(solution)/shard_map/weight_gradient/pallas_call | solution.py:82
  28.0 0.1 collective-permute-start.24
  28.0 1.2 collective-permute-start
  29.3 4.9 %weight_gradient.9 = (bf16[4,512,256]{2,1,0:T(8,128)(2,1)S(1)}, bf16[4,512,256]{2,1,0:T(8,128)(2,1)S(1)}) custom-call(s32[64]{0:T(128)S(1)} %dynamic-slice_bitcast_fusion.row_ref, s32[8]{0:T(128)S(1)} %copy-done.3, bf16[1024,8192]{1,0:T(8,128)(2,1)} %refs_1_.11, bf16[1024,8192]{1,0:T(8,128)(2,1)} %refs_1_.11, bf16[1024,8192]{1,0:T(8,128)(2,1)} %refs_1_.11, ...), custom_call_target="tpu_custom_call" | custom-call | flops 2147483648 | bytes 9437184 | tf_op jit(solution)/shard_map/weight_gradient/pallas_call | solution.py:82
  34.2 0.9 collective-permute-start.20
  35.1 0.7 constant_dynamic-update-slice_fusion.2
  35.8 0.0 collective-permute-done.6
  35.8 1.7 %collective-permute-start.10 = (bf16[1,256,512]{2,1,0:T(8,128)(2,1)S(1)}, bf16[1,256,512]{2,1,0:T(8,128)(2,1)S(1)}, u32[]{:S(2)}, u32[]{:S(2)}) collective-permute-start(bf16[1,256,512]{2,1,0:T(8,128)(2,1)S(1)} %bitcast.13), channel_id=1, source_target_pairs={{0,4},{1,5},{2,6},{3,7},{4,0},{5,1},{6,2},{7,3},{8,12},{9,13},{10,... | collective-permute-start | bytes 786440 | tf_op jit(solution)/shard_map/ppermute | solution.py:281
  37.5 0.7 constant_dynamic-update-slice_fusion.1
  38.2 0.8 constant_dynamic-update-slice_fusion.refs_4_
  39.1 0.0 collective-permute-done
  39.1 0.6 collective-permute-start.7
  39.7 8.9 %collective-permute-done.10 = bf16[1,256,512]{2,1,0:T(8,128)(2,1)S(1)} collective-permute-done((bf16[1,256,512]{2,1,0:T(8,128)(2,1)S(1)}, bf16[1,256,512]{2,1,0:T(8,128)(2,1)S(1)}, u32[]{:S(2)}, u32[]{:S(2)}) %collective-permute-start.10) | collective-permute-done | bytes 262176 | tf_op jit(solution)/shard_map/ppermute | solution.py:281
  48.6 1.5 %collective-permute-start.11 = (bf16[1,256,512]{2,1,0:T(8,128)(2,1)S(1)}, bf16[1,256,512]{2,1,0:T(8,128)(2,1)S(1)}, u32[]{:S(2)}, u32[]{:S(2)}) collective-permute-start(bf16[1,256,512]{2,1,0:T(8,128)(2,1)S(1)} %collective-permute-done.10), channel_id=1, source_target_pairs={{0,16},{1,17},{2,18},{3,19},{4,20},{5,21},{6,22},{7,23},{8,9},{9,8... | collective-permute-start | bytes 786440 | tf_op jit(solution)/shard_map/ppermute | solution.py:281
  50.2 0.1 pad_maximum_fusion.refs_0_
  50.2 0.6 collective-permute-start.1
  50.8 3.3 %weight_gradient.7 = (bf16[2,512,256]{2,1,0:T(8,128)(2,1)S(1)}, bf16[2,512,256]{2,1,0:T(8,128)(2,1)S(1)}) custom-call(s32[64]{0:T(128)S(1)} %dynamic-slice_bitcast_fusion.row_ref, s32[8]{0:T(128)S(1)} %copy-done.3, bf16[1024,8192]{1,0:T(8,128)(2,1)} %refs_1_.11, bf16[1024,8192]{1,0:T(8,128)(2,1)} %refs_1_.11, bf16[512,1024]{1,0:T(8,128)(2,1)S(1)} %bitcast.8, ...), custom_call_target="tpu_custom_call" | custom-call | flops 1073741824 | bytes 5242880 | tf_op jit(solution)/shard_map/weight_gradient/pallas_call | solution.py:82
  54.2 3.7 %collective-permute-done.11 = bf16[1,256,512]{2,1,0:T(8,128)(2,1)S(1)} collective-permute-done((bf16[1,256,512]{2,1,0:T(8,128)(2,1)S(1)}, bf16[1,256,512]{2,1,0:T(8,128)(2,1)S(1)}, u32[]{:S(2)}, u32[]{:S(2)}) %collective-permute-start.11) | collective-permute-done | bytes 262176 | tf_op jit(solution)/shard_map/ppermute | solution.py:281
  57.9 0.5 collective-permute-start.16
  58.5 4.1 %weight_gradient.11 = (bf16[2,512,256]{2,1,0:T(8,128)(2,1)}, bf16[2,512,256]{2,1,0:T(8,128)(2,1)S(1)}) custom-call(s32[64]{0:T(128)S(1)} %dynamic-slice_bitcast_fusion.row_ref, s32[8]{0:T(128)S(1)} %copy-done.3, bf16[1024,8192]{1,0:T(8,128)(2,1)} %refs_1_.11, bf16[1024,8192]{1,0:T(8,128)(2,1)} %refs_1_.11, bf16[512,1024]{1,0:T(8,128)(2,1)S(1)} %bitcast.9, ...), custom_call_target="tpu_custom_call" | custom-call | flops 1073741824 | bytes 5242880 | tf_op jit(solution)/shard_map/weight_gradient/pallas_call | solution.py:82
  62.6 6.1 %collective-permute-done.1.refs_1_ = bf16[2,256,512]{2,1,0:T(8,128)(2,1)S(1)} collective-permute-done((bf16[2,256,512]{2,1,0:T(8,128)(2,1)S(1)}, bf16[2,256,512]{2,1,0:T(8,128)(2,1)S(1)}, u32[]{:S(2)}, u32[]{:S(2)}) %collective-permute-start.1) | collective-permute-done | bytes 524320 | tf_op jit(solution)/shard_map/ppermute | solution.py:281
  68.7 0.8 collective-permute-start.12
  69.5 1.2 collective-permute-start.25
  70.7 1.0 add_convert_fusion
  71.7 0.9 collective-permute-start.21
  72.6 2.4 %collective-permute-done.16 = bf16[2,512,256]{2,1,0:T(8,128)(2,1)S(1)} collective-permute-done((bf16[2,512,256]{2,1,0:T(8,128)(2,1)S(1)}, bf16[2,512,256]{2,1,0:T(8,128)(2,1)S(1)}, u32[]{:S(2)}, u32[]{:S(2)}) %collective-permute-start.16) | collective-permute-done | bytes 524320 | tf_op jit(solution)/shard_map/ppermute | solution.py:281
  75.0 0.5 collective-permute-start.9
  75.5 0.1 add_convert_fusion.5
  75.5 10.0 %collective-permute-done.12.refs_9_ = bf16[2,256,512]{2,1,0:T(8,128)(2,1)S(1)} collective-permute-done((bf16[2,256,512]{2,1,0:T(8,128)(2,1)S(1)}, bf16[2,256,512]{2,1,0:T(8,128)(2,1)S(1)}, u32[]{:S(2)}, u32[]{:S(2)}) %collective-permute-start.12) | collective-permute-done | bytes 524320 | tf_op jit(solution)/shard_map/ppermute | solution.py:281
  85.6 0.8 copy-done.10
  86.3 0.9 collective-permute-start.17
  87.2 2.1 %pack_moments.1 = bf16[32,16,512]{2,1,0:T(8,128)(2,1)} custom-call(s32[8]{0:T(128)} %new_ref.15, f32[256,512]{1,0:T(8,128)} %first_ref.1, f32[256,512]{1,0:T(8,128)} %second_ref.1), custom_call_target="tpu_custom_call" | custom-call | bytes 1572864 | tf_op jit(solution)/shard_map/pack_moments/pallas_call | solution.py:113
  89.3 4.7 %all-to-all-start = ((bf16[32,16,512]{2,1,0:T(8,128)(2,1)}), bf16[32,16,512]{2,1,0:T(8,128)(2,1)S(1)}, u32[]{:S(2)}, u32[]{:S(2)}) async-start(bf16[32,16,512]{2,1,0:T(8,128)(2,1)} %pack_moments.1), calls=%async_computation | async-start | bytes 1048576 | tf_op jit(solution)/shard_map/all_to_all | solution.py:387
  94.0 0.0 copy-start.4
  94.1 0.0 copy-start.5
  94.1 0.0 copy-start.7
  94.1 0.0 copy-start.9
  94.1 0.2 collective-permute-start.13
  94.3 0.4 collective-permute-start.3
  94.7 0.1 collective-permute-start.14
  94.8 0.8 add_convert_fusion.1
  95.6 1.9 %add_convert_fusion.4 = bf16[1,512,256]{2,1,0:T(8,128)(2,1)} fusion(bf16[1,512,256]{2,1,0:T(8,128)(2,1)} %collective-permute-done.17, bf16[2,512,256]{2,1,0:T(8,128)(2,1)} %copy-done.13, bf16[2,512,256]{2,1,0:T(8,128)(2,1)} %copy-done), kind=kLoop, calls=%fused_computation.6 | loop fusion | flops 786432 | bytes 1048576 | tf_op jit(solution)/shard_map/convert_element_type | solution.py:288
  97.5 2.2 %add_convert_fusion.2 = (bf16[1,512,256]{2,1,0:T(8,128)(2,1)}, bf16[1,512,256]{2,1,0:T(8,128)(2,1)}) fusion(bf16[2,512,256]{2,1,0:T(8,128)(2,1)} %collective-permute-done.21, bf16[4,512,256]{2,1,0:T(8,128)(2,1)} %copy-done.12, bf16[4,512,256]{2,1,0:T(8,128)(2,1)S(1)} %get-tuple-element.19), kind=kLoop, calls=%fused_computation.4 | loop fusion | flops 1572864 | bytes 2097152 | tf_op jit(solution)/shard_map/convert_element_type | solution.py:288
  99.8 1.5 %collective-permute-start.26 = (bf16[1,512,256]{2,1,0:T(8,128)(2,1)}, bf16[1,512,256]{2,1,0:T(8,128)(2,1)S(1)}, u32[]{:S(2)}, u32[]{:S(2)}) collective-permute-start(bf16[1,512,256]{2,1,0:T(8,128)(2,1)} %add_convert_fusion.1), channel_id=1, source_target_pairs={{0,16},{1,17},{2,18},{3,19},{4,20},{5,21},{6,22},{7,23},{8,9},{9,8... | collective-permute-start | bytes 786440 | tf_op jit(solution)/shard_map/ppermute | solution.py:281
  101.2 2.4 %collective-permute-start.18 = (bf16[1,512,256]{2,1,0:T(8,128)(2,1)}, bf16[1,512,256]{2,1,0:T(8,128)(2,1)S(1)}, u32[]{:S(2)}, u32[]{:S(2)}) collective-permute-start(bf16[1,512,256]{2,1,0:T(8,128)(2,1)} %add_convert_fusion.4), channel_id=1, source_target_pairs={{0,4},{1,5},{2,6},{3,7},{4,0},{5,1},{6,2},{7,3},{8,12},{9,13},{10,... | collective-permute-start | bytes 786440 | tf_op jit(solution)/shard_map/ppermute | solution.py:281
  103.7 2.0 %collective-permute-start.23 = (bf16[1,512,256]{2,1,0:T(8,128)(2,1)}, bf16[1,512,256]{2,1,0:T(8,128)(2,1)S(1)}, u32[]{:S(2)}, u32[]{:S(2)}) collective-permute-start(bf16[1,512,256]{2,1,0:T(8,128)(2,1)} %get-tuple-element.26), channel_id=1, source_target_pairs={{0,6},{1,7},{2,0},{3,1},{4,2},{5,3},{6,4},{7,5},{8,14},{9,15},{10,... | collective-permute-start | bytes 786440 | tf_op jit(solution)/shard_map/ppermute | solution.py:281
  105.8 16.9 %project.1 = (bf16[1024,512]{1,0:T(8,128)(2,1)}, bf16[256,512]{1,0:T(8,128)(2,1)S(1)}) custom-call(s32[64]{0:T(128)S(1)} %dynamic-slice_bitcast_fusion.row_ref, s32[32]{0:T(128)S(1)} %copy-done.5, s32[8]{0:T(128)S(1)} %copy-done.4, bf16[1024,8192]{1,0:T(8,128)(2,1)} %refs_1_.11, bf16[2,256,512]{2,1,0:T(8,128)(2,1)S(1)} %pad_maximum_fusion.refs_0_, ...), custom_call_target="tpu_custom_call" | custom-call | flops 8589934592 | bytes 26214400 | tf_op jit(solution)/shard_map/project/pallas_call | solution.py:172
  122.8 0.2 collective-permute-done.18.refs_0_
  122.9 5.4 %collective-permute-done.22.refs_1_ = bf16[1,512,256]{2,1,0:T(8,128)(2,1)S(1)} collective-permute-done((bf16[1,512,256]{2,1,0:T(8,128)(2,1)}, bf16[1,512,256]{2,1,0:T(8,128)(2,1)S(1)}, u32[]{:S(2)}, u32[]{:S(2)}) %collective-permute-start.22) | collective-permute-done | bytes 262176 | tf_op jit(solution)/shard_map/ppermute | solution.py:281
  128.3 2.0 %collective-permute-done.23.refs_2_ = bf16[1,512,256]{2,1,0:T(8,128)(2,1)S(1)} collective-permute-done((bf16[1,512,256]{2,1,0:T(8,128)(2,1)}, bf16[1,512,256]{2,1,0:T(8,128)(2,1)S(1)}, u32[]{:S(2)}, u32[]{:S(2)}) %collective-permute-start.23) | collective-permute-done | bytes 262176 | tf_op jit(solution)/shard_map/ppermute | solution.py:281
  130.3 2.2 %adam_rows.1 = (bf16[256,512]{1,0:T(8,128)(2,1)}, f32[256,512]{1,0:T(8,128)}, f32[256,512]{1,0:T(8,128)}) custom-call(s32[32]{0:T(128)S(1)} %copy-done.5, bf16[32,16,512]{2,1,0:T(8,128)(2,1)S(1)} %all-to-all-done.moments_ref, bf16[256,512]{1,0:T(8,128)(2,1)S(1)} %get-tuple-element.16.weight_ref, bf16[1,512,256]{2,1,0:T(8,128)(2,1)S(1)} %collective-permute-done.18.refs_0_, ...), custom_call_target="tpu_custom_call" | custom-call | flops 2621440 | bytes 2097152 | tf_op jit(solution)/shard_map/adam_rows/pallas_call | solution.py:234
  (45 shorter events, 0.1 us)
Async XLA Ops:
  0.6 2.2 %copy-start.3 = (s32[8]{0:T(128)S(1)}, s32[8]{0:T(128)}, u32[]{:S(2)}) copy-start(s32[8]{0:T(128)} %new_ref.15) | copy-start | bytes 100
  2.8 5.0 %copy-start.14 = (bf16[256,512]{1,0:T(8,128)(2,1)S(1)}, bf16[256,512]{1,0:T(8,128)(2,1)}, u32[]{:S(2)}) copy-start(bf16[256,512]{1,0:T(8,128)(2,1)} %param.10) | copy-start | bytes 786436
  7.7 21.6 %collective-permute-start.19 = (bf16[8,512,256]{2,1,0:T(8,128)(2,1)S(1)}, bf16[8,512,256]{2,1,0:T(8,128)(2,1)S(1)}, u32[]{:S(2)}, u32[]{:S(2)}) collective-permute-start(bf16[8,512,256]{2,1,0:T(8,128)(2,1)S(1)} %weight_gradient.8), channel_id=1, source_target_pairs={{0,8},{1,9},{2,10},{3,11},{4,12},{5,13},{6,14},{7,15},{8,0},{9,1},... | collective-permute-start | bytes 6291464 | tf_op jit(solution)/shard_map/ppermute | solution.py:281
  7.8 9.2 %collective-permute-start.4 = (bf16[1,256,512]{2,1,0:T(8,128)(2,1)S(1)}, bf16[1,256,512]{2,1,0:T(8,128)(2,1)S(1)}, u32[]{:S(2)}, u32[]{:S(2)}) collective-permute-start(bf16[1,256,512]{2,1,0:T(8,128)(2,1)S(1)} %bitcast.10), channel_id=1, source_target_pairs={{0,2},{1,3},{2,4},{3,5},{4,6},{5,7},{6,0},{7,1},{8,10},{9,11},{10,... | collective-permute-start | bytes 786440 | tf_op jit(solution)/shard_map/ppermute | solution.py:281
  9.4 13.5 %collective-permute-start.5 = (bf16[1,256,512]{2,1,0:T(8,128)(2,1)S(1)}, bf16[1,256,512]{2,1,0:T(8,128)(2,1)S(1)}, u32[]{:S(2)}, u32[]{:S(2)}) collective-permute-start(bf16[1,256,512]{2,1,0:T(8,128)(2,1)S(1)} %bitcast.11), channel_id=1, source_target_pairs={{0,6},{1,7},{2,0},{3,1},{4,2},{5,3},{6,4},{7,5},{8,14},{9,15},{10,... | collective-permute-start | bytes 786440 | tf_op jit(solution)/shard_map/ppermute | solution.py:281
  13.2 37.0 %collective-permute-start.15 = (bf16[4,512,256]{2,1,0:T(8,128)(2,1)S(1)}, bf16[4,512,256]{2,1,0:T(8,128)(2,1)S(1)}, u32[]{:S(2)}, u32[]{:S(2)}) collective-permute-start(bf16[4,512,256]{2,1,0:T(8,128)(2,1)S(1)} %weight_gradient.6), channel_id=1, source_target_pairs={{0,8},{1,9},{2,10},{3,11},{4,12},{5,13},{6,14},{7,15},{8,0},{9,1},... | collective-permute-start | bytes 3145736 | tf_op jit(solution)/shard_map/ppermute | solution.py:281
  23.0 12.8 %collective-permute-start.6 = (bf16[2,256,512]{2,1,0:T(8,128)(2,1)S(1)}, bf16[2,256,512]{2,1,0:T(8,128)(2,1)S(1)}, u32[]{:S(2)}, u32[]{:S(2)}) collective-permute-start(bf16[2,256,512]{2,1,0:T(8,128)(2,1)S(1)} %pad_maximum_fusion.1), channel_id=1, source_target_pairs={{0,16},{1,17},{2,18},{3,19},{4,20},{5,21},{6,22},{7,23},{8,9},{9,8... | collective-permute-start | bytes 1572872 | tf_op jit(solution)/shard_map/ppermute | solution.py:281
  28.0 29.9 %collective-permute-start.24 = (bf16[4,512,256]{2,1,0:T(8,128)(2,1)S(1)}, bf16[4,512,256]{2,1,0:T(8,128)(2,1)S(1)}, u32[]{:S(2)}, u32[]{:S(2)}) collective-permute-start(bf16[4,512,256]{2,1,0:T(8,128)(2,1)S(1)} %weight_gradient.10), channel_id=1, source_target_pairs={{0,8},{1,9},{2,10},{3,11},{4,12},{5,13},{6,14},{7,15},{8,0},{9,1},... | collective-permute-start | bytes 3145736 | tf_op jit(solution)/shard_map/ppermute | solution.py:281
  28.0 11.0 %collective-permute-start = (bf16[1,256,512]{2,1,0:T(8,128)(2,1)S(1)}, bf16[1,256,512]{2,1,0:T(8,128)(2,1)S(1)}, u32[]{:S(2)}, u32[]{:S(2)}) collective-permute-start(bf16[1,256,512]{2,1,0:T(8,128)(2,1)S(1)} %bitcast.12), channel_id=1, source_target_pairs={{0,16},{1,17},{2,18},{3,19},{4,20},{5,21},{6,22},{7,23},{8,9},{9,8... | collective-permute-start | bytes 786440 | tf_op jit(solution)/shard_map/ppermute | solution.py:281
  34.2 35.4 %collective-permute-start.20 = (bf16[4,512,256]{2,1,0:T(8,128)(2,1)S(1)}, bf16[4,512,256]{2,1,0:T(8,128)(2,1)S(1)}, u32[]{:S(2)}, u32[]{:S(2)}) collective-permute-start(bf16[4,512,256]{2,1,0:T(8,128)(2,1)S(1)} %get-tuple-element.20), channel_id=1, source_target_pairs={{0,1},{1,0},{2,3},{3,2},{4,5},{5,4},{6,7},{7,6},{8,24},{9,25},{10,... | collective-permute-start | bytes 3145736 | tf_op jit(solution)/shard_map/ppermute | solution.py:281
  35.8 12.9 %collective-permute-start.10 = (bf16[1,256,512]{2,1,0:T(8,128)(2,1)S(1)}, bf16[1,256,512]{2,1,0:T(8,128)(2,1)S(1)}, u32[]{:S(2)}, u32[]{:S(2)}) collective-permute-start(bf16[1,256,512]{2,1,0:T(8,128)(2,1)S(1)} %bitcast.13), channel_id=1, source_target_pairs={{0,4},{1,5},{2,6},{3,7},{4,0},{5,1},{6,2},{7,3},{8,12},{9,13},{10,... | collective-permute-start | bytes 786440 | tf_op jit(solution)/shard_map/ppermute | solution.py:281
  39.1 35.9 %collective-permute-start.7 = (bf16[4,256,512]{2,1,0:T(8,128)(2,1)}, bf16[4,256,512]{2,1,0:T(8,128)(2,1)}, u32[]{:S(2)}, u32[]{:S(2)}) collective-permute-start(bf16[4,256,512]{2,1,0:T(8,128)(2,1)} %constant_dynamic-update-slice_fusion.refs_4_), channel_id=1, source_target_pairs={{0,1},{1,0},{2,3},{3,2},{4,5},{5,4},{6,7},{7,6},{8,24},{9,25},{10,... | collective-permute-start | bytes 3145736 | tf_op jit(solution)/shard_map/ppermute | solution.py:281
  48.6 9.2 %collective-permute-start.11 = (bf16[1,256,512]{2,1,0:T(8,128)(2,1)S(1)}, bf16[1,256,512]{2,1,0:T(8,128)(2,1)S(1)}, u32[]{:S(2)}, u32[]{:S(2)}) collective-permute-start(bf16[1,256,512]{2,1,0:T(8,128)(2,1)S(1)} %collective-permute-done.10), channel_id=1, source_target_pairs={{0,16},{1,17},{2,18},{3,19},{4,20},{5,21},{6,22},{7,23},{8,9},{9,8... | collective-permute-start | bytes 786440 | tf_op jit(solution)/shard_map/ppermute | solution.py:281
  50.2 18.5 %collective-permute-start.1 = (bf16[2,256,512]{2,1,0:T(8,128)(2,1)S(1)}, bf16[2,256,512]{2,1,0:T(8,128)(2,1)S(1)}, u32[]{:S(2)}, u32[]{:S(2)}) collective-permute-start(bf16[2,256,512]{2,1,0:T(8,128)(2,1)S(1)} %pad_maximum_fusion.refs_0_), channel_id=1, source_target_pairs={{0,1},{1,0},{2,3},{3,2},{4,5},{5,4},{6,7},{7,6},{8,24},{9,25},{10,... | collective-permute-start | bytes 1572872 | tf_op jit(solution)/shard_map/ppermute | solution.py:281
  54.2 21.3 %copy-start = (bf16[2,512,256]{2,1,0:T(8,128)(2,1)}, bf16[2,512,256]{2,1,0:T(8,128)(2,1)S(1)}, u32[]{:S(2)}) copy-start(bf16[2,512,256]{2,1,0:T(8,128)(2,1)S(1)} %get-tuple-element.17) | copy-start | bytes 1572868
  57.9 13.8 %collective-permute-start.2 = (bf16[2,256,512]{2,1,0:T(8,128)(2,1)S(1)}, bf16[2,256,512]{2,1,0:T(8,128)(2,1)S(1)}, u32[]{:S(2)}, u32[]{:S(2)}) collective-permute-start(bf16[2,256,512]{2,1,0:T(8,128)(2,1)S(1)} %pad_maximum_fusion.refs_0_), channel_id=1, source_target_pairs={{0,8},{1,9},{2,10},{3,11},{4,12},{5,13},{6,14},{7,15},{8,0},{9,1},... | collective-permute-start | bytes 1572872 | tf_op jit(solution)/shard_map/ppermute | solution.py:281
  57.9 17.1 %collective-permute-start.16 = (bf16[2,512,256]{2,1,0:T(8,128)(2,1)S(1)}, bf16[2,512,256]{2,1,0:T(8,128)(2,1)S(1)}, u32[]{:S(2)}, u32[]{:S(2)}) collective-permute-start(bf16[2,512,256]{2,1,0:T(8,128)(2,1)S(1)} %get-tuple-element.18), channel_id=1, source_target_pairs={{0,1},{1,0},{2,3},{3,2},{4,5},{5,4},{6,7},{7,6},{8,24},{9,25},{10,... | collective-permute-start | bytes 1572872 | tf_op jit(solution)/shard_map/ppermute | solution.py:281
  58.5 10.2 %copy-start.1 = (bf16[2,256,512]{2,1,0:T(8,128)(2,1)}, bf16[2,256,512]{2,1,0:T(8,128)(2,1)S(1)}, u32[]{:S(2)}) copy-start(bf16[2,256,512]{2,1,0:T(8,128)(2,1)S(1)} %constant_dynamic-update-slice_fusion.3.refs_8_) | copy-start | bytes 1572868
  68.7 16.9 %copy-start.6 = (bf16[2,256,512]{2,1,0:T(8,128)(2,1)}, bf16[2,256,512]{2,1,0:T(8,128)(2,1)S(1)}, u32[]{:S(2)}) copy-start(bf16[2,256,512]{2,1,0:T(8,128)(2,1)S(1)} %collective-permute-done.1.refs_1_) | copy-start | bytes 1572868
  68.7 16.8 %collective-permute-start.12 = (bf16[2,256,512]{2,1,0:T(8,128)(2,1)S(1)}, bf16[2,256,512]{2,1,0:T(8,128)(2,1)S(1)}, u32[]{:S(2)}, u32[]{:S(2)}) collective-permute-start(bf16[2,256,512]{2,1,0:T(8,128)(2,1)S(1)} %constant_dynamic-update-slice_fusion.3.refs_8_), channel_id=1, source_target_pairs={{0,1},{1,0},{2,3},{3,2},{4,5},{5,4},{6,7},{7,6},{8,24},{9,25},{10,... | collective-permute-start | bytes 1572872 | tf_op jit(solution)/shard_map/ppermute | solution.py:281
  69.5 16.0 %copy-start.12 = (bf16[4,512,256]{2,1,0:T(8,128)(2,1)}, bf16[4,512,256]{2,1,0:T(8,128)(2,1)S(1)}, u32[]{:S(2)}) copy-start(bf16[4,512,256]{2,1,0:T(8,128)(2,1)S(1)} %collective-permute-done.20) | copy-start | bytes 3145732
  69.5 24.6 %collective-permute-start.25 = (bf16[2,512,256]{2,1,0:T(8,128)(2,1)}, bf16[2,512,256]{2,1,0:T(8,128)(2,1)S(1)}, u32[]{:S(2)}, u32[]{:S(2)}) collective-permute-start(bf16[2,512,256]{2,1,0:T(8,128)(2,1)} %get-tuple-element.22), channel_id=1, source_target_pairs={{0,1},{1,0},{2,3},{3,2},{4,5},{5,4},{6,7},{7,6},{8,24},{9,25},{10,... | collective-permute-start | bytes 1572872 | tf_op jit(solution)/shard_map/ppermute | solution.py:281
  71.7 13.8 %copy-start.8 = (bf16[2,256,512]{2,1,0:T(8,128)(2,1)}, bf16[2,256,512]{2,1,0:T(8,128)(2,1)S(1)}, u32[]{:S(2)}) copy-start(bf16[2,256,512]{2,1,0:T(8,128)(2,1)S(1)} %collective-permute-done.2.refs_2_) | copy-start | bytes 1572868
  71.7 23.0 %collective-permute-start.21 = (bf16[2,512,256]{2,1,0:T(8,128)(2,1)}, bf16[2,512,256]{2,1,0:T(8,128)(2,1)}, u32[]{:S(2)}, u32[]{:S(2)}) collective-permute-start(bf16[2,512,256]{2,1,0:T(8,128)(2,1)} %add_convert_fusion), channel_id=1, source_target_pairs={{0,16},{1,17},{2,18},{3,19},{4,20},{5,21},{6,22},{7,23},{8,9},{9,8... | collective-permute-start | bytes 1572872 | tf_op jit(solution)/shard_map/ppermute | solution.py:281
  75.0 10.6 %copy-start.13 = (bf16[2,512,256]{2,1,0:T(8,128)(2,1)}, bf16[2,512,256]{2,1,0:T(8,128)(2,1)S(1)}, u32[]{:S(2)}) copy-start(bf16[2,512,256]{2,1,0:T(8,128)(2,1)S(1)} %collective-permute-done.16) | copy-start | bytes 1572868
  75.0 28.7 %collective-permute-start.8 = (bf16[4,256,512]{2,1,0:T(8,128)(2,1)}, bf16[4,256,512]{2,1,0:T(8,128)(2,1)}, u32[]{:S(2)}, u32[]{:S(2)}) collective-permute-start(bf16[4,256,512]{2,1,0:T(8,128)(2,1)} %constant_dynamic-update-slice_fusion.refs_4_), channel_id=1, source_target_pairs={{0,8},{1,9},{2,10},{3,11},{4,12},{5,13},{6,14},{7,15},{8,0},{9,1},... | collective-permute-start | bytes 3145736 | tf_op jit(solution)/shard_map/ppermute | solution.py:281
  75.0 30.8 %collective-permute-start.9 = (bf16[4,256,512]{2,1,0:T(8,128)(2,1)}, bf16[4,256,512]{2,1,0:T(8,128)(2,1)}, u32[]{:S(2)}, u32[]{:S(2)}) collective-permute-start(bf16[4,256,512]{2,1,0:T(8,128)(2,1)} %collective-permute-done.7.refs_5_), channel_id=1, source_target_pairs={{0,8},{1,9},{2,10},{3,11},{4,12},{5,13},{6,14},{7,15},{8,0},{9,1},... | collective-permute-start | bytes 3145736 | tf_op jit(solution)/shard_map/ppermute | solution.py:281
  85.6 0.8 copy-start.10
  86.3 8.0 %collective-permute-start.17 = (bf16[1,512,256]{2,1,0:T(8,128)(2,1)S(1)}, bf16[1,512,256]{2,1,0:T(8,128)(2,1)}, u32[]{:S(2)}, u32[]{:S(2)}) collective-permute-start(bf16[1,512,256]{2,1,0:T(8,128)(2,1)S(1)} %add_convert_fusion.5), channel_id=1, source_target_pairs={{0,16},{1,17},{2,18},{3,19},{4,20},{5,21},{6,22},{7,23},{8,9},{9,8... | collective-permute-start | bytes 786440 | tf_op jit(solution)/shard_map/ppermute | solution.py:281
  89.3 33.4 %all-to-all-start = ((bf16[32,16,512]{2,1,0:T(8,128)(2,1)}), bf16[32,16,512]{2,1,0:T(8,128)(2,1)S(1)}, u32[]{:S(2)}, u32[]{:S(2)}) async-start(bf16[32,16,512]{2,1,0:T(8,128)(2,1)} %pack_moments.1), calls=%async_computation | async-start | bytes 1048576 | tf_op jit(solution)/shard_map/all_to_all | solution.py:387
  94.0 11.7 %copy-start.2 = (bf16[2,256,512]{2,1,0:T(8,128)(2,1)S(1)}, bf16[2,256,512]{2,1,0:T(8,128)(2,1)}, u32[]{:S(2)}) copy-start(bf16[2,256,512]{2,1,0:T(8,128)(2,1)} %copy-done.1) | copy-start | bytes 1572868
  94.0 11.7 %copy-start.4 = (s32[8]{0:T(128)S(1)}, s32[8]{0:T(128)}, u32[]{:S(2)}) copy-start(s32[8]{0:T(128)} %new_ref.15) | copy-start | bytes 100
  94.1 11.7 %copy-start.5 = (s32[32]{0:T(128)S(1)}, s32[32]{0:T(128)}, u32[]{:S(2)}) copy-start(s32[32]{0:T(128)} %owner_ref.1) | copy-start | bytes 388
  94.1 11.7 %copy-start.7 = (bf16[2,256,512]{2,1,0:T(8,128)(2,1)S(1)}, bf16[2,256,512]{2,1,0:T(8,128)(2,1)}, u32[]{:S(2)}) copy-start(bf16[2,256,512]{2,1,0:T(8,128)(2,1)} %copy-done.6) | copy-start | bytes 1572868
  94.1 11.7 %copy-start.9 = (bf16[2,256,512]{2,1,0:T(8,128)(2,1)S(1)}, bf16[2,256,512]{2,1,0:T(8,128)(2,1)}, u32[]{:S(2)}) copy-start(bf16[2,256,512]{2,1,0:T(8,128)(2,1)} %copy-done.8) | copy-start | bytes 1572868
  94.1 11.7 %copy-start.11 = (bf16[2,256,512]{2,1,0:T(8,128)(2,1)S(1)}, bf16[2,256,512]{2,1,0:T(8,128)(2,1)}, u32[]{:S(2)}) copy-start(bf16[2,256,512]{2,1,0:T(8,128)(2,1)} %copy-done.10) | copy-start | bytes 1572868
  94.1 5.7 %collective-permute-start.13 = (bf16[2,256,512]{2,1,0:T(8,128)(2,1)}, bf16[2,256,512]{2,1,0:T(8,128)(2,1)S(1)}, u32[]{:S(2)}, u32[]{:S(2)}) collective-permute-start(bf16[2,256,512]{2,1,0:T(8,128)(2,1)} %copy-done.1), channel_id=1, source_target_pairs={{0,8},{1,9},{2,10},{3,11},{4,12},{5,13},{6,14},{7,15},{8,0},{9,1},... | collective-permute-start | bytes 1572872 | tf_op jit(solution)/shard_map/ppermute | solution.py:281
  94.3 6.9 %collective-permute-start.3 = (bf16[2,256,512]{2,1,0:T(8,128)(2,1)}, bf16[2,256,512]{2,1,0:T(8,128)(2,1)S(1)}, u32[]{:S(2)}, u32[]{:S(2)}) collective-permute-start(bf16[2,256,512]{2,1,0:T(8,128)(2,1)} %copy-done.6), channel_id=1, source_target_pairs={{0,8},{1,9},{2,10},{3,11},{4,12},{5,13},{6,14},{7,15},{8,0},{9,1},... | collective-permute-start | bytes 1572872 | tf_op jit(solution)/shard_map/ppermute | solution.py:281
  94.7 9.0 %collective-permute-start.14 = (bf16[2,256,512]{2,1,0:T(8,128)(2,1)}, bf16[2,256,512]{2,1,0:T(8,128)(2,1)S(1)}, u32[]{:S(2)}, u32[]{:S(2)}) collective-permute-start(bf16[2,256,512]{2,1,0:T(8,128)(2,1)} %copy-done.10), channel_id=1, source_target_pairs={{0,8},{1,9},{2,10},{3,11},{4,12},{5,13},{6,14},{7,15},{8,0},{9,1},... | collective-permute-start | bytes 1572872 | tf_op jit(solution)/shard_map/ppermute | solution.py:281
  99.8 23.0 %collective-permute-start.26 = (bf16[1,512,256]{2,1,0:T(8,128)(2,1)}, bf16[1,512,256]{2,1,0:T(8,128)(2,1)S(1)}, u32[]{:S(2)}, u32[]{:S(2)}) collective-permute-start(bf16[1,512,256]{2,1,0:T(8,128)(2,1)} %add_convert_fusion.1), channel_id=1, source_target_pairs={{0,16},{1,17},{2,18},{3,19},{4,20},{5,21},{6,22},{7,23},{8,9},{9,8... | collective-permute-start | bytes 786440 | tf_op jit(solution)/shard_map/ppermute | solution.py:281
  101.2 21.7 %collective-permute-start.18 = (bf16[1,512,256]{2,1,0:T(8,128)(2,1)}, bf16[1,512,256]{2,1,0:T(8,128)(2,1)S(1)}, u32[]{:S(2)}, u32[]{:S(2)}) collective-permute-start(bf16[1,512,256]{2,1,0:T(8,128)(2,1)} %add_convert_fusion.4), channel_id=1, source_target_pairs={{0,4},{1,5},{2,6},{3,7},{4,0},{5,1},{6,2},{7,3},{8,12},{9,13},{10,... | collective-permute-start | bytes 786440 | tf_op jit(solution)/shard_map/ppermute | solution.py:281
  103.7 24.6 %collective-permute-start.22 = (bf16[1,512,256]{2,1,0:T(8,128)(2,1)}, bf16[1,512,256]{2,1,0:T(8,128)(2,1)S(1)}, u32[]{:S(2)}, u32[]{:S(2)}) collective-permute-start(bf16[1,512,256]{2,1,0:T(8,128)(2,1)} %get-tuple-element.27), channel_id=1, source_target_pairs={{0,2},{1,3},{2,4},{3,5},{4,6},{5,7},{6,0},{7,1},{8,10},{9,11},{10,... | collective-permute-start | bytes 786440 | tf_op jit(solution)/shard_map/ppermute | solution.py:281
  103.7 26.6 %collective-permute-start.23 = (bf16[1,512,256]{2,1,0:T(8,128)(2,1)}, bf16[1,512,256]{2,1,0:T(8,128)(2,1)S(1)}, u32[]{:S(2)}, u32[]{:S(2)}) collective-permute-start(bf16[1,512,256]{2,1,0:T(8,128)(2,1)} %get-tuple-element.26), channel_id=1, source_target_pairs={{0,6},{1,7},{2,0},{3,1},{4,2},{5,3},{6,4},{7,5},{8,14},{9,15},{10,... | collective-permute-start | bytes 786440 | tf_op jit(solution)/shard_map/ppermute | solution.py:281

commit v7 on v4

--- a/solution.py
+++ b/solution.py
@@ -16,7 +16,7 @@
 correction_two = 1.0 - 0.95**10
 
 AXES = ("rep", "fsdp")
-GRANT = 48 * 1024 * 1024
+GRANT = 45 * 1024 * 1024
 SUB = 8
 
 

time: 133 us -> 133 us (level)
  no operation moved by 1% of the time
where the time goes in v7:
time: 133 us
  waiting for transfers between devices  48.4 us (36%)
  Pallas kernels  45.2 us (34%)
  starting transfers between devices  26.7 us (20%)
  other arithmetic  6.09 us (5%)
  local copies, waits for them, and re-layouts  5.33 us (4%)
    ppermute x27, waiting for transfers between devices, send(): return lax.ppermute(value, AXES, pairs)  48.4 us
    pallas_call x6, Pallas kernels, grad_blocks(): pl.pallas_call(functools.partial(grad_kernel, per_step, len(added)), grid...  24 us
    ppermute x27, starting transfers between devices, send(): return lax.ppermute(value, AXES, pairs)  21.9 us
    pallas_call x1, Pallas kernels, project(): pl.pallas_call(functools.partial(project_kernel, devices // new_owner.sha...  16.9 us
    convert_element_type x5, other arithmetic, rounded_sum(): return total.astype(terms[0].dtype)  5.99 us
    all_to_all x1, starting transfers between devices, body(): lax.all_to_all(packed, AXES, split_axis=0, concat_axis=0, tiled=True)  4.73 us
    unnamed x34, local copies, waits for them, and re-layouts  3.78 us
  transfers between devices with their start and end apart: 28, of which 10 were waited for; matrix products, arithmetic and copies ran while one was open for 6% of the time, Pallas kernels for 29%

profile of v7, /device:TPU:8, one launch (start us, length us, event | category | flops | bytes accessed | tf_op | source)
XLA Modules:
  0.0 132.6 jit_solution(4417416849455012426)
XLA Ops:
  0.6 0.0 copy-start.3
  0.6 1.5 %copy.12 = bf16[1024,512]{0,1:T(8,128)(2,1)S(1)} copy(bf16[1024,512]{1,0:T(8,128)(2,1)} %param.9) | data formatting | bytes 2097152 | tf_op args[1]
  2.1 0.7 dynamic-slice_bitcast_fusion.row_ref
  2.8 4.9 %weight_gradient.8 = bf16[8,512,256]{2,1,0:T(8,128)(2,1)S(1)} custom-call(s32[64]{0:T(128)S(1)} %dynamic-slice_bitcast_fusion.row_ref, s32[8]{0:T(128)S(1)} %copy-done.3, bf16[1024,8192]{1,0:T(8,128)(2,1)} %refs_1_.11, bf16[1024,8192]{1,0:T(8,128)(2,1)} %refs_1_.11, bf16[1024,8192]{1,0:T(8,128)(2,1)} %refs_1_.11, bf16[1024,8192]{1,0:T(8,128)(2,1)} %refs_1_.11, ...), custom_call_target="tpu_custom_call" | custom-call | flops 2147483648 | bytes 7340032 | tf_op jit(solution)/shard_map/weight_gradient/pallas_call | solution.py:79
  7.7 0.1 collective-permute-start.19
  7.8 1.6 %collective-permute-start.4 = (bf16[1,256,512]{2,1,0:T(8,128)(2,1)S(1)}, bf16[1,256,512]{2,1,0:T(8,128)(2,1)S(1)}, u32[]{:S(2)}, u32[]{:S(2)}) collective-permute-start(bf16[1,256,512]{2,1,0:T(8,128)(2,1)S(1)} %bitcast.10), channel_id=1, source_target_pairs={{0,2},{1,3},{2,4},{3,5},{4,6},{5,7},{6,0},{7,1},{8,10},{9,11},{10,... | collective-permute-start | bytes 786440 | tf_op jit(solution)/shard_map/ppermute | solution.py:278
  9.5 0.4 collective-permute-start.5
  9.9 3.3 %weight_gradient.6 = bf16[4,512,256]{2,1,0:T(8,128)(2,1)S(1)} custom-call(s32[64]{0:T(128)S(1)} %dynamic-slice_bitcast_fusion.row_ref, s32[8]{0:T(128)S(1)} %copy-done.3, bf16[1024,8192]{1,0:T(8,128)(2,1)} %refs_1_.11, bf16[1024,8192]{1,0:T(8,128)(2,1)} %refs_1_.11, bf16[512,1024]{1,0:T(8,128)(2,1)S(1)} %bitcast.5), custom_call_target="tpu_custom_call" | custom-call | flops 1073741824 | bytes 4194304 | tf_op jit(solution)/shard_map/weight_gradient/pallas_call | solution.py:79
  13.3 0.1 collective-permute-start.15
  13.3 3.7 %collective-permute-done.4 = bf16[1,256,512]{2,1,0:T(8,128)(2,1)S(1)} collective-permute-done((bf16[1,256,512]{2,1,0:T(8,128)(2,1)S(1)}, bf16[1,256,512]{2,1,0:T(8,128)(2,1)S(1)}, u32[]{:S(2)}, u32[]{:S(2)}) %collective-permute-start.4) | collective-permute-done | bytes 262176 | tf_op jit(solution)/shard_map/ppermute | solution.py:278
  17.0 6.0 %collective-permute-done.5 = bf16[1,256,512]{2,1,0:T(8,128)(2,1)S(1)} collective-permute-done((bf16[1,256,512]{2,1,0:T(8,128)(2,1)S(1)}, bf16[1,256,512]{2,1,0:T(8,128)(2,1)S(1)}, u32[]{:S(2)}, u32[]{:S(2)}) %collective-permute-start.5) | collective-permute-done | bytes 262176 | tf_op jit(solution)/shard_map/ppermute | solution.py:278
  23.0 0.1 pad_maximum_fusion.1
  23.0 1.6 %collective-permute-start.6 = (bf16[2,256,512]{2,1,0:T(8,128)(2,1)S(1)}, bf16[2,256,512]{2,1,0:T(8,128)(2,1)S(1)}, u32[]{:S(2)}, u32[]{:S(2)}) collective-permute-start(bf16[2,256,512]{2,1,0:T(8,128)(2,1)S(1)} %pad_maximum_fusion.1), channel_id=1, source_target_pairs={{0,16},{1,17},{2,18},{3,19},{4,20},{5,21},{6,22},{7,23},{8,9},{9,8... | collective-permute-start | bytes 1572872 | tf_op jit(solution)/shard_map/ppermute | solution.py:278
  24.6 3.3 %weight_gradient.10 = bf16[4,512,256]{2,1,0:T(8,128)(2,1)S(1)} custom-call(s32[64]{0:T(128)S(1)} %dynamic-slice_bitcast_fusion.row_ref, s32[8]{0:T(128)S(1)} %copy-done.3, bf16[1024,8192]{1,0:T(8,128)(2,1)} %refs_1_.11, bf16[1024,8192]{1,0:T(8,128)(2,1)} %refs_1_.11, bf16[512,1024]{1,0:T(8,128)(2,1)S(1)} %bitcast.6), custom_call_target="tpu_custom_call" | custom-call | flops 1073741824 | bytes 4194304 | tf_op jit(solution)/shard_map/weight_gradient/pallas_call | solution.py:79
  28.0 0.1 collective-permute-start.24
  28.1 1.2 collective-permute-start
  29.3 0.0 collective-permute-done.19.refs_5_
  29.3 4.9 %weight_gradient.9 = (bf16[4,512,256]{2,1,0:T(8,128)(2,1)S(1)}, bf16[4,512,256]{2,1,0:T(8,128)(2,1)S(1)}) custom-call(s32[64]{0:T(128)S(1)} %dynamic-slice_bitcast_fusion.row_ref, s32[8]{0:T(128)S(1)} %copy-done.3, bf16[1024,8192]{1,0:T(8,128)(2,1)} %refs_1_.11, bf16[1024,8192]{1,0:T(8,128)(2,1)} %refs_1_.11, bf16[1024,8192]{1,0:T(8,128)(2,1)} %refs_1_.11, ...), custom_call_target="tpu_custom_call" | custom-call | flops 2147483648 | bytes 9437184 | tf_op jit(solution)/shard_map/weight_gradient/pallas_call | solution.py:79
  34.2 0.9 collective-permute-start.20
  35.1 0.7 constant_dynamic-update-slice_fusion.2
  35.8 0.0 collective-permute-done.6
  35.8 1.7 %collective-permute-start.10 = (bf16[1,256,512]{2,1,0:T(8,128)(2,1)S(1)}, bf16[1,256,512]{2,1,0:T(8,128)(2,1)S(1)}, u32[]{:S(2)}, u32[]{:S(2)}) collective-permute-start(bf16[1,256,512]{2,1,0:T(8,128)(2,1)S(1)} %bitcast.13), channel_id=1, source_target_pairs={{0,4},{1,5},{2,6},{3,7},{4,0},{5,1},{6,2},{7,3},{8,12},{9,13},{10,... | collective-permute-start | bytes 786440 | tf_op jit(solution)/shard_map/ppermute | solution.py:278
  37.6 0.7 constant_dynamic-update-slice_fusion.1
  38.3 0.8 constant_dynamic-update-slice_fusion.refs_4_
  39.1 0.6 collective-permute-start.7
  39.7 8.9 %collective-permute-done.10 = bf16[1,256,512]{2,1,0:T(8,128)(2,1)S(1)} collective-permute-done((bf16[1,256,512]{2,1,0:T(8,128)(2,1)S(1)}, bf16[1,256,512]{2,1,0:T(8,128)(2,1)S(1)}, u32[]{:S(2)}, u32[]{:S(2)}) %collective-permute-start.10) | collective-permute-done | bytes 262176 | tf_op jit(solution)/shard_map/ppermute | solution.py:278
  48.7 1.5 %collective-permute-start.11 = (bf16[1,256,512]{2,1,0:T(8,128)(2,1)S(1)}, bf16[1,256,512]{2,1,0:T(8,128)(2,1)S(1)}, u32[]{:S(2)}, u32[]{:S(2)}) collective-permute-start(bf16[1,256,512]{2,1,0:T(8,128)(2,1)S(1)} %collective-permute-done.10), channel_id=1, source_target_pairs={{0,16},{1,17},{2,18},{3,19},{4,20},{5,21},{6,22},{7,23},{8,9},{9,8... | collective-permute-start | bytes 786440 | tf_op jit(solution)/shard_map/ppermute | solution.py:278
  50.2 0.1 pad_maximum_fusion.refs_0_
  50.3 0.6 collective-permute-start.1
  50.9 3.3 %weight_gradient.7 = (bf16[2,512,256]{2,1,0:T(8,128)(2,1)S(1)}, bf16[2,512,256]{2,1,0:T(8,128)(2,1)S(1)}) custom-call(s32[64]{0:T(128)S(1)} %dynamic-slice_bitcast_fusion.row_ref, s32[8]{0:T(128)S(1)} %copy-done.3, bf16[1024,8192]{1,0:T(8,128)(2,1)} %refs_1_.11, bf16[1024,8192]{1,0:T(8,128)(2,1)} %refs_1_.11, bf16[512,1024]{1,0:T(8,128)(2,1)S(1)} %bitcast.8, ...), custom_call_target="tpu_custom_call" | custom-call | flops 1073741824 | bytes 5242880 | tf_op jit(solution)/shard_map/weight_gradient/pallas_call | solution.py:79
  54.2 3.7 %collective-permute-done.11 = bf16[1,256,512]{2,1,0:T(8,128)(2,1)S(1)} collective-permute-done((bf16[1,256,512]{2,1,0:T(8,128)(2,1)S(1)}, bf16[1,256,512]{2,1,0:T(8,128)(2,1)S(1)}, u32[]{:S(2)}, u32[]{:S(2)}) %collective-permute-start.11) | collective-permute-done | bytes 262176 | tf_op jit(solution)/shard_map/ppermute | solution.py:278
  57.9 0.5 collective-permute-start.16
  58.5 4.1 %weight_gradient.11 = (bf16[2,512,256]{2,1,0:T(8,128)(2,1)}, bf16[2,512,256]{2,1,0:T(8,128)(2,1)S(1)}) custom-call(s32[64]{0:T(128)S(1)} %dynamic-slice_bitcast_fusion.row_ref, s32[8]{0:T(128)S(1)} %copy-done.3, bf16[1024,8192]{1,0:T(8,128)(2,1)} %refs_1_.11, bf16[1024,8192]{1,0:T(8,128)(2,1)} %refs_1_.11, bf16[512,1024]{1,0:T(8,128)(2,1)S(1)} %bitcast.9, ...), custom_call_target="tpu_custom_call" | custom-call | flops 1073741824 | bytes 5242880 | tf_op jit(solution)/shard_map/weight_gradient/pallas_call | solution.py:79
  62.7 6.1 %collective-permute-done.1.refs_1_ = bf16[2,256,512]{2,1,0:T(8,128)(2,1)S(1)} collective-permute-done((bf16[2,256,512]{2,1,0:T(8,128)(2,1)S(1)}, bf16[2,256,512]{2,1,0:T(8,128)(2,1)S(1)}, u32[]{:S(2)}, u32[]{:S(2)}) %collective-permute-start.1) | collective-permute-done | bytes 524320 | tf_op jit(solution)/shard_map/ppermute | solution.py:278
  68.7 0.8 collective-permute-start.12
  69.6 1.2 collective-permute-start.25
  70.8 1.0 add_convert_fusion
  71.8 0.9 collective-permute-start.21
  72.6 2.4 %collective-permute-done.16 = bf16[2,512,256]{2,1,0:T(8,128)(2,1)S(1)} collective-permute-done((bf16[2,512,256]{2,1,0:T(8,128)(2,1)S(1)}, bf16[2,512,256]{2,1,0:T(8,128)(2,1)S(1)}, u32[]{:S(2)}, u32[]{:S(2)}) %collective-permute-start.16) | collective-permute-done | bytes 524320 | tf_op jit(solution)/shard_map/ppermute | solution.py:278
  75.0 0.5 collective-permute-start.9
  75.5 0.1 add_convert_fusion.5
  75.6 10.0 %collective-permute-done.12.refs_9_ = bf16[2,256,512]{2,1,0:T(8,128)(2,1)S(1)} collective-permute-done((bf16[2,256,512]{2,1,0:T(8,128)(2,1)S(1)}, bf16[2,256,512]{2,1,0:T(8,128)(2,1)S(1)}, u32[]{:S(2)}, u32[]{:S(2)}) %collective-permute-start.12) | collective-permute-done | bytes 524320 | tf_op jit(solution)/shard_map/ppermute | solution.py:278
  85.6 0.8 copy-done.10
  86.4 0.9 collective-permute-start.17
  87.3 2.1 %pack_moments.1 = bf16[32,16,512]{2,1,0:T(8,128)(2,1)} custom-call(s32[8]{0:T(128)} %new_ref.15, f32[256,512]{1,0:T(8,128)} %first_ref.1, f32[256,512]{1,0:T(8,128)} %second_ref.1), custom_call_target="tpu_custom_call" | custom-call | bytes 1572864 | tf_op jit(solution)/shard_map/pack_moments/pallas_call | solution.py:110
  89.4 4.7 %all-to-all-start = ((bf16[32,16,512]{2,1,0:T(8,128)(2,1)}), bf16[32,16,512]{2,1,0:T(8,128)(2,1)S(1)}, u32[]{:S(2)}, u32[]{:S(2)}) async-start(bf16[32,16,512]{2,1,0:T(8,128)(2,1)} %pack_moments.1), calls=%async_computation | async-start | bytes 1048576 | tf_op jit(solution)/shard_map/all_to_all | solution.py:384
  94.1 0.0 copy-start.4
  94.1 0.0 copy-start.5
  94.1 0.0 copy-start.7
  94.1 0.0 copy-start.9
  94.2 0.2 collective-permute-start.13
  94.4 0.4 collective-permute-start.3
  94.8 0.1 collective-permute-start.14
  94.9 0.8 add_convert_fusion.1
  95.7 1.9 %add_convert_fusion.4 = bf16[1,512,256]{2,1,0:T(8,128)(2,1)} fusion(bf16[1,512,256]{2,1,0:T(8,128)(2,1)} %collective-permute-done.17, bf16[2,512,256]{2,1,0:T(8,128)(2,1)} %copy-done.13, bf16[2,512,256]{2,1,0:T(8,128)(2,1)} %copy-done), kind=kLoop, calls=%fused_computation.6 | loop fusion | flops 786432 | bytes 1048576 | tf_op jit(solution)/shard_map/convert_element_type | solution.py:285
  97.6 2.2 %add_convert_fusion.2 = (bf16[1,512,256]{2,1,0:T(8,128)(2,1)}, bf16[1,512,256]{2,1,0:T(8,128)(2,1)}) fusion(bf16[2,512,256]{2,1,0:T(8,128)(2,1)} %collective-permute-done.21, bf16[4,512,256]{2,1,0:T(8,128)(2,1)} %copy-done.12, bf16[4,512,256]{2,1,0:T(8,128)(2,1)S(1)} %get-tuple-element.19), kind=kLoop, calls=%fused_computation.4 | loop fusion | flops 1572864 | bytes 2097152 | tf_op jit(solution)/shard_map/convert_element_type | solution.py:285
  99.8 1.5 %collective-permute-start.26 = (bf16[1,512,256]{2,1,0:T(8,128)(2,1)}, bf16[1,512,256]{2,1,0:T(8,128)(2,1)S(1)}, u32[]{:S(2)}, u32[]{:S(2)}) collective-permute-start(bf16[1,512,256]{2,1,0:T(8,128)(2,1)} %add_convert_fusion.1), channel_id=1, source_target_pairs={{0,16},{1,17},{2,18},{3,19},{4,20},{5,21},{6,22},{7,23},{8,9},{9,8... | collective-permute-start | bytes 786440 | tf_op jit(solution)/shard_map/ppermute | solution.py:278
  101.3 2.4 %collective-permute-start.18 = (bf16[1,512,256]{2,1,0:T(8,128)(2,1)}, bf16[1,512,256]{2,1,0:T(8,128)(2,1)S(1)}, u32[]{:S(2)}, u32[]{:S(2)}) collective-permute-start(bf16[1,512,256]{2,1,0:T(8,128)(2,1)} %add_convert_fusion.4), channel_id=1, source_target_pairs={{0,4},{1,5},{2,6},{3,7},{4,0},{5,1},{6,2},{7,3},{8,12},{9,13},{10,... | collective-permute-start | bytes 786440 | tf_op jit(solution)/shard_map/ppermute | solution.py:278
  103.8 2.0 %collective-permute-start.23 = (bf16[1,512,256]{2,1,0:T(8,128)(2,1)}, bf16[1,512,256]{2,1,0:T(8,128)(2,1)S(1)}, u32[]{:S(2)}, u32[]{:S(2)}) collective-permute-start(bf16[1,512,256]{2,1,0:T(8,128)(2,1)} %get-tuple-element.26), channel_id=1, source_target_pairs={{0,6},{1,7},{2,0},{3,1},{4,2},{5,3},{6,4},{7,5},{8,14},{9,15},{10,... | collective-permute-start | bytes 786440 | tf_op jit(solution)/shard_map/ppermute | solution.py:278
  105.8 16.9 %project.1 = (bf16[1024,512]{1,0:T(8,128)(2,1)}, bf16[256,512]{1,0:T(8,128)(2,1)S(1)}) custom-call(s32[64]{0:T(128)S(1)} %dynamic-slice_bitcast_fusion.row_ref, s32[32]{0:T(128)S(1)} %copy-done.5, s32[8]{0:T(128)S(1)} %copy-done.4, bf16[1024,8192]{1,0:T(8,128)(2,1)} %refs_1_.11, bf16[2,256,512]{2,1,0:T(8,128)(2,1)S(1)} %pad_maximum_fusion.refs_0_, ...), custom_call_target="tpu_custom_call" | custom-call | flops 8589934592 | bytes 26214400 | tf_op jit(solution)/shard_map/project/pallas_call | solution.py:169
  122.8 0.2 collective-permute-done.18.refs_0_
  123.0 5.4 %collective-permute-done.22.refs_1_ = bf16[1,512,256]{2,1,0:T(8,128)(2,1)S(1)} collective-permute-done((bf16[1,512,256]{2,1,0:T(8,128)(2,1)}, bf16[1,512,256]{2,1,0:T(8,128)(2,1)S(1)}, u32[]{:S(2)}, u32[]{:S(2)}) %collective-permute-start.22) | collective-permute-done | bytes 262176 | tf_op jit(solution)/shard_map/ppermute | solution.py:278
  128.4 2.0 %collective-permute-done.23.refs_2_ = bf16[1,512,256]{2,1,0:T(8,128)(2,1)S(1)} collective-permute-done((bf16[1,512,256]{2,1,0:T(8,128)(2,1)}, bf16[1,512,256]{2,1,0:T(8,128)(2,1)S(1)}, u32[]{:S(2)}, u32[]{:S(2)}) %collective-permute-start.23) | collective-permute-done | bytes 262176 | tf_op jit(solution)/shard_map/ppermute | solution.py:278
  130.4 2.2 %adam_rows.1 = (bf16[256,512]{1,0:T(8,128)(2,1)}, f32[256,512]{1,0:T(8,128)}, f32[256,512]{1,0:T(8,128)}) custom-call(s32[32]{0:T(128)S(1)} %copy-done.5, bf16[32,16,512]{2,1,0:T(8,128)(2,1)S(1)} %all-to-all-done.moments_ref, bf16[256,512]{1,0:T(8,128)(2,1)S(1)} %get-tuple-element.16.weight_ref, bf16[1,512,256]{2,1,0:T(8,128)(2,1)S(1)} %collective-permute-done.18.refs_0_, ...), custom_call_target="tpu_custom_call" | custom-call | flops 2621440 | bytes 2097152 | tf_op jit(solution)/shard_map/adam_rows/pallas_call | solution.py:231
  (45 shorter events, 0.1 us)
Async XLA Ops:
  0.6 2.2 %copy-start.3 = (s32[8]{0:T(128)S(1)}, s32[8]{0:T(128)}, u32[]{:S(2)}) copy-start(s32[8]{0:T(128)} %new_ref.15) | copy-start | bytes 100
  2.8 5.0 %copy-start.14 = (bf16[256,512]{1,0:T(8,128)(2,1)S(1)}, bf16[256,512]{1,0:T(8,128)(2,1)}, u32[]{:S(2)}) copy-start(bf16[256,512]{1,0:T(8,128)(2,1)} %param.10) | copy-start | bytes 786436
  7.7 21.6 %collective-permute-start.19 = (bf16[8,512,256]{2,1,0:T(8,128)(2,1)S(1)}, bf16[8,512,256]{2,1,0:T(8,128)(2,1)S(1)}, u32[]{:S(2)}, u32[]{:S(2)}) collective-permute-start(bf16[8,512,256]{2,1,0:T(8,128)(2,1)S(1)} %weight_gradient.8), channel_id=1, source_target_pairs={{0,8},{1,9},{2,10},{3,11},{4,12},{5,13},{6,14},{7,15},{8,0},{9,1},... | collective-permute-start | bytes 6291464 | tf_op jit(solution)/shard_map/ppermute | solution.py:278
  7.8 9.2 %collective-permute-start.4 = (bf16[1,256,512]{2,1,0:T(8,128)(2,1)S(1)}, bf16[1,256,512]{2,1,0:T(8,128)(2,1)S(1)}, u32[]{:S(2)}, u32[]{:S(2)}) collective-permute-start(bf16[1,256,512]{2,1,0:T(8,128)(2,1)S(1)} %bitcast.10), channel_id=1, source_target_pairs={{0,2},{1,3},{2,4},{3,5},{4,6},{5,7},{6,0},{7,1},{8,10},{9,11},{10,... | collective-permute-start | bytes 786440 | tf_op jit(solution)/shard_map/ppermute | solution.py:278
  9.5 13.5 %collective-permute-start.5 = (bf16[1,256,512]{2,1,0:T(8,128)(2,1)S(1)}, bf16[1,256,512]{2,1,0:T(8,128)(2,1)S(1)}, u32[]{:S(2)}, u32[]{:S(2)}) collective-permute-start(bf16[1,256,512]{2,1,0:T(8,128)(2,1)S(1)} %bitcast.11), channel_id=1, source_target_pairs={{0,6},{1,7},{2,0},{3,1},{4,2},{5,3},{6,4},{7,5},{8,14},{9,15},{10,... | collective-permute-start | bytes 786440 | tf_op jit(solution)/shard_map/ppermute | solution.py:278
  13.3 37.0 %collective-permute-start.15 = (bf16[4,512,256]{2,1,0:T(8,128)(2,1)S(1)}, bf16[4,512,256]{2,1,0:T(8,128)(2,1)S(1)}, u32[]{:S(2)}, u32[]{:S(2)}) collective-permute-start(bf16[4,512,256]{2,1,0:T(8,128)(2,1)S(1)} %weight_gradient.6), channel_id=1, source_target_pairs={{0,8},{1,9},{2,10},{3,11},{4,12},{5,13},{6,14},{7,15},{8,0},{9,1},... | collective-permute-start | bytes 3145736 | tf_op jit(solution)/shard_map/ppermute | solution.py:278
  23.0 12.8 %collective-permute-start.6 = (bf16[2,256,512]{2,1,0:T(8,128)(2,1)S(1)}, bf16[2,256,512]{2,1,0:T(8,128)(2,1)S(1)}, u32[]{:S(2)}, u32[]{:S(2)}) collective-permute-start(bf16[2,256,512]{2,1,0:T(8,128)(2,1)S(1)} %pad_maximum_fusion.1), channel_id=1, source_target_pairs={{0,16},{1,17},{2,18},{3,19},{4,20},{5,21},{6,22},{7,23},{8,9},{9,8... | collective-permute-start | bytes 1572872 | tf_op jit(solution)/shard_map/ppermute | solution.py:278
  28.0 30.0 %collective-permute-start.24 = (bf16[4,512,256]{2,1,0:T(8,128)(2,1)S(1)}, bf16[4,512,256]{2,1,0:T(8,128)(2,1)S(1)}, u32[]{:S(2)}, u32[]{:S(2)}) collective-permute-start(bf16[4,512,256]{2,1,0:T(8,128)(2,1)S(1)} %weight_gradient.10), channel_id=1, source_target_pairs={{0,8},{1,9},{2,10},{3,11},{4,12},{5,13},{6,14},{7,15},{8,0},{9,1},... | collective-permute-start | bytes 3145736 | tf_op jit(solution)/shard_map/ppermute | solution.py:278
  28.1 11.1 %collective-permute-start = (bf16[1,256,512]{2,1,0:T(8,128)(2,1)S(1)}, bf16[1,256,512]{2,1,0:T(8,128)(2,1)S(1)}, u32[]{:S(2)}, u32[]{:S(2)}) collective-permute-start(bf16[1,256,512]{2,1,0:T(8,128)(2,1)S(1)} %bitcast.12), channel_id=1, source_target_pairs={{0,16},{1,17},{2,18},{3,19},{4,20},{5,21},{6,22},{7,23},{8,9},{9,8... | collective-permute-start | bytes 786440 | tf_op jit(solution)/shard_map/ppermute | solution.py:278
  34.2 35.4 %collective-permute-start.20 = (bf16[4,512,256]{2,1,0:T(8,128)(2,1)S(1)}, bf16[4,512,256]{2,1,0:T(8,128)(2,1)S(1)}, u32[]{:S(2)}, u32[]{:S(2)}) collective-permute-start(bf16[4,512,256]{2,1,0:T(8,128)(2,1)S(1)} %get-tuple-element.20), channel_id=1, source_target_pairs={{0,1},{1,0},{2,3},{3,2},{4,5},{5,4},{6,7},{7,6},{8,24},{9,25},{10,... | collective-permute-start | bytes 3145736 | tf_op jit(solution)/shard_map/ppermute | solution.py:278
  35.8 12.9 %collective-permute-start.10 = (bf16[1,256,512]{2,1,0:T(8,128)(2,1)S(1)}, bf16[1,256,512]{2,1,0:T(8,128)(2,1)S(1)}, u32[]{:S(2)}, u32[]{:S(2)}) collective-permute-start(bf16[1,256,512]{2,1,0:T(8,128)(2,1)S(1)} %bitcast.13), channel_id=1, source_target_pairs={{0,4},{1,5},{2,6},{3,7},{4,0},{5,1},{6,2},{7,3},{8,12},{9,13},{10,... | collective-permute-start | bytes 786440 | tf_op jit(solution)/shard_map/ppermute | solution.py:278
  39.1 35.9 %collective-permute-start.7 = (bf16[4,256,512]{2,1,0:T(8,128)(2,1)}, bf16[4,256,512]{2,1,0:T(8,128)(2,1)}, u32[]{:S(2)}, u32[]{:S(2)}) collective-permute-start(bf16[4,256,512]{2,1,0:T(8,128)(2,1)} %constant_dynamic-update-slice_fusion.refs_4_), channel_id=1, source_target_pairs={{0,1},{1,0},{2,3},{3,2},{4,5},{5,4},{6,7},{7,6},{8,24},{9,25},{10,... | collective-permute-start | bytes 3145736 | tf_op jit(solution)/shard_map/ppermute | solution.py:278
  48.7 9.2 %collective-permute-start.11 = (bf16[1,256,512]{2,1,0:T(8,128)(2,1)S(1)}, bf16[1,256,512]{2,1,0:T(8,128)(2,1)S(1)}, u32[]{:S(2)}, u32[]{:S(2)}) collective-permute-start(bf16[1,256,512]{2,1,0:T(8,128)(2,1)S(1)} %collective-permute-done.10), channel_id=1, source_target_pairs={{0,16},{1,17},{2,18},{3,19},{4,20},{5,21},{6,22},{7,23},{8,9},{9,8... | collective-permute-start | bytes 786440 | tf_op jit(solution)/shard_map/ppermute | solution.py:278
  50.3 18.5 %collective-permute-start.1 = (bf16[2,256,512]{2,1,0:T(8,128)(2,1)S(1)}, bf16[2,256,512]{2,1,0:T(8,128)(2,1)S(1)}, u32[]{:S(2)}, u32[]{:S(2)}) collective-permute-start(bf16[2,256,512]{2,1,0:T(8,128)(2,1)S(1)} %pad_maximum_fusion.refs_0_), channel_id=1, source_target_pairs={{0,1},{1,0},{2,3},{3,2},{4,5},{5,4},{6,7},{7,6},{8,24},{9,25},{10,... | collective-permute-start | bytes 1572872 | tf_op jit(solution)/shard_map/ppermute | solution.py:278
  54.2 21.3 %copy-start = (bf16[2,512,256]{2,1,0:T(8,128)(2,1)}, bf16[2,512,256]{2,1,0:T(8,128)(2,1)S(1)}, u32[]{:S(2)}) copy-start(bf16[2,512,256]{2,1,0:T(8,128)(2,1)S(1)} %get-tuple-element.17) | copy-start | bytes 1572868
  57.9 13.8 %collective-permute-start.2 = (bf16[2,256,512]{2,1,0:T(8,128)(2,1)S(1)}, bf16[2,256,512]{2,1,0:T(8,128)(2,1)S(1)}, u32[]{:S(2)}, u32[]{:S(2)}) collective-permute-start(bf16[2,256,512]{2,1,0:T(8,128)(2,1)S(1)} %pad_maximum_fusion.refs_0_), channel_id=1, source_target_pairs={{0,8},{1,9},{2,10},{3,11},{4,12},{5,13},{6,14},{7,15},{8,0},{9,1},... | collective-permute-start | bytes 1572872 | tf_op jit(solution)/shard_map/ppermute | solution.py:278
  57.9 17.1 %collective-permute-start.16 = (bf16[2,512,256]{2,1,0:T(8,128)(2,1)S(1)}, bf16[2,512,256]{2,1,0:T(8,128)(2,1)S(1)}, u32[]{:S(2)}, u32[]{:S(2)}) collective-permute-start(bf16[2,512,256]{2,1,0:T(8,128)(2,1)S(1)} %get-tuple-element.18), channel_id=1, source_target_pairs={{0,1},{1,0},{2,3},{3,2},{4,5},{5,4},{6,7},{7,6},{8,24},{9,25},{10,... | collective-permute-start | bytes 1572872 | tf_op jit(solution)/shard_map/ppermute | solution.py:278
  58.5 10.2 %copy-start.1 = (bf16[2,256,512]{2,1,0:T(8,128)(2,1)}, bf16[2,256,512]{2,1,0:T(8,128)(2,1)S(1)}, u32[]{:S(2)}) copy-start(bf16[2,256,512]{2,1,0:T(8,128)(2,1)S(1)} %constant_dynamic-update-slice_fusion.3.refs_8_) | copy-start | bytes 1572868
  68.7 16.9 %copy-start.6 = (bf16[2,256,512]{2,1,0:T(8,128)(2,1)}, bf16[2,256,512]{2,1,0:T(8,128)(2,1)S(1)}, u32[]{:S(2)}) copy-start(bf16[2,256,512]{2,1,0:T(8,128)(2,1)S(1)} %collective-permute-done.1.refs_1_) | copy-start | bytes 1572868
  68.7 16.8 %collective-permute-start.12 = (bf16[2,256,512]{2,1,0:T(8,128)(2,1)S(1)}, bf16[2,256,512]{2,1,0:T(8,128)(2,1)S(1)}, u32[]{:S(2)}, u32[]{:S(2)}) collective-permute-start(bf16[2,256,512]{2,1,0:T(8,128)(2,1)S(1)} %constant_dynamic-update-slice_fusion.3.refs_8_), channel_id=1, source_target_pairs={{0,1},{1,0},{2,3},{3,2},{4,5},{5,4},{6,7},{7,6},{8,24},{9,25},{10,... | collective-permute-start | bytes 1572872 | tf_op jit(solution)/shard_map/ppermute | solution.py:278
  69.6 16.0 %copy-start.12 = (bf16[4,512,256]{2,1,0:T(8,128)(2,1)}, bf16[4,512,256]{2,1,0:T(8,128)(2,1)S(1)}, u32[]{:S(2)}) copy-start(bf16[4,512,256]{2,1,0:T(8,128)(2,1)S(1)} %collective-permute-done.20) | copy-start | bytes 3145732
  69.6 24.6 %collective-permute-start.25 = (bf16[2,512,256]{2,1,0:T(8,128)(2,1)}, bf16[2,512,256]{2,1,0:T(8,128)(2,1)S(1)}, u32[]{:S(2)}, u32[]{:S(2)}) collective-permute-start(bf16[2,512,256]{2,1,0:T(8,128)(2,1)} %get-tuple-element.22), channel_id=1, source_target_pairs={{0,1},{1,0},{2,3},{3,2},{4,5},{5,4},{6,7},{7,6},{8,24},{9,25},{10,... | collective-permute-start | bytes 1572872 | tf_op jit(solution)/shard_map/ppermute | solution.py:278
  71.8 13.8 %copy-start.8 = (bf16[2,256,512]{2,1,0:T(8,128)(2,1)}, bf16[2,256,512]{2,1,0:T(8,128)(2,1)S(1)}, u32[]{:S(2)}) copy-start(bf16[2,256,512]{2,1,0:T(8,128)(2,1)S(1)} %collective-permute-done.2.refs_2_) | copy-start | bytes 1572868
  71.8 23.0 %collective-permute-start.21 = (bf16[2,512,256]{2,1,0:T(8,128)(2,1)}, bf16[2,512,256]{2,1,0:T(8,128)(2,1)}, u32[]{:S(2)}, u32[]{:S(2)}) collective-permute-start(bf16[2,512,256]{2,1,0:T(8,128)(2,1)} %add_convert_fusion), channel_id=1, source_target_pairs={{0,16},{1,17},{2,18},{3,19},{4,20},{5,21},{6,22},{7,23},{8,9},{9,8... | collective-permute-start | bytes 1572872 | tf_op jit(solution)/shard_map/ppermute | solution.py:278
  75.0 10.6 %copy-start.13 = (bf16[2,512,256]{2,1,0:T(8,128)(2,1)}, bf16[2,512,256]{2,1,0:T(8,128)(2,1)S(1)}, u32[]{:S(2)}) copy-start(bf16[2,512,256]{2,1,0:T(8,128)(2,1)S(1)} %collective-permute-done.16) | copy-start | bytes 1572868
  75.0 28.8 %collective-permute-start.8 = (bf16[4,256,512]{2,1,0:T(8,128)(2,1)}, bf16[4,256,512]{2,1,0:T(8,128)(2,1)}, u32[]{:S(2)}, u32[]{:S(2)}) collective-permute-start(bf16[4,256,512]{2,1,0:T(8,128)(2,1)} %constant_dynamic-update-slice_fusion.refs_4_), channel_id=1, source_target_pairs={{0,8},{1,9},{2,10},{3,11},{4,12},{5,13},{6,14},{7,15},{8,0},{9,1},... | collective-permute-start | bytes 3145736 | tf_op jit(solution)/shard_map/ppermute | solution.py:278
  75.0 30.8 %collective-permute-start.9 = (bf16[4,256,512]{2,1,0:T(8,128)(2,1)}, bf16[4,256,512]{2,1,0:T(8,128)(2,1)}, u32[]{:S(2)}, u32[]{:S(2)}) collective-permute-start(bf16[4,256,512]{2,1,0:T(8,128)(2,1)} %collective-permute-done.7.refs_5_), channel_id=1, source_target_pairs={{0,8},{1,9},{2,10},{3,11},{4,12},{5,13},{6,14},{7,15},{8,0},{9,1},... | collective-permute-start | bytes 3145736 | tf_op jit(solution)/shard_map/ppermute | solution.py:278
  85.6 0.8 copy-start.10
  86.4 8.0 %collective-permute-start.17 = (bf16[1,512,256]{2,1,0:T(8,128)(2,1)S(1)}, bf16[1,512,256]{2,1,0:T(8,128)(2,1)}, u32[]{:S(2)}, u32[]{:S(2)}) collective-permute-start(bf16[1,512,256]{2,1,0:T(8,128)(2,1)S(1)} %add_convert_fusion.5), channel_id=1, source_target_pairs={{0,16},{1,17},{2,18},{3,19},{4,20},{5,21},{6,22},{7,23},{8,9},{9,8... | collective-permute-start | bytes 786440 | tf_op jit(solution)/shard_map/ppermute | solution.py:278
  89.4 33.5 %all-to-all-start = ((bf16[32,16,512]{2,1,0:T(8,128)(2,1)}), bf16[32,16,512]{2,1,0:T(8,128)(2,1)S(1)}, u32[]{:S(2)}, u32[]{:S(2)}) async-start(bf16[32,16,512]{2,1,0:T(8,128)(2,1)} %pack_moments.1), calls=%async_computation | async-start | bytes 1048576 | tf_op jit(solution)/shard_map/all_to_all | solution.py:384
  94.1 11.7 %copy-start.2 = (bf16[2,256,512]{2,1,0:T(8,128)(2,1)S(1)}, bf16[2,256,512]{2,1,0:T(8,128)(2,1)}, u32[]{:S(2)}) copy-start(bf16[2,256,512]{2,1,0:T(8,128)(2,1)} %copy-done.1) | copy-start | bytes 1572868
  94.1 11.7 %copy-start.4 = (s32[8]{0:T(128)S(1)}, s32[8]{0:T(128)}, u32[]{:S(2)}) copy-start(s32[8]{0:T(128)} %new_ref.15) | copy-start | bytes 100
  94.1 11.7 %copy-start.5 = (s32[32]{0:T(128)S(1)}, s32[32]{0:T(128)}, u32[]{:S(2)}) copy-start(s32[32]{0:T(128)} %owner_ref.1) | copy-start | bytes 388
  94.1 11.7 %copy-start.7 = (bf16[2,256,512]{2,1,0:T(8,128)(2,1)S(1)}, bf16[2,256,512]{2,1,0:T(8,128)(2,1)}, u32[]{:S(2)}) copy-start(bf16[2,256,512]{2,1,0:T(8,128)(2,1)} %copy-done.6) | copy-start | bytes 1572868
  94.1 11.7 %copy-start.9 = (bf16[2,256,512]{2,1,0:T(8,128)(2,1)S(1)}, bf16[2,256,512]{2,1,0:T(8,128)(2,1)}, u32[]{:S(2)}) copy-start(bf16[2,256,512]{2,1,0:T(8,128)(2,1)} %copy-done.8) | copy-start | bytes 1572868
  94.2 11.7 %copy-start.11 = (bf16[2,256,512]{2,1,0:T(8,128)(2,1)S(1)}, bf16[2,256,512]{2,1,0:T(8,128)(2,1)}, u32[]{:S(2)}) copy-start(bf16[2,256,512]{2,1,0:T(8,128)(2,1)} %copy-done.10) | copy-start | bytes 1572868
  94.2 5.7 %collective-permute-start.13 = (bf16[2,256,512]{2,1,0:T(8,128)(2,1)}, bf16[2,256,512]{2,1,0:T(8,128)(2,1)S(1)}, u32[]{:S(2)}, u32[]{:S(2)}) collective-permute-start(bf16[2,256,512]{2,1,0:T(8,128)(2,1)} %copy-done.1), channel_id=1, source_target_pairs={{0,8},{1,9},{2,10},{3,11},{4,12},{5,13},{6,14},{7,15},{8,0},{9,1},... | collective-permute-start | bytes 1572872 | tf_op jit(solution)/shard_map/ppermute | solution.py:278
  94.4 6.9 %collective-permute-start.3 = (bf16[2,256,512]{2,1,0:T(8,128)(2,1)}, bf16[2,256,512]{2,1,0:T(8,128)(2,1)S(1)}, u32[]{:S(2)}, u32[]{:S(2)}) collective-permute-start(bf16[2,256,512]{2,1,0:T(8,128)(2,1)} %copy-done.6), channel_id=1, source_target_pairs={{0,8},{1,9},{2,10},{3,11},{4,12},{5,13},{6,14},{7,15},{8,0},{9,1},... | collective-permute-start | bytes 1572872 | tf_op jit(solution)/shard_map/ppermute | solution.py:278
  94.8 9.0 %collective-permute-start.14 = (bf16[2,256,512]{2,1,0:T(8,128)(2,1)}, bf16[2,256,512]{2,1,0:T(8,128)(2,1)S(1)}, u32[]{:S(2)}, u32[]{:S(2)}) collective-permute-start(bf16[2,256,512]{2,1,0:T(8,128)(2,1)} %copy-done.10), channel_id=1, source_target_pairs={{0,8},{1,9},{2,10},{3,11},{4,12},{5,13},{6,14},{7,15},{8,0},{9,1},... | collective-permute-start | bytes 1572872 | tf_op jit(solution)/shard_map/ppermute | solution.py:278
  99.8 23.0 %collective-permute-start.26 = (bf16[1,512,256]{2,1,0:T(8,128)(2,1)}, bf16[1,512,256]{2,1,0:T(8,128)(2,1)S(1)}, u32[]{:S(2)}, u32[]{:S(2)}) collective-permute-start(bf16[1,512,256]{2,1,0:T(8,128)(2,1)} %add_convert_fusion.1), channel_id=1, source_target_pairs={{0,16},{1,17},{2,18},{3,19},{4,20},{5,21},{6,22},{7,23},{8,9},{9,8... | collective-permute-start | bytes 786440 | tf_op jit(solution)/shard_map/ppermute | solution.py:278
  101.3 21.7 %collective-permute-start.18 = (bf16[1,512,256]{2,1,0:T(8,128)(2,1)}, bf16[1,512,256]{2,1,0:T(8,128)(2,1)S(1)}, u32[]{:S(2)}, u32[]{:S(2)}) collective-permute-start(bf16[1,512,256]{2,1,0:T(8,128)(2,1)} %add_convert_fusion.4), channel_id=1, source_target_pairs={{0,4},{1,5},{2,6},{3,7},{4,0},{5,1},{6,2},{7,3},{8,12},{9,13},{10,... | collective-permute-start | bytes 786440 | tf_op jit(solution)/shard_map/ppermute | solution.py:278
  103.8 24.6 %collective-permute-start.22 = (bf16[1,512,256]{2,1,0:T(8,128)(2,1)}, bf16[1,512,256]{2,1,0:T(8,128)(2,1)S(1)}, u32[]{:S(2)}, u32[]{:S(2)}) collective-permute-start(bf16[1,512,256]{2,1,0:T(8,128)(2,1)} %get-tuple-element.27), channel_id=1, source_target_pairs={{0,2},{1,3},{2,4},{3,5},{4,6},{5,7},{6,0},{7,1},{8,10},{9,11},{10,... | collective-permute-start | bytes 786440 | tf_op jit(solution)/shard_map/ppermute | solution.py:278
  103.8 26.6 %collective-permute-start.23 = (bf16[1,512,256]{2,1,0:T(8,128)(2,1)}, bf16[1,512,256]{2,1,0:T(8,128)(2,1)S(1)}, u32[]{:S(2)}, u32[]{:S(2)}) collective-permute-start(bf16[1,512,256]{2,1,0:T(8,128)(2,1)} %get-tuple-element.26), channel_id=1, source_target_pairs={{0,6},{1,7},{2,0},{3,1},{4,2},{5,3},{6,4},{7,5},{8,14},{9,15},{10,... | collective-permute-start | bytes 786440 | tf_op jit(solution)/shard_map/ppermute | solution.py:278
